TPU v7x, 256 devices: a whole 4x4x8 slice. The times are simulated.
256 devices in a mesh: fsdp: 32 (over y_hi, z, core), mp: 8 (over y_lo, x).
Axes of the slice: x: 4, y: 4 (y_hi: 2, y_lo: 2; y = y_hi * 2 + y_lo), z: 8, core: 2. Of those that a mesh axis runs over, the one named last changes fastest.
Arguments:
- tokens: bfloat16 [16384, 3072], P('fsdp', 'mp'), may hold values from -6 to 6
- ln_gain: float32 [3072], replicated, may hold values from 0.1 to 1.9
- w_qkv: bfloat16 [3072, 3, 3072], P('fsdp', None, 'mp'), may hold values from -0.109375 to 0.109375
- w_up: bfloat16 [3072, 12288], P('fsdp', 'mp'), may hold values from -0.109375 to 0.109375
- q_gain: float32 [24, 128], P('mp'), may hold values from 0.4 to 16
- k_gain: float32 [24, 128], P('mp'), may hold values from 0.4 to 16
- w_proj: bfloat16 [3072, 3072], P('mp', 'fsdp'), may hold values from -0.109375 to 0.109375
- w_down: bfloat16 [12288, 3072], P('mp', 'fsdp'), may hold values from -0.0546875 to 0.0546875
Outputs:
- block_out: bfloat16 [16384, 3072], P('fsdp', 'mp')
All inputs are finite; a program needn't handle non-finite values.
Results may differ from a plain program's by a relative error of at most 0.015.
Values may be sent and summed in bfloat16 or wider, within the bound.
No kernel may reach another device: no remote copies, remote signals or barrier semaphores. Data moves between devices by JAX's collectives and lax.ppermute only.
A program may use at most 128 MiB of HBM per device.

v0:
```python
import functools

import jax
import jax.numpy as jnp
from jax import lax
from jax.experimental import pallas as pl
from jax.experimental.pallas import tpu as pltpu
from jax.sharding import Mesh, PartitionSpec as P

HD = 128
PATCHES = 256
FSDP = ("yh", "z", "c")
MP = ("yl", "x")
ROW = ("z", "c")
SWAP = [(0, 1), (1, 0)]


def layer_norm(values, gain):
    mean = jnp.mean(values, axis=-1, keepdims=True)
    centred = values - mean
    variance = jnp.mean(centred * centred, axis=-1, keepdims=True)
    return centred * lax.rsqrt(variance + 1e-06) * gain


def shift(n, k):
    return [(i, (i + k) % n) for i in range(n)]


def tie(values, *after):
    return lax.optimization_barrier((values, *after))[0]


def norm_kernel(x_ref, gain_ref, pair_ref, right_ref, left_ref, far_a_ref, far_b_ref, out_ref):
    panels = [(0, 0, pair_ref.at[0]), (1, 0, pair_ref.at[1])]
    panels += [(0, 1, right_ref.at[0]), (1, 1, right_ref.at[1])]
    panels += [(0, 2, far_a_ref), (1, 2, far_b_ref)]
    panels += [(0, 3, left_ref.at[0]), (1, 3, left_ref.at[1])]
    width = out_ref.shape[1] // len(panels)

    def mean(fn):
        total = sum(fn(ref[...].astype(jnp.float32)) for _, _, ref in panels)
        return jnp.sum(total, axis=-1, keepdims=True) / out_ref.shape[1]

    centre = mean(lambda v: v)
    scale = lax.rsqrt(mean(lambda v: (v - centre) * (v - centre)) + 1e-06)
    for h, k, ref in panels:
        at = h * 4 + lax.rem(x_ref[0] + 4 - k, 4)
        cols = pl.ds(pl.multiple_of(at * width, HD), width)
        values = (ref[...].astype(jnp.float32) - centre) * scale * gain_ref[:, cols]
        out_ref[:, cols] = values.astype(out_ref.dtype)


def norm_tokens(x, gain, pair, right, left, far_a, far_b):
    rows, width = far_a.shape
    tile = 128
    one = pl.BlockSpec((tile, width), lambda i: (i, 0))
    two = pl.BlockSpec((2, tile, width), lambda i: (0, i, 0))
    return pl.pallas_call(
        norm_kernel,
        grid=(rows // tile,),
        in_specs=[
            pl.BlockSpec(memory_space=pltpu.SMEM),
            pl.BlockSpec((1, 8 * width), lambda i: (0, 0)),
            two,
            two,
            two,
            one,
            one,
        ],
        out_specs=pl.BlockSpec((tile, 8 * width), lambda i: (i, 0)),
        out_shape=jax.ShapeDtypeStruct((rows, 8 * width), jnp.bfloat16),
        compiler_params=pltpu.CompilerParams(vmem_limit_bytes=32 * 2**20),
    )(x[None], gain[None], pair, right, left, far_a, far_b)


def both_rows(mine, other):
    yh = lax.axis_index("yh")
    return jnp.where(yh == 0, jnp.stack([mine, other]), jnp.stack([other, mine]))


def pick(blocks, at, axis):
    return lax.dynamic_index_in_dim(blocks, at, axis, keepdims=False)


def to_peers_x(blocks, axis):
    x = lax.axis_index("x")
    return [
        lax.ppermute(pick(blocks, (x + k) % 4, axis), "x", shift(4, k)) for k in (2, 1, 3)
    ]


def scatter_start(mine, theirs):
    yl, x = lax.axis_index("yl"), lax.axis_index("x")
    shape = (2, 4, mine.shape[0] // 8 * mine.shape[1], mine.shape[2])
    mine, theirs = mine.reshape(shape), theirs.reshape(shape)
    over_x = to_peers_x(mine, 1)
    both = [(core * 2 + at, (1 - core) * 2 + 1 - at) for core in range(2) for at in range(2)]
    over_y = lax.ppermute(pick(theirs, 1 - yl, 0), ("c", "yl"), both)
    kept = lax.ppermute(pick(theirs, yl, 0), "c", SWAP)
    over_x = tie(over_x, kept)
    return [pick(mine, x, 1)] + over_x, [kept, over_y]


def scatter_end(over_x, over_y):
    yl, x = lax.axis_index("yl"), lax.axis_index("x")

    def total(values):
        return sum(v.astype(jnp.float32) for v in values)

    by_y, by_x = total(over_x), total(over_y)
    other = lax.ppermute(pick(by_y, 1 - yl, 0).astype(jnp.bfloat16), "yl", SWAP)
    others = to_peers_x(by_x.astype(jnp.bfloat16), 0)
    return total([pick(by_y, yl, 0), other]), total([pick(by_x, x, 0)] + others)


def across(v):
    return lax.ppermute(v, "yh", SWAP)


def up_kernel(x_ref, w_ref, out_ref):
    pre = jnp.dot(x_ref[...], w_ref[...], preferred_element_type=jnp.float32)
    out_ref[...] = (0.5 * pre * (1.0 + lax.erf(pre * 0.7071067811865476))).astype(out_ref.dtype)


def up_gelu(x, w):
    tile = 256
    rows, depth = x.shape
    hidden = w.shape[1]
    return pl.pallas_call(
        up_kernel,
        grid=(hidden // tile,),
        in_specs=[
            pl.BlockSpec((rows, depth), lambda i: (0, 0)),
            pl.BlockSpec((depth, tile), lambda i: (0, i)),
        ],
        out_specs=pl.BlockSpec((rows, tile), lambda i: (0, i)),
        out_shape=jax.ShapeDtypeStruct((rows, hidden), jnp.bfloat16),
        compiler_params=pltpu.CompilerParams(vmem_limit_bytes=53 * 2**20),
    )(x, w)


def attention_kernel(
    starts_ref, x_ref, own_ref, near_ref, far_ref, q_gain_ref, k_gain_ref, out_ref, proj_ref
):
    rows, heads = x_ref.shape[0], q_gain_ref.shape[0]
    pieces = (own_ref, near_ref, far_ref)
    for part in range(3):
        total = None
        for i, w_ref in enumerate(pieces):
            depth = w_ref.shape[1]
            at = pl.multiple_of(starts_ref[i], HD)
            term = jnp.dot(
                x_ref[:, pl.ds(at, depth)], w_ref[part], preferred_element_type=jnp.float32
            )
            total = term if total is None else total + term
        proj_ref[part] = total
    for h in range(heads):
        cols = slice(h * HD, (h + 1) * HD)
        q_gain, k_gain = q_gain_ref[h : h + 1, :], k_gain_ref[h : h + 1, :]
        for image in range(rows // PATCHES):
            at = slice(image * PATCHES, (image + 1) * PATCHES)
            queries = layer_norm(proj_ref[0, at, cols], q_gain).astype(jnp.bfloat16)
            keys = layer_norm(proj_ref[1, at, cols], k_gain).astype(jnp.bfloat16)
            values = proj_ref[2, at, cols].astype(jnp.bfloat16)
            scores = lax.dot_general(
                queries, keys, (((1,), (1,)), ((), ())), preferred_element_type=jnp.float32
            ) * HD ** (-0.5)
            scores = scores - jnp.max(scores, axis=-1, keepdims=True)
            weights = jnp.exp(scores)
            probs = (weights / jnp.sum(weights, axis=-1, keepdims=True)).astype(jnp.bfloat16)
            mixed = jnp.dot(probs, values, preferred_element_type=jnp.float32)
            out_ref[at, cols] = mixed.astype(jnp.bfloat16)


def attention(starts, x, own, near, far, q_gain, k_gain):
    rows, depth = x.shape
    cols = own.shape[2]
    vmem = pl.BlockSpec(memory_space=pltpu.VMEM)
    return pl.pallas_call(
        attention_kernel,
        in_specs=[pl.BlockSpec(memory_space=pltpu.SMEM)] + [vmem] * 6,
        out_specs=vmem,
        out_shape=jax.ShapeDtypeStruct((rows, cols), jnp.bfloat16),
        scratch_shapes=[pltpu.VMEM((3, rows, cols), jnp.float32)],
        compiler_params=pltpu.CompilerParams(vmem_limit_bytes=40 * 2**20),
    )(starts, x, own, near, far, q_gain, k_gain)


def out_kernel(places, rows, *refs):
    at_ref, attended_ref, activated_ref = refs[:3]
    shards = refs[3 : 3 + len(places)]
    out_ref, held, sem = refs[3 + len(places) :]
    yh, z = at_ref[0], at_ref[1]
    slots = list(dict.fromkeys(place[:2] for group in places for place in group))
    copies = [[] for _ in slots]
    count = 0
    for group, shard in zip(places, shards):
        for i, (other, offset, start) in enumerate(group):
            slot = slots.index((other, offset))
            at = pl.ds(slot * rows + start, shard.shape[1])
            copy = pltpu.make_async_copy(shard.at[i], held.at[at], sem.at[count])
            copy.start()
            copies[slot].append(copy)
            count += 1
    split = attended_ref.shape[1]
    contract = (((1,), (1,)), ((), ()))
    step = 4
    for first in range(0, len(slots), step):
        for slot in range(first, first + step):
            for copy in copies[slot]:
                copy.wait()
        at = slice(first * rows, (first + step) * rows)
        total = lax.dot_general(
            held[at, :split], attended_ref[...], contract, preferred_element_type=jnp.float32
        )
        total += lax.dot_general(
            held[at, split:], activated_ref[...], contract, preferred_element_type=jnp.float32
        )
        total = total.astype(out_ref.dtype)
        for i in range(step):
            other, offset = slots[first + i]
            owner = (1 - yh if other else yh) * 8 + lax.rem(z + offset + 8, 8)
            out_ref[owner] = total[i * rows : (i + 1) * rows]


def out_terms(place, rows, attended, activated, shards):
    places = tuple(places for places, _ in shards)
    tokens = attended.shape[0]
    width = attended.shape[1] + activated.shape[1]
    vmem = pl.BlockSpec(memory_space=pltpu.VMEM)
    return pl.pallas_call(
        functools.partial(out_kernel, places, rows),
        in_specs=[pl.BlockSpec(memory_space=pltpu.SMEM), vmem, vmem]
        + [pl.BlockSpec(memory_space=pltpu.HBM)] * len(places),
        out_specs=vmem,
        out_shape=jax.ShapeDtypeStruct((16, rows, tokens), jnp.bfloat16),
        scratch_shapes=[
            pltpu.VMEM((16 * rows, width), jnp.bfloat16),
            pltpu.SemaphoreType.DMA((sum(len(group) for group in places),)),
        ],
        compiler_params=pltpu.CompilerParams(vmem_limit_bytes=58 * 2**20),
        cost_estimate=pl.CostEstimate(
            flops=32 * rows * width * tokens, bytes_accessed=0, transcendentals=0
        ),
    )(place, attended, activated, *(arrays for _, arrays in shards))


def local(tokens, ln_gain, w_qkv, w_up, q_gain, k_gain, w_proj, w_down):
    yh, z, c = lax.axis_index("yh"), lax.axis_index("z"), lax.axis_index("c")
    yl = lax.axis_index("yl")
    tok_count = tokens.shape[0]

    def up(v, axis="z", size=8):
        return lax.ppermute(v, axis, shift(size, 1))

    def down(v, axis="z", size=8):
        return lax.ppermute(v, axis, shift(size, -1))

    own_qkv = lax.all_gather(w_qkv.transpose(1, 0, 2), ROW, axis=1, tiled=True)

    w_out = jnp.concatenate([w_proj.T, w_down.T], axis=1)[None]
    piece = w_out.shape[1]
    half = piece // 2
    other_tokens, other_up, low, high = lax.optimization_barrier(
        (lax.ppermute(tokens, "yl", SWAP), across(w_up), up(w_out), down(w_out))
    )
    up_pair = both_rows(w_up, other_up)
    up_all = lax.all_gather(up_pair, ROW, axis=1, tiled=True).reshape(-1, w_up.shape[1])
    shards = [([(0, 0, 0)], w_out), ([(0, -1, 0)], low), ([(0, 1, 0)], high)]

    first = jnp.where(yl == 0, tokens, other_tokens)
    second = jnp.where(yl == 0, other_tokens, tokens)
    pair = jnp.stack([first, second])
    quarter = own_qkv.shape[1] // 2
    near = across(jnp.concatenate([low, w_out, high]))
    low, high = up(low), down(high)
    mine = lax.dynamic_slice_in_dim(tie(own_qkv, (low, high)), c * quarter, quarter, axis=1)
    right, left, near, mine = lax.optimization_barrier(
        (up(pair, "x", 4), down(pair, "x", 4), near, mine)
    )
    other_c = across(mine)
    shards += [([(0, -2, 0)], low), ([(0, 2, 0)], high)]
    shards += [([(1, -1, 0), (1, 0, 0), (1, 1, 0)], near)]

    low, high = up(low), down(high)
    far_a, far_b = up(right[0], "x", 4), down(left[1], "x", 4)
    shards += [([(0, -3, 0)], low), ([(0, 3, 0)], high)]
    end_a, end_b = up(low[:, :half]), down(high[:, half:])
    other_low, other_high = tie((near[:1], near[2:]), (low, high))
    other_low, other_high = up(other_low), down(other_high)
    shards += [([(0, 4, 0)], end_a), ([(0, 4, half)], end_b)]
    shards += [([(1, -2, 0)], other_low), ([(1, 2, 0)], other_high)]
    other_c = tie(other_c, (far_a, far_b, end_a, end_b, other_low, other_high))
    other_d = lax.ppermute(other_c, "c", SWAP)

    normed = norm_tokens(lax.axis_index("x"), ln_gain, pair, right, left, far_a, far_b)

    base = (1 - yh) * 2 * quarter
    starts = jnp.stack([yh * 2 * quarter, base + c * quarter, base + (1 - c) * quarter])
    distant = jnp.concatenate([low, jnp.concatenate([end_a, end_b], axis=1), high])
    normed = tie(normed, (distant, other_low, other_high))
    distant = across(tie(distant, other_d))
    shards += [([(1, -3, 0), (1, 4, 0), (1, 3, 0)], distant)]
    attended = attention(starts, normed, own_qkv, other_c, other_d, q_gain, k_gain)
    activated = up_gelu(tie(normed, (attended, distant)), up_all)

    place = jnp.stack([yh, z])
    swapped = (lax.ppermute(attended, "c", SWAP), lax.ppermute(activated, "c", SWAP))
    mine = out_terms(place, piece, attended, activated, shards)
    theirs = out_terms(place, piece, *tie(swapped, mine), shards)
    mine, theirs = scatter_end(*scatter_start(mine, theirs))
    mine = mine.reshape(2, 1, piece, tok_count)
    theirs = theirs.reshape(2, 1, piece, tok_count)
    even = jnp.where(c == 0, mine, theirs)
    odd = jnp.where(c == 0, theirs, mine)
    branches = jnp.concatenate([even, odd], axis=1).reshape(4 * piece, tok_count)
    return (tokens.astype(jnp.float32) + branches.T).astype(jnp.bfloat16)


def solution(mesh):
    fine = Mesh(mesh.devices.reshape(2, 8, 2, 2, 4), ("yh", "z", "c", "yl", "x"))
    return jax.shard_map(
        local,
        mesh=fine,
        in_specs=(
            P(FSDP, MP),
            P(),
            P(FSDP, None, MP),
            P(FSDP, MP),
            P(MP, None),
            P(MP, None),
            P(MP, FSDP),
            P(MP, FSDP),
        ),
        out_specs=P(FSDP, MP),
        check_vma=False,
    )
```

profile of v0, /device:TPU:1, one launch (start us, length us, event | category | flops | bytes accessed | tf_op | source)
XLA Modules:
  0.0 230.1 jit_solution(12174255236620409767)
XLA Ops:
  7.3 2.2 collective-permute-start
  10.5 1.7 collective-permute-start.2
  12.2 4.0 %collective-permute-start.3 = (bf16[1,96,1920]{2,1,0:T(8,128)(2,1)S(1)}, bf16[1,96,1920]{2,1,0:T(8,128)(2,1)}, u32[]{:S(2)}, u32[]{:S(2)}) collective-permute-start(bf16[1,96,1920]{2,1,0:T(8,128)(2,1)S(1)} %maximum_bitcast_fusion.refs_3_), channel_id=1, source_target_pairs={{0,112},{16,0},{32,16},{48,32},{64,48},{80,64},{96,80},{112,96},{1... | collective-permute-start | bytes 1105928 | tf_op jit(solution)/shard_map/ppermute | solution.py:257
  16.3 2.6 %collective-permute-start.1 = (bf16[96,1536]{1,0:T(8,128)(2,1)}, bf16[96,1536]{1,0:T(8,128)(2,1)S(1)}, u32[]{:S(2)}, u32[]{:S(2)}) collective-permute-start(bf16[96,1536]{1,0:T(8,128)(2,1)} %param.11), channel_id=1, source_target_pairs={{0,128},{128,0},{1,129},{129,1},{2,130},{130,2},{3,131},{131,3},{4... | collective-permute-start | bytes 884744 | tf_op jit(solution)/shard_map/ppermute | solution.py:117
  18.9 8.3 %collective-permute-done.1 = bf16[96,1536]{1,0:T(8,128)(2,1)S(1)} collective-permute-done((bf16[96,1536]{1,0:T(8,128)(2,1)}, bf16[96,1536]{1,0:T(8,128)(2,1)S(1)}, u32[]{:S(2)}, u32[]{:S(2)}) %collective-permute-start.1) | collective-permute-done | bytes 294944 | tf_op jit(solution)/shard_map/ppermute | solution.py:117
  27.2 2.0 maximum_select_fusion
  29.3 1.3 pad_maximum_fusion
  31.6 1.3 collective-permute-start.4
  32.9 1.5 collective-permute-start.5
  34.4 1.2 collective-permute-start.7
  35.6 4.1 %collective-permute-start.8 = (bf16[1,96,1920]{2,1,0:T(8,128)(2,1)}, bf16[1,96,1920]{2,1,0:T(8,128)(2,1)}, u32[]{:S(2)}, u32[]{:S(2)}) collective-permute-start(bf16[1,96,1920]{2,1,0:T(8,128)(2,1)} %collective-permute-done.3.refs_5_), channel_id=1, source_target_pairs={{0,112},{16,0},{32,16},{48,32},{64,48},{80,64},{96,80},{112,96},{1... | collective-permute-start | bytes 1105928 | tf_op jit(solution)/shard_map/ppermute | solution.py:257
  39.6 15.4 %collective-permute-done.7.refs_6_ = bf16[1,96,1920]{2,1,0:T(8,128)(2,1)} collective-permute-done((bf16[1,96,1920]{2,1,0:T(8,128)(2,1)}, bf16[1,96,1920]{2,1,0:T(8,128)(2,1)}, u32[]{:S(2)}, u32[]{:S(2)}) %collective-permute-start.7) | collective-permute-done | bytes 368672 | tf_op jit(solution)/shard_map/ppermute | solution.py:254
  55.0 2.9 %all-gather.3.cloned.1.call-done.own_ref = bf16[3,1536,384]{2,1,0:T(8,128)(2,1)} async-done(((bf16[3,96,384]{2,1,0:T(8,128)(2,1)}), bf16[3,1536,384]{2,1,0:T(8,128)(2,1)}) %all-gather.3.cloned.1.call-update) | async-done | bytes 3538960 | tf_op jit(solution)/shard_map/all_gather | solution.py:259
  58.0 1.7 constant_dynamic-slice_fusion
  60.5 2.8 %collective-permute-start.17 = (bf16[3,768,384]{2,1,0:T(8,128)(2,1)S(1)}, bf16[3,768,384]{2,1,0:T(8,128)(2,1)S(1)}, u32[]{:S(2)}, u32[]{:S(2)}) collective-permute-start(bf16[3,768,384]{2,1,0:T(8,128)(2,1)S(1)} %constant_dynamic-slice_fusion), channel_id=1, source_target_pairs={{0,128},{128,0},{1,129},{129,1},{2,130},{130,2},{3,131},{131,3},{4... | collective-permute-start | bytes 5308424 | tf_op jit(solution)/shard_map/ppermute | solution.py:117
  63.3 2.2 collective-permute-start.13
  65.4 11.2 %collective-permute-done.13.refs_10_ = bf16[1,96,1920]{2,1,0:T(8,128)(2,1)S(1)} collective-permute-done((bf16[1,96,1920]{2,1,0:T(8,128)(2,1)}, bf16[1,96,1920]{2,1,0:T(8,128)(2,1)S(1)}, u32[]{:S(2)}, u32[]{:S(2)}) %collective-permute-start.13) | collective-permute-done | bytes 368672 | tf_op jit(solution)/shard_map/ppermute | solution.py:257
  76.7 3.5 %collective-permute-start.14 = (bf16[1,48,1920]{2,1,0:T(8,128)(2,1)S(1)}, bf16[1,48,1920]{2,1,0:T(8,128)(2,1)S(1)}, u32[]{:S(2)}, u32[]{:S(2)}) collective-permute-start(bf16[1,48,1920]{2,1,0:T(8,128)(2,1)S(1)} %slice.25), channel_id=1, source_target_pairs={{0,112},{16,0},{32,16},{48,32},{64,48},{80,64},{96,80},{112,96},{1... | collective-permute-start | bytes 552968 | tf_op jit(solution)/shard_map/ppermute | solution.py:257
  80.3 1.2 collective-permute-start.9
  81.6 1.8 collective-permute-start.10
  84.6 2.7 %collective-permute-done.14.refs_12_ = bf16[1,48,1920]{2,1,0:T(8,128)(2,1)S(1)} collective-permute-done((bf16[1,48,1920]{2,1,0:T(8,128)(2,1)S(1)}, bf16[1,48,1920]{2,1,0:T(8,128)(2,1)S(1)}, u32[]{:S(2)}, u32[]{:S(2)}) %collective-permute-start.14) | collective-permute-done | bytes 184352 | tf_op jit(solution)/shard_map/ppermute | solution.py:257
  87.3 3.5 %collective-permute-done.12.refs_11_ = bf16[1,48,1920]{2,1,0:T(8,128)(2,1)S(1)} collective-permute-done((bf16[1,48,1920]{2,1,0:T(8,128)(2,1)S(1)}, bf16[1,48,1920]{2,1,0:T(8,128)(2,1)S(1)}, u32[]{:S(2)}, u32[]{:S(2)}) %collective-permute-start.12) | collective-permute-done | bytes 184352 | tf_op jit(solution)/shard_map/ppermute | solution.py:254
  90.9 16.8 %collective-permute-done.15.refs_13_ = bf16[1,96,1920]{2,1,0:T(8,128)(2,1)S(1)} collective-permute-done((bf16[1,96,1920]{2,1,0:T(8,128)(2,1)S(1)}, bf16[1,96,1920]{2,1,0:T(8,128)(2,1)S(1)}, u32[]{:S(2)}, u32[]{:S(2)}) %collective-permute-start.15) | collective-permute-done | bytes 368672 | tf_op jit(solution)/shard_map/ppermute | solution.py:254
  109.5 5.5 %collective-permute-start.18 = (bf16[3,768,384]{2,1,0:T(8,128)(2,1)S(1)}, bf16[3,768,384]{2,1,0:T(8,128)(2,1)S(1)}, u32[]{:S(2)}, u32[]{:S(2)}) collective-permute-start(bf16[3,768,384]{2,1,0:T(8,128)(2,1)S(1)} %collective-permute-done.17.near_ref), channel_id=1, source_target_pairs={{0,8},{8,0},{1,9},{9,1},{2,10},{10,2},{3,11},{11,3},{4,12},{12,4},... | collective-permute-start | bytes 5308424 | tf_op jit(solution)/shard_map/ppermute | solution.py:294
  116.1 2.4 %collective-permute-done.18.far_ref = bf16[3,768,384]{2,1,0:T(8,128)(2,1)S(1)} collective-permute-done((bf16[3,768,384]{2,1,0:T(8,128)(2,1)S(1)}, bf16[3,768,384]{2,1,0:T(8,128)(2,1)S(1)}, u32[]{:S(2)}, u32[]{:S(2)}) %collective-permute-start.18) | collective-permute-done | bytes 1769504 | tf_op jit(solution)/shard_map/ppermute | solution.py:294
  118.5 1.2 copy-done.2
  119.8 1.2 copy-done.6
  123.0 3.0 %shard_map.82.x_ref = bf16[512,3072]{1,0:T(8,128)(2,1)S(1)} custom-call(s32[1]{0:T(128)} %bitcast.5.x_ref, f32[1,3072]{1,0:T(1,128)S(1)} %bitcast.70, bf16[2,512,384]{2,1,0:T(8,128)(2,1)S(1)} %pad_maximum_fusion.2.pair_ref, bf16[2,512,384]{2,1,0:T(8,128)(2,1)S(1)} %collective-permute-done.4.right_ref, bf16[2,512,384]{2,1,0:T(8,128)(2,1)S(1)} %copy-done.6, ...), custom_call_target="tpu_custom_call" | custom-call | tf_op jit(solution)/shard_map/pallas_call | solution.py:58
  126.0 6.5 %shard_map.83.refs_1_ = bf16[512,384]{1,0:T(8,128)(2,1)S(1)} custom-call(s32[3]{0:T(128)S(1)} %pad_add_fusion.1.starts_ref, bf16[512,3072]{1,0:T(8,128)(2,1)S(1)} %shard_map.82.x_ref, bf16[3,1536,384]{2,1,0:T(8,128)(2,1)S(1)} %copy-done.1, bf16[3,768,384]{2,1,0:T(8,128)(2,1)S(1)} %collective-permute-done.17.near_ref, bf16[3,768,384]{2,1,0:T(8,128)(2,1)S(1)} %copy-done.3, ...), custom_call_target="tpu_custom_call" | custom-call | tf_op jit(solution)/shard_map/pallas_call | solution.py:179
  132.6 14.5 %collective-permute-done.19.refs_15_ = bf16[3,96,1920]{2,1,0:T(8,128)(2,1)} collective-permute-done((bf16[3,96,1920]{2,1,0:T(8,128)(2,1)}, bf16[3,96,1920]{2,1,0:T(8,128)(2,1)}, u32[]{:S(2)}, u32[]{:S(2)}) %collective-permute-start.19) | collective-permute-done | bytes 1105952 | tf_op jit(solution)/shard_map/ppermute | solution.py:117
  147.1 10.3 %shard_map.84.refs_2_ = bf16[512,1536]{1,0:T(8,128)(2,1)} custom-call(bf16[512,3072]{1,0:T(8,128)(2,1)} %copy-done, bf16[3072,1536]{1,0:T(8,128)(2,1)} %bitcast.71), custom_call_target="tpu_custom_call" | custom-call | tf_op jit(solution)/shard_map/pallas_call | solution.py:129
  157.4 1.2 collective-permute-start.24
  159.6 8.3 %shard_map.85 = bf16[16,96,512]{2,1,0:T(8,128)(2,1)} custom-call(s32[2]{0:T(128)} %pad_add_fusion.refs_0_, bf16[512,384]{1,0:T(8,128)(2,1)} %copy-done.7, bf16[512,1536]{1,0:T(8,128)(2,1)} %shard_map.84.refs_2_, bf16[1,96,1920]{2,1,0:T(8,128)(2,1)} %copy-done.18, bf16[1,96,1920]{2,1,0:T(8,128)(2,1)} %collective-permute-done.2.refs_4_, ...), custom_call_target="tpu_custom_call" | custom-call | flops 3019898880 | tf_op jit(solution)/shard_map/pallas_call | solution.py:231
  169.8 8.2 %shard_map.86 = bf16[16,96,512]{2,1,0:T(8,128)(2,1)} custom-call(s32[2]{0:T(128)} %pad_add_fusion.refs_0_, bf16[512,384]{1,0:T(8,128)(2,1)} %copy-done.24, bf16[512,1536]{1,0:T(8,128)(2,1)} %copy-done.23, bf16[1,96,1920]{2,1,0:T(8,128)(2,1)} %copy-done.18, bf16[1,96,1920]{2,1,0:T(8,128)(2,1)} %collective-permute-done.2.refs_4_, ...), custom_call_target="tpu_custom_call" | custom-call | flops 3019898880 | tf_op jit(solution)/shard_map/pallas_call | solution.py:231
  178.1 1.7 dynamic-slice_bitcast_fusion
  181.0 2.7 %collective-permute-start.20 = (bf16[2,192,512]{2,1,0:T(8,128)(2,1)}, bf16[2,192,512]{2,1,0:T(8,128)(2,1)S(1)}, u32[]{:S(2)}, u32[]{:S(2)}) collective-permute-start(bf16[2,192,512]{2,1,0:T(8,128)(2,1)} %get-tuple-element.53), channel_id=1, source_target_pairs={{0,2},{1,3},{2,0},{3,1},{4,6},{5,7},{6,4},{7,5},{8,10},{9,11},{10,... | collective-permute-start | bytes 1179656 | tf_op jit(solution)/shard_map/ppermute | solution.py:88
  184.1 2.4 %collective-permute-start.22 = (bf16[2,192,512]{2,1,0:T(8,128)(2,1)}, bf16[2,192,512]{2,1,0:T(8,128)(2,1)}, u32[]{:S(2)}, u32[]{:S(2)}) collective-permute-start(bf16[2,192,512]{2,1,0:T(8,128)(2,1)} %get-tuple-element.51), channel_id=1, source_target_pairs={{0,3},{1,0},{2,1},{3,2},{4,7},{5,4},{6,5},{7,6},{8,11},{9,8},{10,9... | collective-permute-start | bytes 1179656 | tf_op jit(solution)/shard_map/ppermute | solution.py:88
  186.4 6.8 %collective-permute-done.20 = bf16[2,192,512]{2,1,0:T(8,128)(2,1)S(1)} collective-permute-done((bf16[2,192,512]{2,1,0:T(8,128)(2,1)}, bf16[2,192,512]{2,1,0:T(8,128)(2,1)S(1)}, u32[]{:S(2)}, u32[]{:S(2)}) %collective-permute-start.20) | collective-permute-done | bytes 393248 | tf_op jit(solution)/shard_map/ppermute | solution.py:88
  193.2 9.1 %collective-permute-done.21 = bf16[2,192,512]{2,1,0:T(8,128)(2,1)} collective-permute-done((bf16[2,192,512]{2,1,0:T(8,128)(2,1)}, bf16[2,192,512]{2,1,0:T(8,128)(2,1)}, u32[]{:S(2)}, u32[]{:S(2)}) %collective-permute-start.21) | collective-permute-done | bytes 393248 | tf_op jit(solution)/shard_map/ppermute | solution.py:88
  202.3 1.3 fusion.2
  204.4 1.7 collective-permute-start.26
  206.0 1.6 convert_add_fusion
  208.6 2.4 %collective-permute-start.30 = (bf16[192,512]{1,0:T(8,128)(2,1)}, bf16[192,512]{1,0:T(8,128)(2,1)S(1)}, u32[]{:S(2)}, u32[]{:S(2)}) collective-permute-start(bf16[192,512]{1,0:T(8,128)(2,1)} %get-tuple-element.57), channel_id=1, source_target_pairs={{0,3},{1,0},{2,1},{3,2},{4,7},{5,4},{6,5},{7,6},{8,11},{9,8},{10,9... | collective-permute-start | bytes 589832 | tf_op jit(solution)/shard_map/ppermute | solution.py:88
  211.0 1.2 collective-permute-start.28
  212.4 2.4 %collective-permute-done.30 = bf16[192,512]{1,0:T(8,128)(2,1)S(1)} collective-permute-done((bf16[192,512]{1,0:T(8,128)(2,1)}, bf16[192,512]{1,0:T(8,128)(2,1)S(1)}, u32[]{:S(2)}, u32[]{:S(2)}) %collective-permute-start.30) | collective-permute-done | bytes 196640 | tf_op jit(solution)/shard_map/ppermute | solution.py:88
  214.7 4.3 %collective-permute-done.29 = bf16[192,512]{1,0:T(8,128)(2,1)} collective-permute-done((bf16[192,512]{1,0:T(8,128)(2,1)}, bf16[192,512]{1,0:T(8,128)(2,1)}, u32[]{:S(2)}, u32[]{:S(2)}) %collective-permute-start.29) | collective-permute-done | bytes 196640 | tf_op jit(solution)/shard_map/ppermute | solution.py:88
  219.1 1.8 collective-permute-done.28
  220.9 1.2 fusion.6
  (104 shorter events, 17.5 us)
Async XLA Ops:
  6.5 51.4 %all-gather.3.cloned.1.call-start = ((), (), s32[]{:S(2)}) async-start(), calls=%async_computation | async-start | bytes 3760128 | tf_op jit(solution)/shard_map/all_gather | solution.py:259
  7.3 139.8 %all-gather.5.cloned.1.call-start = ((), (), s32[]{:S(2)}) async-start(), calls=%async_computation.1 | async-start | bytes 10027008 | tf_op jit(solution)/shard_map/all_gather | solution.py:268
  7.3 19.9 %collective-permute-start = (bf16[512,384]{1,0:T(8,128)(2,1)}, bf16[512,384]{1,0:T(8,128)(2,1)S(1)}, u32[]{:S(2)}, u32[]{:S(2)}) collective-permute-start(bf16[512,384]{1,0:T(8,128)(2,1)} %param.8), channel_id=1, source_target_pairs={{0,4},{4,0},{1,5},{5,1},{2,6},{6,2},{3,7},{7,3},{8,12},{12,8},{9,1... | collective-permute-start | bytes 1179656 | tf_op jit(solution)/shard_map/ppermute | solution.py:265
  10.5 20.0 %copy-start.18 = (bf16[1,96,1920]{2,1,0:T(8,128)(2,1)}, bf16[1,96,1920]{2,1,0:T(8,128)(2,1)S(1)}, u32[]{:S(2)}) copy-start(bf16[1,96,1920]{2,1,0:T(8,128)(2,1)S(1)} %maximum_bitcast_fusion.refs_3_) | copy-start | bytes 1105924
  10.5 16.7 %collective-permute-start.2 = (bf16[1,96,1920]{2,1,0:T(8,128)(2,1)S(1)}, bf16[1,96,1920]{2,1,0:T(8,128)(2,1)}, u32[]{:S(2)}, u32[]{:S(2)}) collective-permute-start(bf16[1,96,1920]{2,1,0:T(8,128)(2,1)S(1)} %maximum_bitcast_fusion.refs_3_), channel_id=1, source_target_pairs={{0,16},{16,32},{32,48},{48,64},{64,80},{80,96},{96,112},{112,0},{1... | collective-permute-start | bytes 1105928 | tf_op jit(solution)/shard_map/ppermute | solution.py:254
  12.2 14.9 %collective-permute-start.3 = (bf16[1,96,1920]{2,1,0:T(8,128)(2,1)S(1)}, bf16[1,96,1920]{2,1,0:T(8,128)(2,1)}, u32[]{:S(2)}, u32[]{:S(2)}) collective-permute-start(bf16[1,96,1920]{2,1,0:T(8,128)(2,1)S(1)} %maximum_bitcast_fusion.refs_3_), channel_id=1, source_target_pairs={{0,112},{16,0},{32,16},{48,32},{64,48},{80,64},{96,80},{112,96},{1... | collective-permute-start | bytes 1105928 | tf_op jit(solution)/shard_map/ppermute | solution.py:257
  16.3 10.9 %collective-permute-start.1 = (bf16[96,1536]{1,0:T(8,128)(2,1)}, bf16[96,1536]{1,0:T(8,128)(2,1)S(1)}, u32[]{:S(2)}, u32[]{:S(2)}) collective-permute-start(bf16[96,1536]{1,0:T(8,128)(2,1)} %param.11), channel_id=1, source_target_pairs={{0,128},{128,0},{1,129},{129,1},{2,130},{130,2},{3,131},{131,3},{4... | collective-permute-start | bytes 884744 | tf_op jit(solution)/shard_map/ppermute | solution.py:117
  29.2 2.2 copy-start.16
  30.6 30.0 %collective-permute-start.6 = (bf16[3,96,1920]{2,1,0:T(8,128)(2,1)S(1)}, bf16[3,96,1920]{2,1,0:T(8,128)(2,1)}, u32[]{:S(2)}, u32[]{:S(2)}) collective-permute-start(bf16[3,96,1920]{2,1,0:T(8,128)(2,1)S(1)} %pad_maximum_fusion), channel_id=1, source_target_pairs={{0,128},{128,0},{1,129},{129,1},{2,130},{130,2},{3,131},{131,3},{4... | collective-permute-start | bytes 3317768 | tf_op jit(solution)/shard_map/ppermute | solution.py:117
  31.6 28.0 %collective-permute-start.4 = (bf16[2,512,384]{2,1,0:T(8,128)(2,1)S(1)}, bf16[2,512,384]{2,1,0:T(8,128)(2,1)S(1)}, u32[]{:S(2)}, u32[]{:S(2)}) collective-permute-start(bf16[2,512,384]{2,1,0:T(8,128)(2,1)S(1)} %pad_maximum_fusion.2.pair_ref), channel_id=1, source_target_pairs={{0,1},{1,2},{2,3},{3,0},{4,5},{5,6},{6,7},{7,4},{8,9},{9,10},{10,1... | collective-permute-start | bytes 2359304 | tf_op jit(solution)/shard_map/ppermute | solution.py:254
  32.9 26.7 %collective-permute-start.5 = (bf16[2,512,384]{2,1,0:T(8,128)(2,1)S(1)}, bf16[2,512,384]{2,1,0:T(8,128)(2,1)S(1)}, u32[]{:S(2)}, u32[]{:S(2)}) collective-permute-start(bf16[2,512,384]{2,1,0:T(8,128)(2,1)S(1)} %pad_maximum_fusion.2.pair_ref), channel_id=1, source_target_pairs={{0,3},{1,0},{2,1},{3,2},{4,7},{5,4},{6,5},{7,6},{8,11},{9,8},{10,9... | collective-permute-start | bytes 2359304 | tf_op jit(solution)/shard_map/ppermute | solution.py:257
  34.4 20.6 %collective-permute-start.7 = (bf16[1,96,1920]{2,1,0:T(8,128)(2,1)}, bf16[1,96,1920]{2,1,0:T(8,128)(2,1)}, u32[]{:S(2)}, u32[]{:S(2)}) collective-permute-start(bf16[1,96,1920]{2,1,0:T(8,128)(2,1)} %collective-permute-done.2.refs_4_), channel_id=1, source_target_pairs={{0,16},{16,32},{32,48},{48,64},{64,80},{80,96},{96,112},{112,0},{1... | collective-permute-start | bytes 1105928 | tf_op jit(solution)/shard_map/ppermute | solution.py:254
  35.6 19.4 %collective-permute-start.8 = (bf16[1,96,1920]{2,1,0:T(8,128)(2,1)}, bf16[1,96,1920]{2,1,0:T(8,128)(2,1)}, u32[]{:S(2)}, u32[]{:S(2)}) collective-permute-start(bf16[1,96,1920]{2,1,0:T(8,128)(2,1)} %collective-permute-done.3.refs_5_), channel_id=1, source_target_pairs={{0,112},{16,0},{32,16},{48,32},{64,48},{80,64},{96,80},{112,96},{1... | collective-permute-start | bytes 1105928 | tf_op jit(solution)/shard_map/ppermute | solution.py:257
  60.5 21.0 %copy-start.5 = (bf16[2,512,384]{2,1,0:T(8,128)(2,1)S(1)}, bf16[2,512,384]{2,1,0:T(8,128)(2,1)}, u32[]{:S(2)}) copy-start(bf16[2,512,384]{2,1,0:T(8,128)(2,1)} %copy-done.4) | copy-start | bytes 2359300
  60.5 48.9 %collective-permute-start.17 = (bf16[3,768,384]{2,1,0:T(8,128)(2,1)S(1)}, bf16[3,768,384]{2,1,0:T(8,128)(2,1)S(1)}, u32[]{:S(2)}, u32[]{:S(2)}) collective-permute-start(bf16[3,768,384]{2,1,0:T(8,128)(2,1)S(1)} %constant_dynamic-slice_fusion), channel_id=1, source_target_pairs={{0,128},{128,0},{1,129},{129,1},{2,130},{130,2},{3,131},{131,3},{4... | collective-permute-start | bytes 5308424 | tf_op jit(solution)/shard_map/ppermute | solution.py:117
  63.3 13.4 %collective-permute-start.13 = (bf16[1,96,1920]{2,1,0:T(8,128)(2,1)}, bf16[1,96,1920]{2,1,0:T(8,128)(2,1)S(1)}, u32[]{:S(2)}, u32[]{:S(2)}) collective-permute-start(bf16[1,96,1920]{2,1,0:T(8,128)(2,1)} %collective-permute-done.8.refs_7_), channel_id=1, source_target_pairs={{0,112},{16,0},{32,16},{48,32},{64,48},{80,64},{96,80},{112,96},{1... | collective-permute-start | bytes 1105928 | tf_op jit(solution)/shard_map/ppermute | solution.py:257
  65.4 14.7 %collective-permute-start.11 = (bf16[1,96,1920]{2,1,0:T(8,128)(2,1)}, bf16[1,96,1920]{2,1,0:T(8,128)(2,1)S(1)}, u32[]{:S(2)}, u32[]{:S(2)}) collective-permute-start(bf16[1,96,1920]{2,1,0:T(8,128)(2,1)} %collective-permute-done.7.refs_6_), channel_id=1, source_target_pairs={{0,16},{16,32},{32,48},{48,64},{64,80},{80,96},{96,112},{112,0},{1... | collective-permute-start | bytes 1105928 | tf_op jit(solution)/shard_map/ppermute | solution.py:254
  76.7 38.3 %copy-start.19 = (bf16[1,96,1920]{2,1,0:T(8,128)(2,1)}, bf16[1,96,1920]{2,1,0:T(8,128)(2,1)S(1)}, u32[]{:S(2)}) copy-start(bf16[1,96,1920]{2,1,0:T(8,128)(2,1)S(1)} %collective-permute-done.13.refs_10_) | copy-start | bytes 1105924
  76.7 10.6 %collective-permute-start.14 = (bf16[1,48,1920]{2,1,0:T(8,128)(2,1)S(1)}, bf16[1,48,1920]{2,1,0:T(8,128)(2,1)S(1)}, u32[]{:S(2)}, u32[]{:S(2)}) collective-permute-start(bf16[1,48,1920]{2,1,0:T(8,128)(2,1)S(1)} %slice.25), channel_id=1, source_target_pairs={{0,112},{16,0},{32,16},{48,32},{64,48},{80,64},{96,80},{112,96},{1... | collective-permute-start | bytes 552968 | tf_op jit(solution)/shard_map/ppermute | solution.py:257
  80.2 34.8 %copy-start.20 = (bf16[1,96,1920]{2,1,0:T(8,128)(2,1)}, bf16[1,96,1920]{2,1,0:T(8,128)(2,1)S(1)}, u32[]{:S(2)}) copy-start(bf16[1,96,1920]{2,1,0:T(8,128)(2,1)S(1)} %collective-permute-done.11.refs_9_) | copy-start | bytes 1105924
  80.2 10.6 %collective-permute-start.12 = (bf16[1,48,1920]{2,1,0:T(8,128)(2,1)S(1)}, bf16[1,48,1920]{2,1,0:T(8,128)(2,1)S(1)}, u32[]{:S(2)}, u32[]{:S(2)}) collective-permute-start(bf16[1,48,1920]{2,1,0:T(8,128)(2,1)S(1)} %slice.24), channel_id=1, source_target_pairs={{0,16},{16,32},{32,48},{48,64},{64,80},{80,96},{96,112},{112,0},{1... | collective-permute-start | bytes 552968 | tf_op jit(solution)/shard_map/ppermute | solution.py:254
  80.3 27.4 %collective-permute-start.9 = (bf16[512,384]{1,0:T(8,128)(2,1)S(1)}, bf16[512,384]{1,0:T(8,128)(2,1)S(1)}, u32[]{:S(2)}, u32[]{:S(2)}) collective-permute-start(bf16[512,384]{1,0:T(8,128)(2,1)S(1)} %slice_bitcast_fusion.1), channel_id=1, source_target_pairs={{0,1},{1,2},{2,3},{3,0},{4,5},{5,6},{6,7},{7,4},{8,9},{9,10},{10,1... | collective-permute-start | bytes 1179656 | tf_op jit(solution)/shard_map/ppermute | solution.py:254
  81.6 38.1 %copy-start.12 = (f32[3072]{0:T(1024)S(1)}, f32[3072]{0:T(1024)}, u32[]{:S(2)}) copy-start(f32[3072]{0:T(1024)} %param.9) | copy-start | bytes 36868
  81.6 27.1 %collective-permute-start.10 = (bf16[512,384]{1,0:T(8,128)(2,1)S(1)}, bf16[512,384]{1,0:T(8,128)(2,1)S(1)}, u32[]{:S(2)}, u32[]{:S(2)}) collective-permute-start(bf16[512,384]{1,0:T(8,128)(2,1)S(1)} %slice_bitcast_fusion), channel_id=1, source_target_pairs={{0,3},{1,0},{2,1},{3,2},{4,7},{5,4},{6,5},{7,6},{8,11},{9,8},{10,9... | collective-permute-start | bytes 1179656 | tf_op jit(solution)/shard_map/ppermute | solution.py:257
  87.3 45.3 %copy-start.21 = (bf16[1,48,1920]{2,1,0:T(8,128)(2,1)}, bf16[1,48,1920]{2,1,0:T(8,128)(2,1)S(1)}, u32[]{:S(2)}) copy-start(bf16[1,48,1920]{2,1,0:T(8,128)(2,1)S(1)} %collective-permute-done.14.refs_12_) | copy-start | bytes 552964
  87.3 20.4 %collective-permute-start.15 = (bf16[1,96,1920]{2,1,0:T(8,128)(2,1)S(1)}, bf16[1,96,1920]{2,1,0:T(8,128)(2,1)S(1)}, u32[]{:S(2)}, u32[]{:S(2)}) collective-permute-start(bf16[1,96,1920]{2,1,0:T(8,128)(2,1)S(1)} %get-tuple-element.32), channel_id=1, source_target_pairs={{0,16},{16,32},{32,48},{48,64},{64,80},{80,96},{96,112},{112,0},{1... | collective-permute-start | bytes 1105928 | tf_op jit(solution)/shard_map/ppermute | solution.py:254
  90.8 27.7 %copy-start.22 = (bf16[1,48,1920]{2,1,0:T(8,128)(2,1)}, bf16[1,48,1920]{2,1,0:T(8,128)(2,1)S(1)}, u32[]{:S(2)}) copy-start(bf16[1,48,1920]{2,1,0:T(8,128)(2,1)S(1)} %collective-permute-done.12.refs_11_) | copy-start | bytes 552964
  90.8 16.9 %collective-permute-start.16 = (bf16[1,96,1920]{2,1,0:T(8,128)(2,1)S(1)}, bf16[1,96,1920]{2,1,0:T(8,128)(2,1)S(1)}, u32[]{:S(2)}, u32[]{:S(2)}) collective-permute-start(bf16[1,96,1920]{2,1,0:T(8,128)(2,1)S(1)} %get-tuple-element.33), channel_id=1, source_target_pairs={{0,112},{16,0},{32,16},{48,32},{64,48},{80,64},{96,80},{112,96},{1... | collective-permute-start | bytes 1105928 | tf_op jit(solution)/shard_map/ppermute | solution.py:257
  109.5 9.0 %collective-permute-start.18 = (bf16[3,768,384]{2,1,0:T(8,128)(2,1)S(1)}, bf16[3,768,384]{2,1,0:T(8,128)(2,1)S(1)}, u32[]{:S(2)}, u32[]{:S(2)}) collective-permute-start(bf16[3,768,384]{2,1,0:T(8,128)(2,1)S(1)} %collective-permute-done.17.near_ref), channel_id=1, source_target_pairs={{0,8},{8,0},{1,9},{9,1},{2,10},{10,2},{3,11},{11,3},{4,12},{12,4},... | collective-permute-start | bytes 5308424 | tf_op jit(solution)/shard_map/ppermute | solution.py:294
  119.7 27.4 %collective-permute-start.19 = (bf16[3,96,1920]{2,1,0:T(8,128)(2,1)}, bf16[3,96,1920]{2,1,0:T(8,128)(2,1)}, u32[]{:S(2)}, u32[]{:S(2)}) collective-permute-start(bf16[3,96,1920]{2,1,0:T(8,128)(2,1)} %pad_maximum_fusion.1), channel_id=1, source_target_pairs={{0,128},{128,0},{1,129},{129,1},{2,130},{130,2},{3,131},{131,3},{4... | collective-permute-start | bytes 3317768 | tf_op jit(solution)/shard_map/ppermute | solution.py:117
  123.0 3.0 %copy-start.1 = (bf16[3,1536,384]{2,1,0:T(8,128)(2,1)S(1)}, bf16[3,1536,384]{2,1,0:T(8,128)(2,1)}, u32[]{:S(2)}) copy-start(bf16[3,1536,384]{2,1,0:T(8,128)(2,1)} %all-gather.3.cloned.1.call-done.own_ref) | copy-start | bytes 10616836
  123.0 3.0 %copy-start.3 = (bf16[3,768,384]{2,1,0:T(8,128)(2,1)S(1)}, bf16[3,768,384]{2,1,0:T(8,128)(2,1)}, u32[]{:S(2)}) copy-start(bf16[3,768,384]{2,1,0:T(8,128)(2,1)} %copy-done.2) | copy-start | bytes 5308420
  123.0 3.0 %copy-start.13 = (f32[3,128]{1,0:T(4,128)S(1)}, f32[3,128]{1,0:T(4,128)}, u32[]{:S(2)}) copy-start(f32[3,128]{1,0:T(4,128)} %q_gain_ref.1) | copy-start | bytes 4612
  123.0 3.0 %copy-start.14 = (f32[3,128]{1,0:T(4,128)S(1)}, f32[3,128]{1,0:T(4,128)}, u32[]{:S(2)}) copy-start(f32[3,128]{1,0:T(4,128)} %k_gain_ref.1) | copy-start | bytes 4612
  126.0 6.6 %copy-start = (bf16[512,3072]{1,0:T(8,128)(2,1)}, bf16[512,3072]{1,0:T(8,128)(2,1)S(1)}, u32[]{:S(2)}) copy-start(bf16[512,3072]{1,0:T(8,128)(2,1)S(1)} %shard_map.82.x_ref) | copy-start | bytes 9437188
  132.6 26.1 %copy-start.7 = (bf16[512,384]{1,0:T(8,128)(2,1)}, bf16[512,384]{1,0:T(8,128)(2,1)S(1)}, u32[]{:S(2)}) copy-start(bf16[512,384]{1,0:T(8,128)(2,1)S(1)} %shard_map.83.refs_1_) | copy-start | bytes 1179652
  157.4 10.5 %collective-permute-start.24 = (bf16[512,1536]{1,0:T(8,128)(2,1)}, bf16[512,1536]{1,0:T(8,128)(2,1)S(1)}, u32[]{:S(2)}, u32[]{:S(2)}) collective-permute-start(bf16[512,1536]{1,0:T(8,128)(2,1)} %shard_map.84.refs_2_), channel_id=1, source_target_pairs={{0,8},{8,0},{1,9},{9,1},{2,10},{10,2},{3,11},{11,3},{4,12},{12,4},... | collective-permute-start | bytes 4718600 | tf_op jit(solution)/shard_map/ppermute | solution.py:308
  158.6 9.3 %collective-permute-start.23 = (bf16[512,384]{1,0:T(8,128)(2,1)S(1)}, bf16[512,384]{1,0:T(8,128)(2,1)S(1)}, u32[]{:S(2)}, u32[]{:S(2)}) collective-permute-start(bf16[512,384]{1,0:T(8,128)(2,1)S(1)} %shard_map.83.refs_1_), channel_id=1, source_target_pairs={{0,8},{8,0},{1,9},{9,1},{2,10},{10,2},{3,11},{11,3},{4,12},{12,4},... | collective-permute-start | bytes 1179656 | tf_op jit(solution)/shard_map/ppermute | solution.py:308
  179.7 22.6 %collective-permute-start.25 = (bf16[4,192,512]{2,1,0:T(8,128)(2,1)S(1)}, bf16[4,192,512]{2,1,0:T(8,128)(2,1)}, u32[]{:S(2)}, u32[]{:S(2)}) collective-permute-start(bf16[4,192,512]{2,1,0:T(8,128)(2,1)S(1)} %get-tuple-element.50), channel_id=1, source_target_pairs={{0,8},{8,0},{1,9},{9,1},{2,10},{10,2},{3,11},{11,3},{4,12},{12,4},... | collective-permute-start | bytes 2359304 | tf_op jit(solution)/shard_map/ppermute | solution.py:99
  180.0 26.0 %collective-permute-start.27 = (bf16[4,192,512]{2,1,0:T(8,128)(2,1)S(1)}, bf16[4,192,512]{2,1,0:T(8,128)(2,1)}, u32[]{:S(2)}, u32[]{:S(2)}) collective-permute-start(bf16[4,192,512]{2,1,0:T(8,128)(2,1)S(1)} %get-tuple-element.49), channel_id=1, source_target_pairs={{0,12},{4,8},{8,4},{12,0},{1,13},{5,9},{9,5},{13,1},{2,14},{6,10},... | collective-permute-start | bytes 2359304 | tf_op jit(solution)/shard_map/ppermute | solution.py:98
  181.0 12.2 %collective-permute-start.20 = (bf16[2,192,512]{2,1,0:T(8,128)(2,1)}, bf16[2,192,512]{2,1,0:T(8,128)(2,1)S(1)}, u32[]{:S(2)}, u32[]{:S(2)}) collective-permute-start(bf16[2,192,512]{2,1,0:T(8,128)(2,1)} %get-tuple-element.53), channel_id=1, source_target_pairs={{0,2},{1,3},{2,0},{3,1},{4,6},{5,7},{6,4},{7,5},{8,10},{9,11},{10,... | collective-permute-start | bytes 1179656 | tf_op jit(solution)/shard_map/ppermute | solution.py:88
  183.8 18.6 %collective-permute-start.21 = (bf16[2,192,512]{2,1,0:T(8,128)(2,1)}, bf16[2,192,512]{2,1,0:T(8,128)(2,1)}, u32[]{:S(2)}, u32[]{:S(2)}) collective-permute-start(bf16[2,192,512]{2,1,0:T(8,128)(2,1)} %get-tuple-element.52), channel_id=1, source_target_pairs={{0,1},{1,2},{2,3},{3,0},{4,5},{5,6},{6,7},{7,4},{8,9},{9,10},{10,1... | collective-permute-start | bytes 1179656 | tf_op jit(solution)/shard_map/ppermute | solution.py:88
  184.1 18.3 %collective-permute-start.22 = (bf16[2,192,512]{2,1,0:T(8,128)(2,1)}, bf16[2,192,512]{2,1,0:T(8,128)(2,1)}, u32[]{:S(2)}, u32[]{:S(2)}) collective-permute-start(bf16[2,192,512]{2,1,0:T(8,128)(2,1)} %get-tuple-element.51), channel_id=1, source_target_pairs={{0,3},{1,0},{2,1},{3,2},{4,7},{5,4},{6,5},{7,6},{8,11},{9,8},{10,9... | collective-permute-start | bytes 1179656 | tf_op jit(solution)/shard_map/ppermute | solution.py:88
  204.4 7.8 %copy-start.17 = (bf16[512,384]{1,0:T(8,128)(2,1)S(1)}, bf16[512,384]{1,0:T(8,128)(2,1)}, u32[]{:S(2)}) copy-start(bf16[512,384]{1,0:T(8,128)(2,1)} %param.8) | copy-start | bytes 1179652
  204.4 8.0 %collective-permute-start.26 = (bf16[192,512]{1,0:T(8,128)(2,1)}, bf16[192,512]{1,0:T(8,128)(2,1)S(1)}, u32[]{:S(2)}, u32[]{:S(2)}) collective-permute-start(bf16[192,512]{1,0:T(8,128)(2,1)} %fusion.7), channel_id=1, source_target_pairs={{0,4},{4,0},{1,5},{5,1},{2,6},{6,2},{3,7},{7,3},{8,12},{12,8},{9,1... | collective-permute-start | bytes 589832 | tf_op jit(solution)/shard_map/ppermute | solution.py:111
  208.6 6.2 %collective-permute-start.30 = (bf16[192,512]{1,0:T(8,128)(2,1)}, bf16[192,512]{1,0:T(8,128)(2,1)S(1)}, u32[]{:S(2)}, u32[]{:S(2)}) collective-permute-start(bf16[192,512]{1,0:T(8,128)(2,1)} %get-tuple-element.57), channel_id=1, source_target_pairs={{0,3},{1,0},{2,1},{3,2},{4,7},{5,4},{6,5},{7,6},{8,11},{9,8},{10,9... | collective-permute-start | bytes 589832 | tf_op jit(solution)/shard_map/ppermute | solution.py:88
  211.0 8.1 %collective-permute-start.29 = (bf16[192,512]{1,0:T(8,128)(2,1)}, bf16[192,512]{1,0:T(8,128)(2,1)}, u32[]{:S(2)}, u32[]{:S(2)}) collective-permute-start(bf16[192,512]{1,0:T(8,128)(2,1)} %get-tuple-element.58), channel_id=1, source_target_pairs={{0,1},{1,2},{2,3},{3,0},{4,5},{5,6},{6,7},{7,4},{8,9},{9,10},{10,1... | collective-permute-start | bytes 589832 | tf_op jit(solution)/shard_map/ppermute | solution.py:88
  211.0 9.9 %collective-permute-start.28 = (bf16[192,512]{1,0:T(8,128)(2,1)}, bf16[192,512]{1,0:T(8,128)(2,1)}, u32[]{:S(2)}, u32[]{:S(2)}) collective-permute-start(bf16[192,512]{1,0:T(8,128)(2,1)} %get-tuple-element.56), channel_id=1, source_target_pairs={{0,2},{1,3},{2,0},{3,1},{4,6},{5,7},{6,4},{7,5},{8,10},{9,11},{10,... | collective-permute-start | bytes 589832 | tf_op jit(solution)/shard_map/ppermute | solution.py:88
  (12 other events, 14.4 us)
Sparse Core Ops, SparseCore 0:
  9.2 48.7 all-gather.2
  59.8 75.5 all-gather.4
where the time goes:
time: 231 us; the launch traced here: 230 us
  waiting for transfers between devices  103 us (45%)
  starting transfers between devices  49.1 us (21%)
  Pallas kernels  36.4 us (16%)
  local copies, waits for them, and re-layouts  17.2 us (7%)
  between operations  13.8 us (6%)
  other arithmetic  10.6 us (5%)
    ppermute x7, waiting for transfers between devices, up(): return lax.ppermute(v, axis, shift(size, 1))  35.7 us
    ppermute x6, waiting for transfers between devices, to_peers_x(): lax.ppermute(pick(blocks, (x + k) % 4, axis), 'x', shift(4, k))  24.4 us
    ppermute x4, waiting for transfers between devices, across(): return lax.ppermute(v, 'yh', SWAP)  22.8 us
    ppermute x7, starting transfers between devices, down(): return lax.ppermute(v, axis, shift(size, -1))  17.1 us
    pallas_call x2, Pallas kernels, out_terms(): pl.pallas_call(functools.partial(out_kernel, places, rows), in_specs=[pl....  16.5 us
    ppermute x7, waiting for transfers between devices, down(): return lax.ppermute(v, axis, shift(size, -1))  13.9 us
    pallas_call x1, Pallas kernels, up_gelu(): pl.pallas_call(up_kernel, grid=(hidden // tile,), in_specs=[pl.BlockSpec(...  10.3 us
    unnamed x55, local copies, waits for them, and re-layouts  9.13 us
  transfers between devices with their start and end apart: 33, of which 14 were waited for; matrix products, arithmetic and copies ran while one was open for 7% of the time, Pallas kernels for 8%

commit v1 on v0

--- a/solution.py
+++ b/solution.py
@@ -123,7 +123,7 @@
 
 
 def up_gelu(x, w):
-    tile = 256
+    tile = 512
     rows, depth = x.shape
     hidden = w.shape[1]
     return pl.pallas_call(
@@ -135,7 +135,7 @@
         ],
         out_specs=pl.BlockSpec((rows, tile), lambda i: (0, i)),
         out_shape=jax.ShapeDtypeStruct((rows, hidden), jnp.bfloat16),
-        compiler_params=pltpu.CompilerParams(vmem_limit_bytes=53 * 2**20),
+        compiler_params=pltpu.CompilerParams(vmem_limit_bytes=46 * 2**20),
     )(x, w)
 
 
@@ -186,35 +186,42 @@
     )(starts, x, own, near, far, q_gain, k_gain)
 
 
-def out_kernel(places, rows, *refs):
-    at_ref, attended_ref, activated_ref = refs[:3]
-    shards = refs[3 : 3 + len(places)]
-    out_ref, held, sem = refs[3 + len(places) :]
+def gather_kernel(places, slots, rows, *refs):
+    out_ref = refs[-1]
+    for group, ref in zip(places, refs):
+        for i, (other, offset, start) in enumerate(group):
+            at = slots.index((other, offset)) * rows + start
+            out_ref[at : at + ref.shape[1]] = ref[i]
+
+
+def side_by_side(rows, shards):
+    places = tuple(places for places, _ in shards)
+    slots = list(dict.fromkeys(place[:2] for group in places for place in group))
+    width = shards[0][1].shape[2]
+    vmem = pl.BlockSpec(memory_space=pltpu.VMEM)
+    gathered = pl.pallas_call(
+        functools.partial(gather_kernel, places, slots, rows),
+        in_specs=[vmem] * len(shards),
+        out_specs=vmem,
+        out_shape=jax.ShapeDtypeStruct((16 * rows, width), jnp.bfloat16),
+        compiler_params=pltpu.CompilerParams(vmem_limit_bytes=32 * 2**20),
+    )(*(arrays for _, arrays in shards))
+    return gathered, slots
+
+
+def out_kernel(slots, at_ref, weights_ref, attended_ref, activated_ref, out_ref):
     yh, z = at_ref[0], at_ref[1]
-    slots = list(dict.fromkeys(place[:2] for group in places for place in group))
-    copies = [[] for _ in slots]
-    count = 0
-    for group, shard in zip(places, shards):
-        for i, (other, offset, start) in enumerate(group):
-            slot = slots.index((other, offset))
-            at = pl.ds(slot * rows + start, shard.shape[1])
-            copy = pltpu.make_async_copy(shard.at[i], held.at[at], sem.at[count])
-            copy.start()
-            copies[slot].append(copy)
-            count += 1
+    rows = out_ref.shape[1]
     split = attended_ref.shape[1]
     contract = (((1,), (1,)), ((), ()))
     step = 4
     for first in range(0, len(slots), step):
-        for slot in range(first, first + step):
-            for copy in copies[slot]:
-                copy.wait()
         at = slice(first * rows, (first + step) * rows)
         total = lax.dot_general(
-            held[at, :split], attended_ref[...], contract, preferred_element_type=jnp.float32
+            weights_ref[at, :split], attended_ref[...], contract, preferred_element_type=jnp.float32
         )
         total += lax.dot_general(
-            held[at, split:], activated_ref[...], contract, preferred_element_type=jnp.float32
+            weights_ref[at, split:], activated_ref[...], contract, preferred_element_type=jnp.float32
         )
         total = total.astype(out_ref.dtype)
         for i in range(step):
@@ -223,26 +230,17 @@
             out_ref[owner] = total[i * rows : (i + 1) * rows]
 
 
-def out_terms(place, rows, attended, activated, shards):
-    places = tuple(places for places, _ in shards)
+def out_terms(place, slots, weights, attended, activated):
+    rows = weights.shape[0] // 16
     tokens = attended.shape[0]
-    width = attended.shape[1] + activated.shape[1]
     vmem = pl.BlockSpec(memory_space=pltpu.VMEM)
     return pl.pallas_call(
-        functools.partial(out_kernel, places, rows),
-        in_specs=[pl.BlockSpec(memory_space=pltpu.SMEM), vmem, vmem]
-        + [pl.BlockSpec(memory_space=pltpu.HBM)] * len(places),
+        functools.partial(out_kernel, slots),
+        in_specs=[pl.BlockSpec(memory_space=pltpu.SMEM), vmem, vmem, vmem],
         out_specs=vmem,
         out_shape=jax.ShapeDtypeStruct((16, rows, tokens), jnp.bfloat16),
-        scratch_shapes=[
-            pltpu.VMEM((16 * rows, width), jnp.bfloat16),
-            pltpu.SemaphoreType.DMA((sum(len(group) for group in places),)),
-        ],
-        compiler_params=pltpu.CompilerParams(vmem_limit_bytes=58 * 2**20),
-        cost_estimate=pl.CostEstimate(
-            flops=32 * rows * width * tokens, bytes_accessed=0, transcendentals=0
-        ),
-    )(place, attended, activated, *(arrays for _, arrays in shards))
+        compiler_params=pltpu.CompilerParams(vmem_limit_bytes=32 * 2**20),
+    )(place, weights, attended, activated)
 
 
 def local(tokens, ln_gain, w_qkv, w_up, q_gain, k_gain, w_proj, w_down):
@@ -290,7 +288,7 @@
     other_low, other_high = up(other_low), down(other_high)
     shards += [([(0, 4, 0)], end_a), ([(0, 4, half)], end_b)]
     shards += [([(1, -2, 0)], other_low), ([(1, 2, 0)], other_high)]
-    other_c = tie(other_c, (far_a, far_b, end_a, end_b, other_low, other_high))
+    other_c = tie(other_c, (far_a, far_b, end_a, end_b))
     other_d = lax.ppermute(other_c, "c", SWAP)
 
     normed = norm_tokens(lax.axis_index("x"), ln_gain, pair, right, left, far_a, far_b)
@@ -302,12 +300,13 @@
     distant = across(tie(distant, other_d))
     shards += [([(1, -3, 0), (1, 4, 0), (1, 3, 0)], distant)]
     attended = attention(starts, normed, own_qkv, other_c, other_d, q_gain, k_gain)
-    activated = up_gelu(tie(normed, (attended, distant)), up_all)
+    weights, slots = side_by_side(piece, shards)
+    activated = up_gelu(tie(normed, (attended, weights)), up_all)
 
     place = jnp.stack([yh, z])
     swapped = (lax.ppermute(attended, "c", SWAP), lax.ppermute(activated, "c", SWAP))
-    mine = out_terms(place, piece, attended, activated, shards)
-    theirs = out_terms(place, piece, *tie(swapped, mine), shards)
+    mine = out_terms(place, slots, weights, attended, activated)
+    theirs = out_terms(place, slots, weights, *tie(swapped, mine))
     mine, theirs = scatter_end(*scatter_start(mine, theirs))
     mine = mine.reshape(2, 1, piece, tok_count)
     theirs = theirs.reshape(2, 1, piece, tok_count)

time: 231 us -> 212 us (0.918)
  waiting for transfers between devices: 103 us -> 82.1 us
  Pallas kernels: 36.4 us -> 31.3 us
  local copies, waits for them, and re-layouts: 17.2 us -> 21.9 us
    ppermute x6, waiting for transfers between devices: 24.4 us -> 4.66 us  [to_peers_x(): lax.ppermute(pick(blocks, (x + k) % 4, axis), 'x', shift(4, k))]
    ppermute x7, waiting for transfers between devices: 13.9 us -> 0.02 us  [down(): return lax.ppermute(v, axis, shift(size, -1))]
    ppermute x1, waiting for transfers between devices: 0.01 us -> 13.6 us  [scatter_start(): over_y = lax.ppermute(pick(theirs, 1 - yl, 0), ('c', 'yl'), both)]
    unnamed x55 -> x65, local copies, waits for them, and re-layouts: 9.13 us -> 15.2 us
    pallas_call x2 -> x3, Pallas kernels: 16.5 us -> 11.2 us  [the longest x2 8.96 us: out_terms(): pl.pallas_call(functools.partial(out_kernel, slots), in_specs=[pl.BlockSp...]
    ppermute x1, starting transfers between devices: 5.53 us -> 1.14 us  [local(): other_d = lax.ppermute(other_c, 'c', SWAP)]
    ppermute x4, starting transfers between devices: 6.26 us -> 8.97 us  [across(): return lax.ppermute(v, 'yh', SWAP)]
    squeeze x3, local copies, waits for them, and re-layouts: 3.56 us -> 1.08 us  [pick(): return lax.dynamic_index_in_dim(blocks, at, axis, keepdims=False)]
  transfers between devices with their start and end apart: 33 -> 33, of which waited for: 14 -> 12; matrix products, arithmetic and copies ran while one was open for 7% -> 7% of each run, Pallas kernels for 8% -> 9%
where the time goes in v1:
time: 212 us; the launch traced here: 211 us
  waiting for transfers between devices  82.1 us (39%)
  starting transfers between devices  50.9 us (24%)
  Pallas kernels  31.3 us (15%)
  local copies, waits for them, and re-layouts  21.9 us (10%)
  between operations  13.8 us (7%)
  other arithmetic  11 us (5%)
    ppermute x7, waiting for transfers between devices, up(): return lax.ppermute(v, axis, shift(size, 1))  37.2 us
    ppermute x4, waiting for transfers between devices, across(): return lax.ppermute(v, 'yh', SWAP)  21.3 us
    ppermute x7, starting transfers between devices, down(): return lax.ppermute(v, axis, shift(size, -1))  19.3 us
    unnamed x65, local copies, waits for them, and re-layouts  15.2 us
    ppermute x1, waiting for transfers between devices, scatter_start(): over_y = lax.ppermute(pick(theirs, 1 - yl, 0), ('c', 'yl'), both)  13.6 us
    ppermute x6, starting transfers between devices, to_peers_x(): lax.ppermute(pick(blocks, (x + k) % 4, axis), 'x', shift(4, k))  11.1 us
    ppermute x4, starting transfers between devices, across(): return lax.ppermute(v, 'yh', SWAP)  8.97 us
    pallas_call x2, Pallas kernels, out_terms(): pl.pallas_call(functools.partial(out_kernel, slots), in_specs=[pl.BlockSp...  8.96 us
  transfers between devices with their start and end apart: 33, of which 12 were waited for; matrix products, arithmetic and copies ran while one was open for 7% of the time, Pallas kernels for 9%

profile of v1, /device:TPU:1, one launch (start us, length us, event | category | flops | bytes accessed | tf_op | source)
XLA Modules:
  0.0 211.1 jit_solution(732129782650689630)
XLA Ops:
  7.3 2.2 %collective-permute-start = (bf16[512,384]{1,0:T(8,128)(2,1)}, bf16[512,384]{1,0:T(8,128)(2,1)S(1)}, u32[]{:S(2)}, u32[]{:S(2)}) collective-permute-start(bf16[512,384]{1,0:T(8,128)(2,1)} %param.8), channel_id=1, source_target_pairs={{0,4},{4,0},{1,5},{5,1},{2,6},{6,2},{3,7},{7,3},{8,12},{12,8},{9,1... | collective-permute-start | bytes 1179656 | tf_op jit(solution)/shard_map/ppermute | solution.py:263
  10.5 1.7 collective-permute-start.2
  12.2 4.0 %collective-permute-start.3 = (bf16[1,96,1920]{2,1,0:T(8,128)(2,1)S(1)}, bf16[1,96,1920]{2,1,0:T(8,128)(2,1)}, u32[]{:S(2)}, u32[]{:S(2)}) collective-permute-start(bf16[1,96,1920]{2,1,0:T(8,128)(2,1)S(1)} %maximum_bitcast_fusion.refs_0_), channel_id=1, source_target_pairs={{0,112},{16,0},{32,16},{48,32},{64,48},{80,64},{96,80},{112,96},{1... | collective-permute-start | bytes 1105928 | tf_op jit(solution)/shard_map/ppermute | solution.py:255
  16.3 2.6 %collective-permute-start.1 = (bf16[96,1536]{1,0:T(8,128)(2,1)}, bf16[96,1536]{1,0:T(8,128)(2,1)S(1)}, u32[]{:S(2)}, u32[]{:S(2)}) collective-permute-start(bf16[96,1536]{1,0:T(8,128)(2,1)} %param.11), channel_id=1, source_target_pairs={{0,128},{128,0},{1,129},{129,1},{2,130},{130,2},{3,131},{131,3},{4... | collective-permute-start | bytes 884744 | tf_op jit(solution)/shard_map/ppermute | solution.py:117
  18.9 8.3 %collective-permute-done.1 = bf16[96,1536]{1,0:T(8,128)(2,1)S(1)} collective-permute-done((bf16[96,1536]{1,0:T(8,128)(2,1)}, bf16[96,1536]{1,0:T(8,128)(2,1)S(1)}, u32[]{:S(2)}, u32[]{:S(2)}) %collective-permute-start.1) | collective-permute-done | bytes 294944 | tf_op jit(solution)/shard_map/ppermute | solution.py:117
  27.2 2.1 maximum_select_fusion
  29.3 2.2 %pad_maximum_fusion = bf16[3,96,1920]{2,1,0:T(8,128)(2,1)} fusion(bf16[1,96,1920]{2,1,0:T(8,128)(2,1)} %collective-permute-done.3.refs_2_, bf16[1,96,1920]{2,1,0:T(8,128)(2,1)S(1)} %maximum_bitcast_fusion.refs_0_, bf16[1,96,1920]{2,1,0:T(8,128)(2,1)S(1)} %collective-permute-done.2.refs_1_), kind=kLoop, calls=%fused_computation.1 | loop fusion | flops 1105920 | bytes 2211840 | tf_op jit(solution)/shard_map/concatenate | solution.py:273
  32.4 1.3 collective-permute-start.6
  33.7 1.5 collective-permute-start.7
  35.2 1.3 collective-permute-start.4
  36.5 4.1 %collective-permute-start.5 = (bf16[1,96,1920]{2,1,0:T(8,128)(2,1)}, bf16[1,96,1920]{2,1,0:T(8,128)(2,1)}, u32[]{:S(2)}, u32[]{:S(2)}) collective-permute-start(bf16[1,96,1920]{2,1,0:T(8,128)(2,1)} %collective-permute-done.3.refs_2_), channel_id=1, source_target_pairs={{0,112},{16,0},{32,16},{48,32},{64,48},{80,64},{96,80},{112,96},{1... | collective-permute-start | bytes 1105928 | tf_op jit(solution)/shard_map/ppermute | solution.py:255
  40.5 14.1 %collective-permute-done.4.refs_3_ = bf16[1,96,1920]{2,1,0:T(8,128)(2,1)} collective-permute-done((bf16[1,96,1920]{2,1,0:T(8,128)(2,1)S(1)}, bf16[1,96,1920]{2,1,0:T(8,128)(2,1)}, u32[]{:S(2)}, u32[]{:S(2)}) %collective-permute-start.4) | collective-permute-done | bytes 368672 | tf_op jit(solution)/shard_map/ppermute | solution.py:252
  54.7 3.3 %all-gather.3.cloned.1.call-done.own_ref = bf16[3,1536,384]{2,1,0:T(8,128)(2,1)} async-done(((bf16[3,96,384]{2,1,0:T(8,128)(2,1)}), bf16[3,1536,384]{2,1,0:T(8,128)(2,1)}) %all-gather.3.cloned.1.call-update) | async-done | bytes 3538960 | tf_op jit(solution)/shard_map/all_gather | solution.py:257
  57.9 1.7 constant_dynamic-slice_fusion
  59.6 2.8 %collective-permute-start.15 = (bf16[3,768,384]{2,1,0:T(8,128)(2,1)S(1)}, bf16[3,768,384]{2,1,0:T(8,128)(2,1)S(1)}, u32[]{:S(2)}, u32[]{:S(2)}) collective-permute-start(bf16[3,768,384]{2,1,0:T(8,128)(2,1)S(1)} %constant_dynamic-slice_fusion), channel_id=1, source_target_pairs={{0,128},{128,0},{1,129},{129,1},{2,130},{130,2},{3,131},{131,3},{4... | collective-permute-start | bytes 5308424 | tf_op jit(solution)/shard_map/ppermute | solution.py:117
  62.5 2.3 %collective-permute-start.10 = (bf16[1,96,1920]{2,1,0:T(8,128)(2,1)}, bf16[1,96,1920]{2,1,0:T(8,128)(2,1)S(1)}, u32[]{:S(2)}, u32[]{:S(2)}) collective-permute-start(bf16[1,96,1920]{2,1,0:T(8,128)(2,1)} %collective-permute-done.5.refs_4_), channel_id=1, source_target_pairs={{0,112},{16,0},{32,16},{48,32},{64,48},{80,64},{96,80},{112,96},{1... | collective-permute-start | bytes 1105928 | tf_op jit(solution)/shard_map/ppermute | solution.py:255
  66.6 2.0 collective-permute-start.17
  68.7 6.9 %collective-permute-done.9.refs_6_ = bf16[1,96,1920]{2,1,0:T(8,128)(2,1)S(1)} collective-permute-done((bf16[1,96,1920]{2,1,0:T(8,128)(2,1)}, bf16[1,96,1920]{2,1,0:T(8,128)(2,1)S(1)}, u32[]{:S(2)}, u32[]{:S(2)}) %collective-permute-start.9) | collective-permute-done | bytes 368672 | tf_op jit(solution)/shard_map/ppermute | solution.py:252
  75.7 2.9 %collective-permute-start.12 = (bf16[1,48,1920]{2,1,0:T(8,128)(2,1)S(1)}, bf16[1,48,1920]{2,1,0:T(8,128)(2,1)S(1)}, u32[]{:S(2)}, u32[]{:S(2)}) collective-permute-start(bf16[1,48,1920]{2,1,0:T(8,128)(2,1)S(1)} %slice.25), channel_id=1, source_target_pairs={{0,112},{16,0},{32,16},{48,32},{64,48},{80,64},{96,80},{112,96},{1... | collective-permute-start | bytes 552968 | tf_op jit(solution)/shard_map/ppermute | solution.py:255
  78.6 8.0 %collective-permute-done.11.refs_8_ = bf16[1,48,1920]{2,1,0:T(8,128)(2,1)S(1)} collective-permute-done((bf16[1,48,1920]{2,1,0:T(8,128)(2,1)S(1)}, bf16[1,48,1920]{2,1,0:T(8,128)(2,1)S(1)}, u32[]{:S(2)}, u32[]{:S(2)}) %collective-permute-start.11) | collective-permute-done | bytes 184352 | tf_op jit(solution)/shard_map/ppermute | solution.py:252
  88.1 13.0 %collective-permute-done.15.near_ref = bf16[3,768,384]{2,1,0:T(8,128)(2,1)S(1)} collective-permute-done((bf16[3,768,384]{2,1,0:T(8,128)(2,1)S(1)}, bf16[3,768,384]{2,1,0:T(8,128)(2,1)S(1)}, u32[]{:S(2)}, u32[]{:S(2)}) %collective-permute-start.15) | collective-permute-done | bytes 1769504 | tf_op jit(solution)/shard_map/ppermute | solution.py:117
  101.1 1.1 collective-permute-start.18
  102.3 1.1 pad_maximum_fusion.1
  105.6 1.2 copy-done.13
  106.8 2.8 %collective-permute-start.19 = (bf16[3,96,1920]{2,1,0:T(8,128)(2,1)}, bf16[3,96,1920]{2,1,0:T(8,128)(2,1)}, u32[]{:S(2)}, u32[]{:S(2)}) collective-permute-start(bf16[3,96,1920]{2,1,0:T(8,128)(2,1)} %pad_maximum_fusion.1), channel_id=1, source_target_pairs={{0,128},{128,0},{1,129},{129,1},{2,130},{130,2},{3,131},{131,3},{4... | collective-permute-start | bytes 3317768 | tf_op jit(solution)/shard_map/ppermute | solution.py:117
  110.8 2.5 %collective-permute-start.14 = (bf16[1,96,1920]{2,1,0:T(8,128)(2,1)}, bf16[1,96,1920]{2,1,0:T(8,128)(2,1)}, u32[]{:S(2)}, u32[]{:S(2)}) collective-permute-start(bf16[1,96,1920]{2,1,0:T(8,128)(2,1)} %get-tuple-element.31), channel_id=1, source_target_pairs={{0,112},{16,0},{32,16},{48,32},{64,48},{80,64},{96,80},{112,96},{1... | collective-permute-start | bytes 1105928 | tf_op jit(solution)/shard_map/ppermute | solution.py:255
  113.4 1.1 copy-done.4
  114.5 1.1 copy-done.16
  117.7 4.3 %shard_map.83.x_ref = bf16[512,3072]{1,0:T(8,128)(2,1)S(1)} custom-call(s32[1]{0:T(128)} %bitcast.13.x_ref, f32[1,3072]{1,0:T(1,128)S(1)} %bitcast.73, bf16[2,512,384]{2,1,0:T(8,128)(2,1)S(1)} %copy-done.4, bf16[2,512,384]{2,1,0:T(8,128)(2,1)S(1)} %copy-done.16, bf16[2,512,384]{2,1,0:T(8,128)(2,1)} %collective-permute-done.7.left_ref, ...), custom_call_target="tpu_custom_call" | custom-call | tf_op jit(solution)/shard_map/pallas_call | solution.py:58
  122.1 8.2 %collective-permute-done.13.refs_10_ = bf16[1,96,1920]{2,1,0:T(8,128)(2,1)} collective-permute-done((bf16[1,96,1920]{2,1,0:T(8,128)(2,1)}, bf16[1,96,1920]{2,1,0:T(8,128)(2,1)}, u32[]{:S(2)}, u32[]{:S(2)}) %collective-permute-start.13) | collective-permute-done | bytes 368672 | tf_op jit(solution)/shard_map/ppermute | solution.py:252
  130.3 1.5 copy-done.14
  131.8 7.3 %shard_map.84.attended_ref = bf16[512,384]{1,0:T(8,128)(2,1)} custom-call(s32[3]{0:T(128)S(1)} %pad_add_fusion.1.starts_ref, bf16[512,3072]{1,0:T(8,128)(2,1)S(1)} %shard_map.83.x_ref, bf16[3,1536,384]{2,1,0:T(8,128)(2,1)S(1)} %copy-done.2, bf16[3,768,384]{2,1,0:T(8,128)(2,1)S(1)} %copy-done.12, bf16[3,768,384]{2,1,0:T(8,128)(2,1)S(1)} %copy-done.14, ...), custom_call_target="tpu_custom_call" | custom-call | tf_op jit(solution)/shard_map/pallas_call | solution.py:179
  139.1 2.2 %shard_map.82.weights_ref = bf16[1536,1920]{1,0:T(8,128)(2,1)S(1)} custom-call(bf16[1,96,1920]{2,1,0:T(8,128)(2,1)S(1)} %maximum_bitcast_fusion.refs_0_, bf16[1,96,1920]{2,1,0:T(8,128)(2,1)S(1)} %copy-done.18, bf16[1,96,1920]{2,1,0:T(8,128)(2,1)} %collective-permute-done.3.refs_2_, bf16[1,96,1920]{2,1,0:T(8,128)(2,1)} %collective-permute-done.4.refs_3_, ...), custom_call_target="tpu_custom_call" | custom-call | tf_op jit(solution)/shard_map/pallas_call | solution.py:202
  141.4 2.5 %copy-done = bf16[1536,1920]{1,0:T(8,128)(2,1)} copy-done((bf16[1536,1920]{1,0:T(8,128)(2,1)}, bf16[1536,1920]{1,0:T(8,128)(2,1)S(1)}, u32[]{:S(2)}) %copy-start) | copy-done | bytes 5898264
  143.8 8.5 %shard_map.85.activated_ref = bf16[512,1536]{1,0:T(8,128)(2,1)} custom-call(bf16[512,3072]{1,0:T(8,128)(2,1)S(1)} %shard_map.83.x_ref, bf16[3072,1536]{1,0:T(8,128)(2,1)} %bitcast.74), custom_call_target="tpu_custom_call" | custom-call | tf_op jit(solution)/shard_map/pallas_call | solution.py:129
  152.3 1.5 collective-permute-start.24
  153.9 2.7 %copy-done.1 = bf16[1536,1920]{1,0:T(8,128)(2,1)S(1)} copy-done((bf16[1536,1920]{1,0:T(8,128)(2,1)S(1)}, bf16[1536,1920]{1,0:T(8,128)(2,1)}, u32[]{:S(2)}) %copy-start.1) | copy-done | bytes 5898264
  156.5 5.0 %shard_map.86 = bf16[16,96,512]{2,1,0:T(8,128)(2,1)S(1)} custom-call(s32[2]{0:T(128)S(1)} %pad_add_fusion.at_ref, bf16[1536,1920]{1,0:T(8,128)(2,1)S(1)} %copy-done.1, bf16[512,384]{1,0:T(8,128)(2,1)} %shard_map.84.attended_ref, bf16[512,1536]{1,0:T(8,128)(2,1)} %shard_map.85.activated_ref), custom_call_target="tpu_custom_call" | custom-call | tf_op jit(solution)/shard_map/pallas_call | solution.py:237
  161.6 4.0 %shard_map.87 = bf16[16,96,512]{2,1,0:T(8,128)(2,1)S(1)} custom-call(s32[2]{0:T(128)S(1)} %pad_add_fusion.at_ref, bf16[1536,1920]{1,0:T(8,128)(2,1)S(1)} %copy-done.1, bf16[512,384]{1,0:T(8,128)(2,1)S(1)} %collective-permute-done.23.attended_ref, bf16[512,1536]{1,0:T(8,128)(2,1)S(1)} %collective-permute-done.24.activated_ref), custom_call_target="tpu_custom_call" | custom-call | tf_op jit(solution)/shard_map/pallas_call | solution.py:237
  166.6 3.0 %collective-permute-start.20 = (bf16[2,192,512]{2,1,0:T(8,128)(2,1)S(1)}, bf16[2,192,512]{2,1,0:T(8,128)(2,1)S(1)}, u32[]{:S(2)}, u32[]{:S(2)}) collective-permute-start(bf16[2,192,512]{2,1,0:T(8,128)(2,1)S(1)} %get-tuple-element.53), channel_id=1, source_target_pairs={{0,2},{1,3},{2,0},{3,1},{4,6},{5,7},{6,4},{7,5},{8,10},{9,11},{10,... | collective-permute-start | bytes 1179656 | tf_op jit(solution)/shard_map/ppermute | solution.py:88
  169.9 2.4 %collective-permute-start.22 = (bf16[2,192,512]{2,1,0:T(8,128)(2,1)S(1)}, bf16[2,192,512]{2,1,0:T(8,128)(2,1)S(1)}, u32[]{:S(2)}, u32[]{:S(2)}) collective-permute-start(bf16[2,192,512]{2,1,0:T(8,128)(2,1)S(1)} %get-tuple-element.51), channel_id=1, source_target_pairs={{0,3},{1,0},{2,1},{3,2},{4,7},{5,4},{6,5},{7,6},{8,11},{9,8},{10,9... | collective-permute-start | bytes 1179656 | tf_op jit(solution)/shard_map/ppermute | solution.py:88
  172.3 13.6 %collective-permute-done.27 = bf16[4,192,512]{2,1,0:T(8,128)(2,1)} collective-permute-done((bf16[4,192,512]{2,1,0:T(8,128)(2,1)S(1)}, bf16[4,192,512]{2,1,0:T(8,128)(2,1)}, u32[]{:S(2)}, u32[]{:S(2)}) %collective-permute-start.27) | collective-permute-done | bytes 786464 | tf_op jit(solution)/shard_map/ppermute | solution.py:98
  185.9 1.6 convert_add_fusion
  188.4 2.8 %collective-permute-start.28 = (bf16[192,512]{1,0:T(8,128)(2,1)}, bf16[192,512]{1,0:T(8,128)(2,1)}, u32[]{:S(2)}, u32[]{:S(2)}) collective-permute-start(bf16[192,512]{1,0:T(8,128)(2,1)} %get-tuple-element.56), channel_id=1, source_target_pairs={{0,2},{1,3},{2,0},{3,1},{4,6},{5,7},{6,4},{7,5},{8,10},{9,11},{10,... | collective-permute-start | bytes 589832 | tf_op jit(solution)/shard_map/ppermute | solution.py:88
  191.5 2.4 %collective-permute-start.30 = (bf16[192,512]{1,0:T(8,128)(2,1)}, bf16[192,512]{1,0:T(8,128)(2,1)}, u32[]{:S(2)}, u32[]{:S(2)}) collective-permute-start(bf16[192,512]{1,0:T(8,128)(2,1)} %get-tuple-element.57), channel_id=1, source_target_pairs={{0,3},{1,0},{2,1},{3,2},{4,7},{5,4},{6,5},{7,6},{8,11},{9,8},{10,9... | collective-permute-start | bytes 589832 | tf_op jit(solution)/shard_map/ppermute | solution.py:88
  193.9 1.1 fusion.2
  196.8 4.5 %collective-permute-done.29 = bf16[192,512]{1,0:T(8,128)(2,1)} collective-permute-done((bf16[192,512]{1,0:T(8,128)(2,1)}, bf16[192,512]{1,0:T(8,128)(2,1)}, u32[]{:S(2)}, u32[]{:S(2)}) %collective-permute-start.29) | collective-permute-done | bytes 196640 | tf_op jit(solution)/shard_map/ppermute | solution.py:88
  201.8 1.4 fusion.6
  (115 shorter events, 17.6 us)
Async XLA Ops:
  6.5 51.4 %all-gather.3.cloned.1.call-start = ((), (), s32[]{:S(2)}) async-start(), calls=%async_computation | async-start | bytes 3760128 | tf_op jit(solution)/shard_map/all_gather | solution.py:257
  7.3 136.6 %all-gather.5.cloned.1.call-start = ((), (), s32[]{:S(2)}) async-start(), calls=%async_computation.1 | async-start | bytes 10027008 | tf_op jit(solution)/shard_map/all_gather | solution.py:266
  7.3 19.9 %collective-permute-start = (bf16[512,384]{1,0:T(8,128)(2,1)}, bf16[512,384]{1,0:T(8,128)(2,1)S(1)}, u32[]{:S(2)}, u32[]{:S(2)}) collective-permute-start(bf16[512,384]{1,0:T(8,128)(2,1)} %param.8), channel_id=1, source_target_pairs={{0,4},{4,0},{1,5},{5,1},{2,6},{6,2},{3,7},{7,3},{8,12},{12,8},{9,1... | collective-permute-start | bytes 1179656 | tf_op jit(solution)/shard_map/ppermute | solution.py:263
  10.5 16.7 %collective-permute-start.2 = (bf16[1,96,1920]{2,1,0:T(8,128)(2,1)S(1)}, bf16[1,96,1920]{2,1,0:T(8,128)(2,1)S(1)}, u32[]{:S(2)}, u32[]{:S(2)}) collective-permute-start(bf16[1,96,1920]{2,1,0:T(8,128)(2,1)S(1)} %maximum_bitcast_fusion.refs_0_), channel_id=1, source_target_pairs={{0,16},{16,32},{32,48},{48,64},{64,80},{80,96},{96,112},{112,0},{1... | collective-permute-start | bytes 1105928 | tf_op jit(solution)/shard_map/ppermute | solution.py:252
  12.2 15.0 %collective-permute-start.3 = (bf16[1,96,1920]{2,1,0:T(8,128)(2,1)S(1)}, bf16[1,96,1920]{2,1,0:T(8,128)(2,1)}, u32[]{:S(2)}, u32[]{:S(2)}) collective-permute-start(bf16[1,96,1920]{2,1,0:T(8,128)(2,1)S(1)} %maximum_bitcast_fusion.refs_0_), channel_id=1, source_target_pairs={{0,112},{16,0},{32,16},{48,32},{64,48},{80,64},{96,80},{112,96},{1... | collective-permute-start | bytes 1105928 | tf_op jit(solution)/shard_map/ppermute | solution.py:255
  16.3 10.9 %collective-permute-start.1 = (bf16[96,1536]{1,0:T(8,128)(2,1)}, bf16[96,1536]{1,0:T(8,128)(2,1)S(1)}, u32[]{:S(2)}, u32[]{:S(2)}) collective-permute-start(bf16[96,1536]{1,0:T(8,128)(2,1)} %param.11), channel_id=1, source_target_pairs={{0,128},{128,0},{1,129},{129,1},{2,130},{130,2},{3,131},{131,3},{4... | collective-permute-start | bytes 884744 | tf_op jit(solution)/shard_map/ppermute | solution.py:117
  31.5 28.1 %collective-permute-start.8 = (bf16[3,96,1920]{2,1,0:T(8,128)(2,1)}, bf16[3,96,1920]{2,1,0:T(8,128)(2,1)S(1)}, u32[]{:S(2)}, u32[]{:S(2)}) collective-permute-start(bf16[3,96,1920]{2,1,0:T(8,128)(2,1)} %pad_maximum_fusion), channel_id=1, source_target_pairs={{0,128},{128,0},{1,129},{129,1},{2,130},{130,2},{3,131},{131,3},{4... | collective-permute-start | bytes 3317768 | tf_op jit(solution)/shard_map/ppermute | solution.py:117
  32.4 27.2 %copy-start.3 = (bf16[2,512,384]{2,1,0:T(8,128)(2,1)}, bf16[2,512,384]{2,1,0:T(8,128)(2,1)S(1)}, u32[]{:S(2)}) copy-start(bf16[2,512,384]{2,1,0:T(8,128)(2,1)S(1)} %pad_maximum_fusion.2.pair_ref) | copy-start | bytes 2359300
  32.4 27.2 %collective-permute-start.6 = (bf16[2,512,384]{2,1,0:T(8,128)(2,1)S(1)}, bf16[2,512,384]{2,1,0:T(8,128)(2,1)S(1)}, u32[]{:S(2)}, u32[]{:S(2)}) collective-permute-start(bf16[2,512,384]{2,1,0:T(8,128)(2,1)S(1)} %pad_maximum_fusion.2.pair_ref), channel_id=1, source_target_pairs={{0,1},{1,2},{2,3},{3,0},{4,5},{5,6},{6,7},{7,4},{8,9},{9,10},{10,1... | collective-permute-start | bytes 2359304 | tf_op jit(solution)/shard_map/ppermute | solution.py:252
  33.7 25.9 %collective-permute-start.7 = (bf16[2,512,384]{2,1,0:T(8,128)(2,1)S(1)}, bf16[2,512,384]{2,1,0:T(8,128)(2,1)}, u32[]{:S(2)}, u32[]{:S(2)}) collective-permute-start(bf16[2,512,384]{2,1,0:T(8,128)(2,1)S(1)} %pad_maximum_fusion.2.pair_ref), channel_id=1, source_target_pairs={{0,3},{1,0},{2,1},{3,2},{4,7},{5,4},{6,5},{7,6},{8,11},{9,8},{10,9... | collective-permute-start | bytes 2359304 | tf_op jit(solution)/shard_map/ppermute | solution.py:255
  35.2 19.5 %collective-permute-start.4 = (bf16[1,96,1920]{2,1,0:T(8,128)(2,1)S(1)}, bf16[1,96,1920]{2,1,0:T(8,128)(2,1)}, u32[]{:S(2)}, u32[]{:S(2)}) collective-permute-start(bf16[1,96,1920]{2,1,0:T(8,128)(2,1)S(1)} %collective-permute-done.2.refs_1_), channel_id=1, source_target_pairs={{0,16},{16,32},{32,48},{48,64},{64,80},{80,96},{96,112},{112,0},{1... | collective-permute-start | bytes 1105928 | tf_op jit(solution)/shard_map/ppermute | solution.py:252
  36.5 18.2 %collective-permute-start.5 = (bf16[1,96,1920]{2,1,0:T(8,128)(2,1)}, bf16[1,96,1920]{2,1,0:T(8,128)(2,1)}, u32[]{:S(2)}, u32[]{:S(2)}) collective-permute-start(bf16[1,96,1920]{2,1,0:T(8,128)(2,1)} %collective-permute-done.3.refs_2_), channel_id=1, source_target_pairs={{0,112},{16,0},{32,16},{48,32},{64,48},{80,64},{96,80},{112,96},{1... | collective-permute-start | bytes 1105928 | tf_op jit(solution)/shard_map/ppermute | solution.py:255
  59.6 53.8 %copy-start.15 = (bf16[2,512,384]{2,1,0:T(8,128)(2,1)}, bf16[2,512,384]{2,1,0:T(8,128)(2,1)S(1)}, u32[]{:S(2)}) copy-start(bf16[2,512,384]{2,1,0:T(8,128)(2,1)S(1)} %collective-permute-done.6.right_ref) | copy-start | bytes 2359300
  59.6 50.0 %copy-start.5 = (bf16[3,96,1920]{2,1,0:T(8,128)(2,1)}, bf16[3,96,1920]{2,1,0:T(8,128)(2,1)S(1)}, u32[]{:S(2)}) copy-start(bf16[3,96,1920]{2,1,0:T(8,128)(2,1)S(1)} %collective-permute-done.8.refs_5_) | copy-start | bytes 3317764
  59.6 41.5 %collective-permute-start.15 = (bf16[3,768,384]{2,1,0:T(8,128)(2,1)S(1)}, bf16[3,768,384]{2,1,0:T(8,128)(2,1)S(1)}, u32[]{:S(2)}, u32[]{:S(2)}) collective-permute-start(bf16[3,768,384]{2,1,0:T(8,128)(2,1)S(1)} %constant_dynamic-slice_fusion), channel_id=1, source_target_pairs={{0,128},{128,0},{1,129},{129,1},{2,130},{130,2},{3,131},{131,3},{4... | collective-permute-start | bytes 5308424 | tf_op jit(solution)/shard_map/ppermute | solution.py:117
  62.5 13.2 %collective-permute-start.10 = (bf16[1,96,1920]{2,1,0:T(8,128)(2,1)}, bf16[1,96,1920]{2,1,0:T(8,128)(2,1)S(1)}, u32[]{:S(2)}, u32[]{:S(2)}) collective-permute-start(bf16[1,96,1920]{2,1,0:T(8,128)(2,1)} %collective-permute-done.5.refs_4_), channel_id=1, source_target_pairs={{0,112},{16,0},{32,16},{48,32},{64,48},{80,64},{96,80},{112,96},{1... | collective-permute-start | bytes 1105928 | tf_op jit(solution)/shard_map/ppermute | solution.py:255
  64.7 10.8 %collective-permute-start.9 = (bf16[1,96,1920]{2,1,0:T(8,128)(2,1)}, bf16[1,96,1920]{2,1,0:T(8,128)(2,1)S(1)}, u32[]{:S(2)}, u32[]{:S(2)}) collective-permute-start(bf16[1,96,1920]{2,1,0:T(8,128)(2,1)} %collective-permute-done.4.refs_3_), channel_id=1, source_target_pairs={{0,16},{16,32},{32,48},{48,64},{64,80},{80,96},{96,112},{112,0},{1... | collective-permute-start | bytes 1105928 | tf_op jit(solution)/shard_map/ppermute | solution.py:252
  64.8 21.8 %collective-permute-start.16 = (bf16[512,384]{1,0:T(8,128)(2,1)S(1)}, bf16[512,384]{1,0:T(8,128)(2,1)S(1)}, u32[]{:S(2)}, u32[]{:S(2)}) collective-permute-start(bf16[512,384]{1,0:T(8,128)(2,1)S(1)} %slice_bitcast_fusion.1), channel_id=1, source_target_pairs={{0,1},{1,2},{2,3},{3,0},{4,5},{5,6},{6,7},{7,4},{8,9},{9,10},{10,1... | collective-permute-start | bytes 1179656 | tf_op jit(solution)/shard_map/ppermute | solution.py:252
  66.6 20.8 %collective-permute-start.17 = (bf16[512,384]{1,0:T(8,128)(2,1)S(1)}, bf16[512,384]{1,0:T(8,128)(2,1)S(1)}, u32[]{:S(2)}, u32[]{:S(2)}) collective-permute-start(bf16[512,384]{1,0:T(8,128)(2,1)S(1)} %slice_bitcast_fusion), channel_id=1, source_target_pairs={{0,3},{1,0},{2,1},{3,2},{4,7},{5,4},{6,5},{7,6},{8,11},{9,8},{10,9... | collective-permute-start | bytes 1179656 | tf_op jit(solution)/shard_map/ppermute | solution.py:255
  75.6 35.0 %copy-start.9 = (bf16[1,96,1920]{2,1,0:T(8,128)(2,1)}, bf16[1,96,1920]{2,1,0:T(8,128)(2,1)S(1)}, u32[]{:S(2)}) copy-start(bf16[1,96,1920]{2,1,0:T(8,128)(2,1)S(1)} %collective-permute-done.9.refs_6_) | copy-start | bytes 1105924
  75.6 11.1 %collective-permute-start.11 = (bf16[1,48,1920]{2,1,0:T(8,128)(2,1)S(1)}, bf16[1,48,1920]{2,1,0:T(8,128)(2,1)S(1)}, u32[]{:S(2)}, u32[]{:S(2)}) collective-permute-start(bf16[1,48,1920]{2,1,0:T(8,128)(2,1)S(1)} %slice.24), channel_id=1, source_target_pairs={{0,16},{16,32},{32,48},{48,64},{64,80},{80,96},{96,112},{112,0},{1... | collective-permute-start | bytes 552968 | tf_op jit(solution)/shard_map/ppermute | solution.py:252
  75.7 34.9 %copy-start.7 = (bf16[1,96,1920]{2,1,0:T(8,128)(2,1)}, bf16[1,96,1920]{2,1,0:T(8,128)(2,1)S(1)}, u32[]{:S(2)}) copy-start(bf16[1,96,1920]{2,1,0:T(8,128)(2,1)S(1)} %collective-permute-done.10.refs_7_) | copy-start | bytes 1105924
  75.7 37.7 %copy-start.27 = (f32[3072]{0:T(1024)S(1)}, f32[3072]{0:T(1024)}, u32[]{:S(2)}) copy-start(f32[3072]{0:T(1024)} %param.9) | copy-start | bytes 36868
  75.7 10.9 %collective-permute-start.12 = (bf16[1,48,1920]{2,1,0:T(8,128)(2,1)S(1)}, bf16[1,48,1920]{2,1,0:T(8,128)(2,1)S(1)}, u32[]{:S(2)}, u32[]{:S(2)}) collective-permute-start(bf16[1,48,1920]{2,1,0:T(8,128)(2,1)S(1)} %slice.25), channel_id=1, source_target_pairs={{0,112},{16,0},{32,16},{48,32},{64,48},{80,64},{96,80},{112,96},{1... | collective-permute-start | bytes 552968 | tf_op jit(solution)/shard_map/ppermute | solution.py:255
  101.1 4.5 %collective-permute-start.18 = (bf16[3,768,384]{2,1,0:T(8,128)(2,1)S(1)}, bf16[3,768,384]{2,1,0:T(8,128)(2,1)S(1)}, u32[]{:S(2)}, u32[]{:S(2)}) collective-permute-start(bf16[3,768,384]{2,1,0:T(8,128)(2,1)S(1)} %collective-permute-done.15.near_ref), channel_id=1, source_target_pairs={{0,8},{8,0},{1,9},{9,1},{2,10},{10,2},{3,11},{11,3},{4,12},{12,4},... | collective-permute-start | bytes 5308424 | tf_op jit(solution)/shard_map/ppermute | solution.py:292
  106.8 32.3 %collective-permute-start.19 = (bf16[3,96,1920]{2,1,0:T(8,128)(2,1)}, bf16[3,96,1920]{2,1,0:T(8,128)(2,1)}, u32[]{:S(2)}, u32[]{:S(2)}) collective-permute-start(bf16[3,96,1920]{2,1,0:T(8,128)(2,1)} %pad_maximum_fusion.1), channel_id=1, source_target_pairs={{0,128},{128,0},{1,129},{129,1},{2,130},{130,2},{3,131},{131,3},{4... | collective-permute-start | bytes 3317768 | tf_op jit(solution)/shard_map/ppermute | solution.py:117
  110.6 19.7 %collective-permute-start.13 = (bf16[1,96,1920]{2,1,0:T(8,128)(2,1)}, bf16[1,96,1920]{2,1,0:T(8,128)(2,1)}, u32[]{:S(2)}, u32[]{:S(2)}) collective-permute-start(bf16[1,96,1920]{2,1,0:T(8,128)(2,1)} %get-tuple-element.30), channel_id=1, source_target_pairs={{0,16},{16,32},{32,48},{48,64},{64,80},{80,96},{96,112},{112,0},{1... | collective-permute-start | bytes 1105928 | tf_op jit(solution)/shard_map/ppermute | solution.py:252
  110.8 19.5 %collective-permute-start.14 = (bf16[1,96,1920]{2,1,0:T(8,128)(2,1)}, bf16[1,96,1920]{2,1,0:T(8,128)(2,1)}, u32[]{:S(2)}, u32[]{:S(2)}) collective-permute-start(bf16[1,96,1920]{2,1,0:T(8,128)(2,1)} %get-tuple-element.31), channel_id=1, source_target_pairs={{0,112},{16,0},{32,16},{48,32},{64,48},{80,64},{96,80},{112,96},{1... | collective-permute-start | bytes 1105928 | tf_op jit(solution)/shard_map/ppermute | solution.py:255
  117.7 12.6 %copy-start.12 = (bf16[3,768,384]{2,1,0:T(8,128)(2,1)S(1)}, bf16[3,768,384]{2,1,0:T(8,128)(2,1)}, u32[]{:S(2)}) copy-start(bf16[3,768,384]{2,1,0:T(8,128)(2,1)} %copy-done.11) | copy-start | bytes 5308420
  117.7 12.6 %copy-start.28 = (f32[3,128]{1,0:T(4,128)S(1)}, f32[3,128]{1,0:T(4,128)}, u32[]{:S(2)}) copy-start(f32[3,128]{1,0:T(4,128)} %q_gain_ref.1) | copy-start | bytes 4612
  117.7 12.6 %copy-start.29 = (f32[3,128]{1,0:T(4,128)S(1)}, f32[3,128]{1,0:T(4,128)}, u32[]{:S(2)}) copy-start(f32[3,128]{1,0:T(4,128)} %k_gain_ref.1) | copy-start | bytes 4612
  117.7 21.4 %copy-start.18 = (bf16[1,96,1920]{2,1,0:T(8,128)(2,1)S(1)}, bf16[1,96,1920]{2,1,0:T(8,128)(2,1)}, u32[]{:S(2)}) copy-start(bf16[1,96,1920]{2,1,0:T(8,128)(2,1)} %copy-done.17) | copy-start | bytes 1105924
  117.7 21.4 %copy-start.20 = (bf16[1,48,1920]{2,1,0:T(8,128)(2,1)S(1)}, bf16[1,48,1920]{2,1,0:T(8,128)(2,1)}, u32[]{:S(2)}) copy-start(bf16[1,48,1920]{2,1,0:T(8,128)(2,1)} %copy-done.19) | copy-start | bytes 552964
  117.7 21.4 %copy-start.22 = (bf16[1,48,1920]{2,1,0:T(8,128)(2,1)S(1)}, bf16[1,48,1920]{2,1,0:T(8,128)(2,1)}, u32[]{:S(2)}) copy-start(bf16[1,48,1920]{2,1,0:T(8,128)(2,1)} %copy-done.21) | copy-start | bytes 552964
  122.1 17.0 %copy-start.6 = (bf16[3,96,1920]{2,1,0:T(8,128)(2,1)S(1)}, bf16[3,96,1920]{2,1,0:T(8,128)(2,1)}, u32[]{:S(2)}) copy-start(bf16[3,96,1920]{2,1,0:T(8,128)(2,1)} %copy-done.5) | copy-start | bytes 3317764
  122.1 17.0 %copy-start.8 = (bf16[1,96,1920]{2,1,0:T(8,128)(2,1)S(1)}, bf16[1,96,1920]{2,1,0:T(8,128)(2,1)}, u32[]{:S(2)}) copy-start(bf16[1,96,1920]{2,1,0:T(8,128)(2,1)} %copy-done.7) | copy-start | bytes 1105924
  122.1 17.0 %copy-start.10 = (bf16[1,96,1920]{2,1,0:T(8,128)(2,1)S(1)}, bf16[1,96,1920]{2,1,0:T(8,128)(2,1)}, u32[]{:S(2)}) copy-start(bf16[1,96,1920]{2,1,0:T(8,128)(2,1)} %copy-done.9) | copy-start | bytes 1105924
  152.3 9.2 %collective-permute-start.24 = (bf16[512,1536]{1,0:T(8,128)(2,1)}, bf16[512,1536]{1,0:T(8,128)(2,1)S(1)}, u32[]{:S(2)}, u32[]{:S(2)}) collective-permute-start(bf16[512,1536]{1,0:T(8,128)(2,1)} %shard_map.85.activated_ref), channel_id=1, source_target_pairs={{0,8},{8,0},{1,9},{9,1},{2,10},{10,2},{3,11},{11,3},{4,12},{12,4},... | collective-permute-start | bytes 4718600 | tf_op jit(solution)/shard_map/ppermute | solution.py:307
  153.8 7.7 %collective-permute-start.23 = (bf16[512,384]{1,0:T(8,128)(2,1)}, bf16[512,384]{1,0:T(8,128)(2,1)S(1)}, u32[]{:S(2)}, u32[]{:S(2)}) collective-permute-start(bf16[512,384]{1,0:T(8,128)(2,1)} %shard_map.84.attended_ref), channel_id=1, source_target_pairs={{0,8},{8,0},{1,9},{9,1},{2,10},{10,2},{3,11},{11,3},{4,12},{12,4},... | collective-permute-start | bytes 1179656 | tf_op jit(solution)/shard_map/ppermute | solution.py:307
  165.7 6.6 %collective-permute-start.25 = (bf16[4,192,512]{2,1,0:T(8,128)(2,1)S(1)}, bf16[4,192,512]{2,1,0:T(8,128)(2,1)}, u32[]{:S(2)}, u32[]{:S(2)}) collective-permute-start(bf16[4,192,512]{2,1,0:T(8,128)(2,1)S(1)} %get-tuple-element.50), channel_id=1, source_target_pairs={{0,8},{8,0},{1,9},{9,1},{2,10},{10,2},{3,11},{11,3},{4,12},{12,4},... | collective-permute-start | bytes 2359304 | tf_op jit(solution)/shard_map/ppermute | solution.py:99
  166.3 19.5 %collective-permute-start.27 = (bf16[4,192,512]{2,1,0:T(8,128)(2,1)S(1)}, bf16[4,192,512]{2,1,0:T(8,128)(2,1)}, u32[]{:S(2)}, u32[]{:S(2)}) collective-permute-start(bf16[4,192,512]{2,1,0:T(8,128)(2,1)S(1)} %get-tuple-element.49), channel_id=1, source_target_pairs={{0,12},{4,8},{8,4},{12,0},{1,13},{5,9},{9,5},{13,1},{2,14},{6,10},... | collective-permute-start | bytes 2359304 | tf_op jit(solution)/shard_map/ppermute | solution.py:98
  166.6 24.8 %collective-permute-start.20 = (bf16[2,192,512]{2,1,0:T(8,128)(2,1)S(1)}, bf16[2,192,512]{2,1,0:T(8,128)(2,1)S(1)}, u32[]{:S(2)}, u32[]{:S(2)}) collective-permute-start(bf16[2,192,512]{2,1,0:T(8,128)(2,1)S(1)} %get-tuple-element.53), channel_id=1, source_target_pairs={{0,2},{1,3},{2,0},{3,1},{4,6},{5,7},{6,4},{7,5},{8,10},{9,11},{10,... | collective-permute-start | bytes 1179656 | tf_op jit(solution)/shard_map/ppermute | solution.py:88
  169.6 24.3 %collective-permute-start.21 = (bf16[2,192,512]{2,1,0:T(8,128)(2,1)S(1)}, bf16[2,192,512]{2,1,0:T(8,128)(2,1)S(1)}, u32[]{:S(2)}, u32[]{:S(2)}) collective-permute-start(bf16[2,192,512]{2,1,0:T(8,128)(2,1)S(1)} %get-tuple-element.52), channel_id=1, source_target_pairs={{0,1},{1,2},{2,3},{3,0},{4,5},{5,6},{6,7},{7,4},{8,9},{9,10},{10,1... | collective-permute-start | bytes 1179656 | tf_op jit(solution)/shard_map/ppermute | solution.py:88
  169.9 24.0 %collective-permute-start.22 = (bf16[2,192,512]{2,1,0:T(8,128)(2,1)S(1)}, bf16[2,192,512]{2,1,0:T(8,128)(2,1)S(1)}, u32[]{:S(2)}, u32[]{:S(2)}) collective-permute-start(bf16[2,192,512]{2,1,0:T(8,128)(2,1)S(1)} %get-tuple-element.51), channel_id=1, source_target_pairs={{0,3},{1,0},{2,1},{3,2},{4,7},{5,4},{6,5},{7,6},{8,11},{9,8},{10,9... | collective-permute-start | bytes 1179656 | tf_op jit(solution)/shard_map/ppermute | solution.py:88
  188.4 8.4 %collective-permute-start.28 = (bf16[192,512]{1,0:T(8,128)(2,1)}, bf16[192,512]{1,0:T(8,128)(2,1)}, u32[]{:S(2)}, u32[]{:S(2)}) collective-permute-start(bf16[192,512]{1,0:T(8,128)(2,1)} %get-tuple-element.56), channel_id=1, source_target_pairs={{0,2},{1,3},{2,0},{3,1},{4,6},{5,7},{6,4},{7,5},{8,10},{9,11},{10,... | collective-permute-start | bytes 589832 | tf_op jit(solution)/shard_map/ppermute | solution.py:88
  191.2 10.1 %collective-permute-start.29 = (bf16[192,512]{1,0:T(8,128)(2,1)}, bf16[192,512]{1,0:T(8,128)(2,1)}, u32[]{:S(2)}, u32[]{:S(2)}) collective-permute-start(bf16[192,512]{1,0:T(8,128)(2,1)} %get-tuple-element.58), channel_id=1, source_target_pairs={{0,1},{1,2},{2,3},{3,0},{4,5},{5,6},{6,7},{7,4},{8,9},{9,10},{10,1... | collective-permute-start | bytes 589832 | tf_op jit(solution)/shard_map/ppermute | solution.py:88
  191.5 9.8 %collective-permute-start.30 = (bf16[192,512]{1,0:T(8,128)(2,1)}, bf16[192,512]{1,0:T(8,128)(2,1)}, u32[]{:S(2)}, u32[]{:S(2)}) collective-permute-start(bf16[192,512]{1,0:T(8,128)(2,1)} %get-tuple-element.57), channel_id=1, source_target_pairs={{0,3},{1,0},{2,1},{3,2},{4,7},{5,4},{6,5},{7,6},{8,11},{9,8},{10,9... | collective-permute-start | bytes 589832 | tf_op jit(solution)/shard_map/ppermute | solution.py:88
  196.0 5.7 %collective-permute-start.26 = (bf16[192,512]{1,0:T(8,128)(2,1)S(1)}, bf16[192,512]{1,0:T(8,128)(2,1)S(1)}, u32[]{:S(2)}, u32[]{:S(2)}) collective-permute-start(bf16[192,512]{1,0:T(8,128)(2,1)S(1)} %fusion.7), channel_id=1, source_target_pairs={{0,4},{4,0},{1,5},{5,1},{2,6},{6,2},{3,7},{7,3},{8,12},{12,8},{9,1... | collective-permute-start | bytes 589832 | tf_op jit(solution)/shard_map/ppermute | solution.py:111
  (17 other events, 55.9 us)
Sparse Core Ops, SparseCore 0:
  9.2 48.6 all-gather.2
  59.8 74.9 all-gather.4

commit v2 on v1

--- a/solution.py
+++ b/solution.py
@@ -107,9 +107,11 @@
     def total(values):
         return sum(v.astype(jnp.float32) for v in values)
 
-    by_y, by_x = total(over_x), total(over_y)
+    by_x = total(over_y)
+    rounded = by_x.astype(jnp.bfloat16)
+    others = to_peers_x(rounded, 0)
+    by_y = total(tie(over_x, rounded))
     other = lax.ppermute(pick(by_y, 1 - yl, 0).astype(jnp.bfloat16), "yl", SWAP)
-    others = to_peers_x(by_x.astype(jnp.bfloat16), 0)
     return total([pick(by_y, yl, 0), other]), total([pick(by_x, x, 0)] + others)
 
 
@@ -296,10 +298,12 @@
     base = (1 - yh) * 2 * quarter
     starts = jnp.stack([yh * 2 * quarter, base + c * quarter, base + (1 - c) * quarter])
     distant = jnp.concatenate([low, jnp.concatenate([end_a, end_b], axis=1), high])
-    normed = tie(normed, (distant, other_low, other_high))
-    distant = across(tie(distant, other_d))
+    normed = tie(normed, distant)
+    distant, other_d = lax.optimization_barrier((distant, other_d))
+    distant = across(distant)
     shards += [([(1, -3, 0), (1, 4, 0), (1, 3, 0)], distant)]
     attended = attention(starts, normed, own_qkv, other_c, other_d, q_gain, k_gain)
+    shards = [(places, tie(arrays, attended)) for places, arrays in shards[-3:]] + shards[:-3]
     weights, slots = side_by_side(piece, shards)
     activated = up_gelu(tie(normed, (attended, weights)), up_all)
 

time: 212 us -> 211 us (level)
    ppermute x7, waiting for transfers between devices: 37.2 us -> 17.6 us  [up(): return lax.ppermute(v, axis, shift(size, 1))]
    ppermute x6, waiting for transfers between devices: 4.66 us -> 22 us  [to_peers_x(): lax.ppermute(pick(blocks, (x + k) % 4, axis), 'x', shift(4, k))]
    ppermute x1, waiting for transfers between devices: 13.6 us -> 0.01 us  [scatter_start(): over_y = lax.ppermute(pick(theirs, 1 - yl, 0), ('c', 'yl'), both)]
    ppermute x7, waiting for transfers between devices: 0.02 us -> 12.2 us  [down(): return lax.ppermute(v, axis, shift(size, -1))]
  transfers between devices with their start and end apart: 33 -> 33, of which waited for: 12 -> 15; matrix products, arithmetic and copies ran while one was open for 7% -> 5% of each run, Pallas kernels for 9% -> 9%
where the time goes in v2:
time: 211 us; the launch traced here: 209 us
  waiting for transfers between devices  81.3 us (39%)
  starting transfers between devices  50.9 us (24%)
  Pallas kernels  31.1 us (15%)
  local copies, waits for them, and re-layouts  21.6 us (10%)
  between operations  13.8 us (7%)
  other arithmetic  10.1 us (5%)
    ppermute x4, waiting for transfers between devices, across(): return lax.ppermute(v, 'yh', SWAP)  22.9 us
    ppermute x6, waiting for transfers between devices, to_peers_x(): lax.ppermute(pick(blocks, (x + k) % 4, axis), 'x', shift(4, k))  22 us
    ppermute x7, starting transfers between devices, down(): return lax.ppermute(v, axis, shift(size, -1))  19.5 us
    ppermute x7, waiting for transfers between devices, up(): return lax.ppermute(v, axis, shift(size, 1))  17.6 us
    unnamed x65, local copies, waits for them, and re-layouts  15.2 us
    ppermute x7, waiting for transfers between devices, down(): return lax.ppermute(v, axis, shift(size, -1))  12.2 us
    ppermute x6, starting transfers between devices, to_peers_x(): lax.ppermute(pick(blocks, (x + k) % 4, axis), 'x', shift(4, k))  9.35 us
    ppermute x4, starting transfers between devices, across(): return lax.ppermute(v, 'yh', SWAP)  9.31 us
  transfers between devices with their start and end apart: 33, of which 15 were waited for; matrix products, arithmetic and copies ran while one was open for 5% of the time, Pallas kernels for 9%

profile of v2, /device:TPU:1, one launch (start us, length us, event | category | flops | bytes accessed | tf_op | source)
XLA Modules:
  0.0 208.8 jit_solution(15267264937411769860)
XLA Ops:
  7.3 2.2 %collective-permute-start = (bf16[512,384]{1,0:T(8,128)(2,1)}, bf16[512,384]{1,0:T(8,128)(2,1)S(1)}, u32[]{:S(2)}, u32[]{:S(2)}) collective-permute-start(bf16[512,384]{1,0:T(8,128)(2,1)} %param.8), channel_id=1, source_target_pairs={{0,4},{4,0},{1,5},{5,1},{2,6},{6,2},{3,7},{7,3},{8,12},{12,8},{9,1... | collective-permute-start | bytes 1179656 | tf_op jit(solution)/shard_map/ppermute | solution.py:265
  10.5 1.7 collective-permute-start.2
  12.2 4.0 %collective-permute-start.3 = (bf16[1,96,1920]{2,1,0:T(8,128)(2,1)S(1)}, bf16[1,96,1920]{2,1,0:T(8,128)(2,1)}, u32[]{:S(2)}, u32[]{:S(2)}) collective-permute-start(bf16[1,96,1920]{2,1,0:T(8,128)(2,1)S(1)} %maximum_bitcast_fusion.refs_3_), channel_id=1, source_target_pairs={{0,112},{16,0},{32,16},{48,32},{64,48},{80,64},{96,80},{112,96},{1... | collective-permute-start | bytes 1105928 | tf_op jit(solution)/shard_map/ppermute | solution.py:257
  16.3 2.6 %collective-permute-start.1 = (bf16[96,1536]{1,0:T(8,128)(2,1)}, bf16[96,1536]{1,0:T(8,128)(2,1)S(1)}, u32[]{:S(2)}, u32[]{:S(2)}) collective-permute-start(bf16[96,1536]{1,0:T(8,128)(2,1)} %param.11), channel_id=1, source_target_pairs={{0,128},{128,0},{1,129},{129,1},{2,130},{130,2},{3,131},{131,3},{4... | collective-permute-start | bytes 884744 | tf_op jit(solution)/shard_map/ppermute | solution.py:119
  18.9 8.3 %collective-permute-done.1 = bf16[96,1536]{1,0:T(8,128)(2,1)S(1)} collective-permute-done((bf16[96,1536]{1,0:T(8,128)(2,1)}, bf16[96,1536]{1,0:T(8,128)(2,1)S(1)}, u32[]{:S(2)}, u32[]{:S(2)}) %collective-permute-start.1) | collective-permute-done | bytes 294944 | tf_op jit(solution)/shard_map/ppermute | solution.py:119
  27.2 2.1 %maximum_select_fusion = bf16[2,96,1536]{2,1,0:T(8,128)(2,1)} fusion(bf16[1,96,1536]{2,1,0:T(8,128)(2,1)S(1)} %bitcast.77, bf16[1,96,1536]{2,1,0:T(8,128)(2,1)} %bitcast.76, pred[]{:T(512)S(6)} %eq.20), kind=kLoop, calls=%fused_computation.10 | loop fusion | flops 884736 | bytes 1179649 | tf_op jit(solution)/shard_map/jit(_where)/select_n | solution.py:78
  29.3 2.2 %pad_maximum_fusion = bf16[3,96,1920]{2,1,0:T(8,128)(2,1)} fusion(bf16[1,96,1920]{2,1,0:T(8,128)(2,1)} %collective-permute-done.3.refs_5_, bf16[1,96,1920]{2,1,0:T(8,128)(2,1)S(1)} %maximum_bitcast_fusion.refs_3_, bf16[1,96,1920]{2,1,0:T(8,128)(2,1)S(1)} %collective-permute-done.2.refs_4_), kind=kLoop, calls=%fused_computation.1 | loop fusion | flops 1105920 | bytes 2211840 | tf_op jit(solution)/shard_map/concatenate | solution.py:275
  32.4 1.3 collective-permute-start.4
  33.7 1.5 collective-permute-start.5
  35.2 1.3 collective-permute-start.7
  36.5 4.1 %collective-permute-start.8 = (bf16[1,96,1920]{2,1,0:T(8,128)(2,1)}, bf16[1,96,1920]{2,1,0:T(8,128)(2,1)}, u32[]{:S(2)}, u32[]{:S(2)}) collective-permute-start(bf16[1,96,1920]{2,1,0:T(8,128)(2,1)} %collective-permute-done.3.refs_5_), channel_id=1, source_target_pairs={{0,112},{16,0},{32,16},{48,32},{64,48},{80,64},{96,80},{112,96},{1... | collective-permute-start | bytes 1105928 | tf_op jit(solution)/shard_map/ppermute | solution.py:257
  40.5 14.1 %collective-permute-done.7.refs_6_ = bf16[1,96,1920]{2,1,0:T(8,128)(2,1)} collective-permute-done((bf16[1,96,1920]{2,1,0:T(8,128)(2,1)S(1)}, bf16[1,96,1920]{2,1,0:T(8,128)(2,1)}, u32[]{:S(2)}, u32[]{:S(2)}) %collective-permute-start.7) | collective-permute-done | bytes 368672 | tf_op jit(solution)/shard_map/ppermute | solution.py:254
  54.7 3.3 %all-gather.3.cloned.1.call-done.own_ref = bf16[3,1536,384]{2,1,0:T(8,128)(2,1)} async-done(((bf16[3,96,384]{2,1,0:T(8,128)(2,1)}), bf16[3,1536,384]{2,1,0:T(8,128)(2,1)}) %all-gather.3.cloned.1.call-update) | async-done | bytes 3538960 | tf_op jit(solution)/shard_map/all_gather | solution.py:259
  57.9 1.7 constant_dynamic-slice_fusion
  59.6 2.8 %collective-permute-start.16 = (bf16[3,768,384]{2,1,0:T(8,128)(2,1)S(1)}, bf16[3,768,384]{2,1,0:T(8,128)(2,1)S(1)}, u32[]{:S(2)}, u32[]{:S(2)}) collective-permute-start(bf16[3,768,384]{2,1,0:T(8,128)(2,1)S(1)} %constant_dynamic-slice_fusion), channel_id=1, source_target_pairs={{0,128},{128,0},{1,129},{129,1},{2,130},{130,2},{3,131},{131,3},{4... | collective-permute-start | bytes 5308424 | tf_op jit(solution)/shard_map/ppermute | solution.py:119
  62.8 2.4 %collective-permute-start.10 = (bf16[1,96,1920]{2,1,0:T(8,128)(2,1)}, bf16[1,96,1920]{2,1,0:T(8,128)(2,1)S(1)}, u32[]{:S(2)}, u32[]{:S(2)}) collective-permute-start(bf16[1,96,1920]{2,1,0:T(8,128)(2,1)} %collective-permute-done.8.refs_7_), channel_id=1, source_target_pairs={{0,112},{16,0},{32,16},{48,32},{64,48},{80,64},{96,80},{112,96},{1... | collective-permute-start | bytes 1105928 | tf_op jit(solution)/shard_map/ppermute | solution.py:257
  65.2 1.5 collective-permute-start.12
  67.7 1.3 collective-permute-start.13
  69.1 5.7 %collective-permute-done.10.refs_10_ = bf16[1,96,1920]{2,1,0:T(8,128)(2,1)S(1)} collective-permute-done((bf16[1,96,1920]{2,1,0:T(8,128)(2,1)}, bf16[1,96,1920]{2,1,0:T(8,128)(2,1)S(1)}, u32[]{:S(2)}, u32[]{:S(2)}) %collective-permute-start.10) | collective-permute-done | bytes 368672 | tf_op jit(solution)/shard_map/ppermute | solution.py:257
  74.8 3.5 %collective-permute-start.15 = (bf16[1,48,1920]{2,1,0:T(8,128)(2,1)S(1)}, bf16[1,48,1920]{2,1,0:T(8,128)(2,1)S(1)}, u32[]{:S(2)}, u32[]{:S(2)}) collective-permute-start(bf16[1,48,1920]{2,1,0:T(8,128)(2,1)S(1)} %slice.25), channel_id=1, source_target_pairs={{0,112},{16,0},{32,16},{48,32},{64,48},{80,64},{96,80},{112,96},{1... | collective-permute-start | bytes 552968 | tf_op jit(solution)/shard_map/ppermute | solution.py:257
  78.6 6.5 %collective-permute-done.15.refs_12_ = bf16[1,48,1920]{2,1,0:T(8,128)(2,1)S(1)} collective-permute-done((bf16[1,48,1920]{2,1,0:T(8,128)(2,1)S(1)}, bf16[1,48,1920]{2,1,0:T(8,128)(2,1)S(1)}, u32[]{:S(2)}, u32[]{:S(2)}) %collective-permute-start.15) | collective-permute-done | bytes 184352 | tf_op jit(solution)/shard_map/ppermute | solution.py:257
  85.1 3.4 %collective-permute-done.14.refs_11_ = bf16[1,48,1920]{2,1,0:T(8,128)(2,1)S(1)} collective-permute-done((bf16[1,48,1920]{2,1,0:T(8,128)(2,1)S(1)}, bf16[1,48,1920]{2,1,0:T(8,128)(2,1)S(1)}, u32[]{:S(2)}, u32[]{:S(2)}) %collective-permute-start.14) | collective-permute-done | bytes 184352 | tf_op jit(solution)/shard_map/ppermute | solution.py:254
  90.0 11.1 %collective-permute-done.16.near_ref = bf16[3,768,384]{2,1,0:T(8,128)(2,1)S(1)} collective-permute-done((bf16[3,768,384]{2,1,0:T(8,128)(2,1)S(1)}, bf16[3,768,384]{2,1,0:T(8,128)(2,1)S(1)}, u32[]{:S(2)}, u32[]{:S(2)}) %collective-permute-start.16) | collective-permute-done | bytes 1769504 | tf_op jit(solution)/shard_map/ppermute | solution.py:119
  105.6 1.2 copy-done.13
  106.8 3.2 %collective-permute-start.19 = (bf16[3,96,1920]{2,1,0:T(8,128)(2,1)}, bf16[3,96,1920]{2,1,0:T(8,128)(2,1)}, u32[]{:S(2)}, u32[]{:S(2)}) collective-permute-start(bf16[3,96,1920]{2,1,0:T(8,128)(2,1)} %pad_maximum_fusion.1), channel_id=1, source_target_pairs={{0,128},{128,0},{1,129},{129,1},{2,130},{130,2},{3,131},{131,3},{4... | collective-permute-start | bytes 3317768 | tf_op jit(solution)/shard_map/ppermute | solution.py:119
  111.0 2.7 %collective-permute-start.18 = (bf16[1,96,1920]{2,1,0:T(8,128)(2,1)}, bf16[1,96,1920]{2,1,0:T(8,128)(2,1)}, u32[]{:S(2)}, u32[]{:S(2)}) collective-permute-start(bf16[1,96,1920]{2,1,0:T(8,128)(2,1)} %get-tuple-element.46), channel_id=1, source_target_pairs={{0,112},{16,0},{32,16},{48,32},{64,48},{80,64},{96,80},{112,96},{1... | collective-permute-start | bytes 1105928 | tf_op jit(solution)/shard_map/ppermute | solution.py:257
  113.7 1.2 copy-done.4
  118.0 4.2 %shard_map.82.x_ref = bf16[512,3072]{1,0:T(8,128)(2,1)S(1)} custom-call(s32[1]{0:T(128)} %bitcast.11.x_ref, f32[1,3072]{1,0:T(1,128)S(1)} %bitcast.71, bf16[2,512,384]{2,1,0:T(8,128)(2,1)S(1)} %copy-done.4, bf16[2,512,384]{2,1,0:T(8,128)(2,1)S(1)} %copy-done.16, bf16[2,512,384]{2,1,0:T(8,128)(2,1)} %collective-permute-done.5.left_ref, ...), custom_call_target="tpu_custom_call" | custom-call | tf_op jit(solution)/shard_map/pallas_call | solution.py:58
  122.3 1.5 copy-done.14
  123.8 7.3 %shard_map.83.attended_ref = bf16[512,384]{1,0:T(8,128)(2,1)} custom-call(s32[3]{0:T(128)S(1)} %pad_add_fusion.1.starts_ref, bf16[512,3072]{1,0:T(8,128)(2,1)S(1)} %shard_map.82.x_ref, bf16[3,1536,384]{2,1,0:T(8,128)(2,1)S(1)} %copy-done.2, bf16[3,768,384]{2,1,0:T(8,128)(2,1)S(1)} %copy-done.12, bf16[3,768,384]{2,1,0:T(8,128)(2,1)S(1)} %copy-done.14, ...), custom_call_target="tpu_custom_call" | custom-call | tf_op jit(solution)/shard_map/pallas_call | solution.py:181
  131.1 3.6 %collective-permute-done.19.refs_2_ = bf16[3,96,1920]{2,1,0:T(8,128)(2,1)} collective-permute-done((bf16[3,96,1920]{2,1,0:T(8,128)(2,1)}, bf16[3,96,1920]{2,1,0:T(8,128)(2,1)}, u32[]{:S(2)}, u32[]{:S(2)}) %collective-permute-start.19) | collective-permute-done | bytes 1105952 | tf_op jit(solution)/shard_map/ppermute | solution.py:119
  134.7 2.2 %shard_map.84.weights_ref = bf16[1536,1920]{1,0:T(8,128)(2,1)S(1)} custom-call(bf16[1,96,1920]{2,1,0:T(8,128)(2,1)} %collective-permute-done.11.refs_0_, bf16[1,96,1920]{2,1,0:T(8,128)(2,1)} %collective-permute-done.18.refs_1_, bf16[3,96,1920]{2,1,0:T(8,128)(2,1)} %collective-permute-done.19.refs_2_, bf16[1,96,1920]{2,1,0:T(8,128)(2,1)S(1)} %maximum_bitcast_fusion.refs_3_, ...), custom_call_target="tpu_custom_call" | custom-call | tf_op jit(solution)/shard_map/pallas_call | solution.py:204
  136.9 2.5 %copy-done = bf16[1536,1920]{1,0:T(8,128)(2,1)} copy-done((bf16[1536,1920]{1,0:T(8,128)(2,1)}, bf16[1536,1920]{1,0:T(8,128)(2,1)S(1)}, u32[]{:S(2)}) %copy-start) | copy-done | bytes 5898264
  139.3 8.5 %shard_map.85.activated_ref = bf16[512,1536]{1,0:T(8,128)(2,1)} custom-call(bf16[512,3072]{1,0:T(8,128)(2,1)S(1)} %shard_map.82.x_ref, bf16[3072,1536]{1,0:T(8,128)(2,1)} %bitcast.72), custom_call_target="tpu_custom_call" | custom-call | tf_op jit(solution)/shard_map/pallas_call | solution.py:131
  148.9 2.7 %copy-done.1 = bf16[1536,1920]{1,0:T(8,128)(2,1)S(1)} copy-done((bf16[1536,1920]{1,0:T(8,128)(2,1)S(1)}, bf16[1536,1920]{1,0:T(8,128)(2,1)}, u32[]{:S(2)}) %copy-start.1) | copy-done | bytes 5898264
  151.6 5.0 %shard_map.86 = bf16[16,96,512]{2,1,0:T(8,128)(2,1)S(1)} custom-call(s32[2]{0:T(128)S(1)} %pad_add_fusion.at_ref, bf16[1536,1920]{1,0:T(8,128)(2,1)S(1)} %copy-done.1, bf16[512,384]{1,0:T(8,128)(2,1)} %shard_map.83.attended_ref, bf16[512,1536]{1,0:T(8,128)(2,1)} %shard_map.85.activated_ref), custom_call_target="tpu_custom_call" | custom-call | tf_op jit(solution)/shard_map/pallas_call | solution.py:239
  156.6 4.0 %shard_map.87 = bf16[16,96,512]{2,1,0:T(8,128)(2,1)S(1)} custom-call(s32[2]{0:T(128)S(1)} %pad_add_fusion.at_ref, bf16[1536,1920]{1,0:T(8,128)(2,1)S(1)} %copy-done.1, bf16[512,384]{1,0:T(8,128)(2,1)S(1)} %collective-permute-done.23.attended_ref, bf16[512,1536]{1,0:T(8,128)(2,1)S(1)} %collective-permute-done.24.activated_ref), custom_call_target="tpu_custom_call" | custom-call | tf_op jit(solution)/shard_map/pallas_call | solution.py:239
  162.4 3.1 %collective-permute-start.20 = (bf16[2,192,512]{2,1,0:T(8,128)(2,1)S(1)}, bf16[2,192,512]{2,1,0:T(8,128)(2,1)S(1)}, u32[]{:S(2)}, u32[]{:S(2)}) collective-permute-start(bf16[2,192,512]{2,1,0:T(8,128)(2,1)S(1)} %get-tuple-element.69), channel_id=1, source_target_pairs={{0,2},{1,3},{2,0},{3,1},{4,6},{5,7},{6,4},{7,5},{8,10},{9,11},{10,... | collective-permute-start | bytes 1179656 | tf_op jit(solution)/shard_map/ppermute | solution.py:88
  165.8 2.4 %collective-permute-start.22 = (bf16[2,192,512]{2,1,0:T(8,128)(2,1)S(1)}, bf16[2,192,512]{2,1,0:T(8,128)(2,1)S(1)}, u32[]{:S(2)}, u32[]{:S(2)}) collective-permute-start(bf16[2,192,512]{2,1,0:T(8,128)(2,1)S(1)} %get-tuple-element.67), channel_id=1, source_target_pairs={{0,3},{1,0},{2,1},{3,2},{4,7},{5,4},{6,5},{7,6},{8,11},{9,8},{10,9... | collective-permute-start | bytes 1179656 | tf_op jit(solution)/shard_map/ppermute | solution.py:88
  168.1 6.2 %collective-permute-done.20 = bf16[2,192,512]{2,1,0:T(8,128)(2,1)S(1)} collective-permute-done((bf16[2,192,512]{2,1,0:T(8,128)(2,1)S(1)}, bf16[2,192,512]{2,1,0:T(8,128)(2,1)S(1)}, u32[]{:S(2)}, u32[]{:S(2)}) %collective-permute-start.20) | collective-permute-done | bytes 393248 | tf_op jit(solution)/shard_map/ppermute | solution.py:88
  174.4 9.1 %collective-permute-done.21 = bf16[2,192,512]{2,1,0:T(8,128)(2,1)S(1)} collective-permute-done((bf16[2,192,512]{2,1,0:T(8,128)(2,1)S(1)}, bf16[2,192,512]{2,1,0:T(8,128)(2,1)S(1)}, u32[]{:S(2)}, u32[]{:S(2)}) %collective-permute-start.21) | collective-permute-done | bytes 393248 | tf_op jit(solution)/shard_map/ppermute | solution.py:88
  183.5 1.7 convert_add_fusion
  187.3 2.4 %collective-permute-start.30 = (bf16[192,512]{1,0:T(8,128)(2,1)}, bf16[192,512]{1,0:T(8,128)(2,1)}, u32[]{:S(2)}, u32[]{:S(2)}) collective-permute-start(bf16[192,512]{1,0:T(8,128)(2,1)} %get-tuple-element.74), channel_id=1, source_target_pairs={{0,3},{1,0},{2,1},{3,2},{4,7},{5,4},{6,5},{7,6},{8,11},{9,8},{10,9... | collective-permute-start | bytes 589832 | tf_op jit(solution)/shard_map/ppermute | solution.py:88
  189.7 1.2 collective-permute-start.28
  191.1 1.7 collective-permute-done.27
  193.5 4.0 %collective-permute-done.29 = bf16[192,512]{1,0:T(8,128)(2,1)} collective-permute-done((bf16[192,512]{1,0:T(8,128)(2,1)S(1)}, bf16[192,512]{1,0:T(8,128)(2,1)}, u32[]{:S(2)}, u32[]{:S(2)}) %collective-permute-start.29) | collective-permute-done | bytes 196640 | tf_op jit(solution)/shard_map/ppermute | solution.py:88
  197.6 1.9 collective-permute-done.28
  199.4 1.4 fusion.4
  (116 shorter events, 22.0 us)
Async XLA Ops:
  6.5 51.4 %all-gather.3.cloned.1.call-start = ((), (), s32[]{:S(2)}) async-start(), calls=%async_computation | async-start | bytes 3760128 | tf_op jit(solution)/shard_map/all_gather | solution.py:259
  7.3 132.1 %all-gather.5.cloned.1.call-start = ((), (), s32[]{:S(2)}) async-start(), calls=%async_computation.1 | async-start | bytes 10027008 | tf_op jit(solution)/shard_map/all_gather | solution.py:268
  7.3 19.9 %collective-permute-start = (bf16[512,384]{1,0:T(8,128)(2,1)}, bf16[512,384]{1,0:T(8,128)(2,1)S(1)}, u32[]{:S(2)}, u32[]{:S(2)}) collective-permute-start(bf16[512,384]{1,0:T(8,128)(2,1)} %param.8), channel_id=1, source_target_pairs={{0,4},{4,0},{1,5},{5,1},{2,6},{6,2},{3,7},{7,3},{8,12},{12,8},{9,1... | collective-permute-start | bytes 1179656 | tf_op jit(solution)/shard_map/ppermute | solution.py:265
  10.5 16.7 %collective-permute-start.2 = (bf16[1,96,1920]{2,1,0:T(8,128)(2,1)S(1)}, bf16[1,96,1920]{2,1,0:T(8,128)(2,1)S(1)}, u32[]{:S(2)}, u32[]{:S(2)}) collective-permute-start(bf16[1,96,1920]{2,1,0:T(8,128)(2,1)S(1)} %maximum_bitcast_fusion.refs_3_), channel_id=1, source_target_pairs={{0,16},{16,32},{32,48},{48,64},{64,80},{80,96},{96,112},{112,0},{1... | collective-permute-start | bytes 1105928 | tf_op jit(solution)/shard_map/ppermute | solution.py:254
  12.2 15.0 %collective-permute-start.3 = (bf16[1,96,1920]{2,1,0:T(8,128)(2,1)S(1)}, bf16[1,96,1920]{2,1,0:T(8,128)(2,1)}, u32[]{:S(2)}, u32[]{:S(2)}) collective-permute-start(bf16[1,96,1920]{2,1,0:T(8,128)(2,1)S(1)} %maximum_bitcast_fusion.refs_3_), channel_id=1, source_target_pairs={{0,112},{16,0},{32,16},{48,32},{64,48},{80,64},{96,80},{112,96},{1... | collective-permute-start | bytes 1105928 | tf_op jit(solution)/shard_map/ppermute | solution.py:257
  16.3 10.9 %collective-permute-start.1 = (bf16[96,1536]{1,0:T(8,128)(2,1)}, bf16[96,1536]{1,0:T(8,128)(2,1)S(1)}, u32[]{:S(2)}, u32[]{:S(2)}) collective-permute-start(bf16[96,1536]{1,0:T(8,128)(2,1)} %param.11), channel_id=1, source_target_pairs={{0,128},{128,0},{1,129},{129,1},{2,130},{130,2},{3,131},{131,3},{4... | collective-permute-start | bytes 884744 | tf_op jit(solution)/shard_map/ppermute | solution.py:119
  27.2 8.0 %copy-start.17 = (bf16[1,96,1920]{2,1,0:T(8,128)(2,1)}, bf16[1,96,1920]{2,1,0:T(8,128)(2,1)S(1)}, u32[]{:S(2)}) copy-start(bf16[1,96,1920]{2,1,0:T(8,128)(2,1)S(1)} %collective-permute-done.2.refs_4_) | copy-start | bytes 1105924
  31.5 28.1 %collective-permute-start.6 = (bf16[3,96,1920]{2,1,0:T(8,128)(2,1)}, bf16[3,96,1920]{2,1,0:T(8,128)(2,1)S(1)}, u32[]{:S(2)}, u32[]{:S(2)}) collective-permute-start(bf16[3,96,1920]{2,1,0:T(8,128)(2,1)} %pad_maximum_fusion), channel_id=1, source_target_pairs={{0,128},{128,0},{1,129},{129,1},{2,130},{130,2},{3,131},{131,3},{4... | collective-permute-start | bytes 3317768 | tf_op jit(solution)/shard_map/ppermute | solution.py:119
  32.4 27.2 %copy-start.3 = (bf16[2,512,384]{2,1,0:T(8,128)(2,1)}, bf16[2,512,384]{2,1,0:T(8,128)(2,1)S(1)}, u32[]{:S(2)}) copy-start(bf16[2,512,384]{2,1,0:T(8,128)(2,1)S(1)} %pad_maximum_fusion.2.pair_ref) | copy-start | bytes 2359300
  32.4 27.2 %collective-permute-start.4 = (bf16[2,512,384]{2,1,0:T(8,128)(2,1)S(1)}, bf16[2,512,384]{2,1,0:T(8,128)(2,1)S(1)}, u32[]{:S(2)}, u32[]{:S(2)}) collective-permute-start(bf16[2,512,384]{2,1,0:T(8,128)(2,1)S(1)} %pad_maximum_fusion.2.pair_ref), channel_id=1, source_target_pairs={{0,1},{1,2},{2,3},{3,0},{4,5},{5,6},{6,7},{7,4},{8,9},{9,10},{10,1... | collective-permute-start | bytes 2359304 | tf_op jit(solution)/shard_map/ppermute | solution.py:254
  33.7 25.9 %collective-permute-start.5 = (bf16[2,512,384]{2,1,0:T(8,128)(2,1)S(1)}, bf16[2,512,384]{2,1,0:T(8,128)(2,1)}, u32[]{:S(2)}, u32[]{:S(2)}) collective-permute-start(bf16[2,512,384]{2,1,0:T(8,128)(2,1)S(1)} %pad_maximum_fusion.2.pair_ref), channel_id=1, source_target_pairs={{0,3},{1,0},{2,1},{3,2},{4,7},{5,4},{6,5},{7,6},{8,11},{9,8},{10,9... | collective-permute-start | bytes 2359304 | tf_op jit(solution)/shard_map/ppermute | solution.py:257
  35.2 19.5 %collective-permute-start.7 = (bf16[1,96,1920]{2,1,0:T(8,128)(2,1)S(1)}, bf16[1,96,1920]{2,1,0:T(8,128)(2,1)}, u32[]{:S(2)}, u32[]{:S(2)}) collective-permute-start(bf16[1,96,1920]{2,1,0:T(8,128)(2,1)S(1)} %collective-permute-done.2.refs_4_), channel_id=1, source_target_pairs={{0,16},{16,32},{32,48},{48,64},{64,80},{80,96},{96,112},{112,0},{1... | collective-permute-start | bytes 1105928 | tf_op jit(solution)/shard_map/ppermute | solution.py:254
  36.5 18.2 %collective-permute-start.8 = (bf16[1,96,1920]{2,1,0:T(8,128)(2,1)}, bf16[1,96,1920]{2,1,0:T(8,128)(2,1)}, u32[]{:S(2)}, u32[]{:S(2)}) collective-permute-start(bf16[1,96,1920]{2,1,0:T(8,128)(2,1)} %collective-permute-done.3.refs_5_), channel_id=1, source_target_pairs={{0,112},{16,0},{32,16},{48,32},{64,48},{80,64},{96,80},{112,96},{1... | collective-permute-start | bytes 1105928 | tf_op jit(solution)/shard_map/ppermute | solution.py:257
  59.6 54.1 %copy-start.15 = (bf16[2,512,384]{2,1,0:T(8,128)(2,1)}, bf16[2,512,384]{2,1,0:T(8,128)(2,1)S(1)}, u32[]{:S(2)}) copy-start(bf16[2,512,384]{2,1,0:T(8,128)(2,1)S(1)} %collective-permute-done.4.right_ref) | copy-start | bytes 2359300
  59.6 50.3 %copy-start.5 = (bf16[3,96,1920]{2,1,0:T(8,128)(2,1)}, bf16[3,96,1920]{2,1,0:T(8,128)(2,1)S(1)}, u32[]{:S(2)}) copy-start(bf16[3,96,1920]{2,1,0:T(8,128)(2,1)S(1)} %collective-permute-done.6.refs_8_) | copy-start | bytes 3317764
  59.6 41.5 %collective-permute-start.16 = (bf16[3,768,384]{2,1,0:T(8,128)(2,1)S(1)}, bf16[3,768,384]{2,1,0:T(8,128)(2,1)S(1)}, u32[]{:S(2)}, u32[]{:S(2)}) collective-permute-start(bf16[3,768,384]{2,1,0:T(8,128)(2,1)S(1)} %constant_dynamic-slice_fusion), channel_id=1, source_target_pairs={{0,128},{128,0},{1,129},{129,1},{2,130},{130,2},{3,131},{131,3},{4... | collective-permute-start | bytes 5308424 | tf_op jit(solution)/shard_map/ppermute | solution.py:119
  62.5 15.8 %collective-permute-start.9 = (bf16[1,96,1920]{2,1,0:T(8,128)(2,1)}, bf16[1,96,1920]{2,1,0:T(8,128)(2,1)S(1)}, u32[]{:S(2)}, u32[]{:S(2)}) collective-permute-start(bf16[1,96,1920]{2,1,0:T(8,128)(2,1)} %collective-permute-done.7.refs_6_), channel_id=1, source_target_pairs={{0,16},{16,32},{32,48},{48,64},{64,80},{80,96},{96,112},{112,0},{1... | collective-permute-start | bytes 1105928 | tf_op jit(solution)/shard_map/ppermute | solution.py:254
  62.8 12.0 %collective-permute-start.10 = (bf16[1,96,1920]{2,1,0:T(8,128)(2,1)}, bf16[1,96,1920]{2,1,0:T(8,128)(2,1)S(1)}, u32[]{:S(2)}, u32[]{:S(2)}) collective-permute-start(bf16[1,96,1920]{2,1,0:T(8,128)(2,1)} %collective-permute-done.8.refs_7_), channel_id=1, source_target_pairs={{0,112},{16,0},{32,16},{48,32},{64,48},{80,64},{96,80},{112,96},{1... | collective-permute-start | bytes 1105928 | tf_op jit(solution)/shard_map/ppermute | solution.py:257
  65.2 23.3 %collective-permute-start.12 = (bf16[512,384]{1,0:T(8,128)(2,1)S(1)}, bf16[512,384]{1,0:T(8,128)(2,1)S(1)}, u32[]{:S(2)}, u32[]{:S(2)}) collective-permute-start(bf16[512,384]{1,0:T(8,128)(2,1)S(1)} %slice_bitcast_fusion.1), channel_id=1, source_target_pairs={{0,1},{1,2},{2,3},{3,0},{4,5},{5,6},{6,7},{7,4},{8,9},{9,10},{10,1... | collective-permute-start | bytes 1179656 | tf_op jit(solution)/shard_map/ppermute | solution.py:254
  67.7 21.5 %collective-permute-start.13 = (bf16[512,384]{1,0:T(8,128)(2,1)S(1)}, bf16[512,384]{1,0:T(8,128)(2,1)S(1)}, u32[]{:S(2)}, u32[]{:S(2)}) collective-permute-start(bf16[512,384]{1,0:T(8,128)(2,1)S(1)} %slice_bitcast_fusion), channel_id=1, source_target_pairs={{0,3},{1,0},{2,1},{3,2},{4,7},{5,4},{6,5},{7,6},{8,11},{9,8},{10,9... | collective-permute-start | bytes 1179656 | tf_op jit(solution)/shard_map/ppermute | solution.py:257
  74.8 36.1 %copy-start.9 = (bf16[1,96,1920]{2,1,0:T(8,128)(2,1)}, bf16[1,96,1920]{2,1,0:T(8,128)(2,1)S(1)}, u32[]{:S(2)}) copy-start(bf16[1,96,1920]{2,1,0:T(8,128)(2,1)S(1)} %collective-permute-done.10.refs_10_) | copy-start | bytes 1105924
  74.8 10.3 %collective-permute-start.15 = (bf16[1,48,1920]{2,1,0:T(8,128)(2,1)S(1)}, bf16[1,48,1920]{2,1,0:T(8,128)(2,1)S(1)}, u32[]{:S(2)}, u32[]{:S(2)}) collective-permute-start(bf16[1,48,1920]{2,1,0:T(8,128)(2,1)S(1)} %slice.25), channel_id=1, source_target_pairs={{0,112},{16,0},{32,16},{48,32},{64,48},{80,64},{96,80},{112,96},{1... | collective-permute-start | bytes 552968 | tf_op jit(solution)/shard_map/ppermute | solution.py:257
  78.3 32.6 %copy-start.7 = (bf16[1,96,1920]{2,1,0:T(8,128)(2,1)}, bf16[1,96,1920]{2,1,0:T(8,128)(2,1)S(1)}, u32[]{:S(2)}) copy-start(bf16[1,96,1920]{2,1,0:T(8,128)(2,1)S(1)} %collective-permute-done.9.refs_9_) | copy-start | bytes 1105924
  78.3 35.4 %copy-start.27 = (f32[3072]{0:T(1024)S(1)}, f32[3072]{0:T(1024)}, u32[]{:S(2)}) copy-start(f32[3072]{0:T(1024)} %param.9) | copy-start | bytes 36868
  78.4 10.2 %collective-permute-start.14 = (bf16[1,48,1920]{2,1,0:T(8,128)(2,1)S(1)}, bf16[1,48,1920]{2,1,0:T(8,128)(2,1)S(1)}, u32[]{:S(2)}, u32[]{:S(2)}) collective-permute-start(bf16[1,48,1920]{2,1,0:T(8,128)(2,1)S(1)} %slice.24), channel_id=1, source_target_pairs={{0,16},{16,32},{32,48},{48,64},{64,80},{80,96},{96,112},{112,0},{1... | collective-permute-start | bytes 552968 | tf_op jit(solution)/shard_map/ppermute | solution.py:254
  101.1 9.8 %copy-start.11 = (bf16[3,768,384]{2,1,0:T(8,128)(2,1)}, bf16[3,768,384]{2,1,0:T(8,128)(2,1)S(1)}, u32[]{:S(2)}) copy-start(bf16[3,768,384]{2,1,0:T(8,128)(2,1)S(1)} %collective-permute-done.16.near_ref) | copy-start | bytes 5308420
  101.1 4.5 %collective-permute-start.17 = (bf16[3,768,384]{2,1,0:T(8,128)(2,1)S(1)}, bf16[3,768,384]{2,1,0:T(8,128)(2,1)S(1)}, u32[]{:S(2)}, u32[]{:S(2)}) collective-permute-start(bf16[3,768,384]{2,1,0:T(8,128)(2,1)S(1)} %collective-permute-done.16.near_ref), channel_id=1, source_target_pairs={{0,8},{8,0},{1,9},{9,1},{2,10},{10,2},{3,11},{11,3},{4,12},{12,4},... | collective-permute-start | bytes 5308424 | tf_op jit(solution)/shard_map/ppermute | solution.py:294
  106.8 27.9 %collective-permute-start.19 = (bf16[3,96,1920]{2,1,0:T(8,128)(2,1)}, bf16[3,96,1920]{2,1,0:T(8,128)(2,1)}, u32[]{:S(2)}, u32[]{:S(2)}) collective-permute-start(bf16[3,96,1920]{2,1,0:T(8,128)(2,1)} %pad_maximum_fusion.1), channel_id=1, source_target_pairs={{0,128},{128,0},{1,129},{129,1},{2,130},{130,2},{3,131},{131,3},{4... | collective-permute-start | bytes 3317768 | tf_op jit(solution)/shard_map/ppermute | solution.py:119
  110.9 20.2 %collective-permute-start.11 = (bf16[1,96,1920]{2,1,0:T(8,128)(2,1)}, bf16[1,96,1920]{2,1,0:T(8,128)(2,1)}, u32[]{:S(2)}, u32[]{:S(2)}) collective-permute-start(bf16[1,96,1920]{2,1,0:T(8,128)(2,1)} %get-tuple-element.38), channel_id=1, source_target_pairs={{0,16},{16,32},{32,48},{48,64},{64,80},{80,96},{96,112},{112,0},{1... | collective-permute-start | bytes 1105928 | tf_op jit(solution)/shard_map/ppermute | solution.py:254
  111.0 20.1 %collective-permute-start.18 = (bf16[1,96,1920]{2,1,0:T(8,128)(2,1)}, bf16[1,96,1920]{2,1,0:T(8,128)(2,1)}, u32[]{:S(2)}, u32[]{:S(2)}) collective-permute-start(bf16[1,96,1920]{2,1,0:T(8,128)(2,1)} %get-tuple-element.46), channel_id=1, source_target_pairs={{0,112},{16,0},{32,16},{48,32},{64,48},{80,64},{96,80},{112,96},{1... | collective-permute-start | bytes 1105928 | tf_op jit(solution)/shard_map/ppermute | solution.py:257
  123.8 10.9 %copy-start.6 = (bf16[3,96,1920]{2,1,0:T(8,128)(2,1)S(1)}, bf16[3,96,1920]{2,1,0:T(8,128)(2,1)}, u32[]{:S(2)}) copy-start(bf16[3,96,1920]{2,1,0:T(8,128)(2,1)} %copy-done.5) | copy-start | bytes 3317764
  123.8 10.9 %copy-start.8 = (bf16[1,96,1920]{2,1,0:T(8,128)(2,1)S(1)}, bf16[1,96,1920]{2,1,0:T(8,128)(2,1)}, u32[]{:S(2)}) copy-start(bf16[1,96,1920]{2,1,0:T(8,128)(2,1)} %copy-done.7) | copy-start | bytes 1105924
  123.8 10.9 %copy-start.10 = (bf16[1,96,1920]{2,1,0:T(8,128)(2,1)S(1)}, bf16[1,96,1920]{2,1,0:T(8,128)(2,1)}, u32[]{:S(2)}) copy-start(bf16[1,96,1920]{2,1,0:T(8,128)(2,1)} %copy-done.9) | copy-start | bytes 1105924
  123.8 10.9 %copy-start.18 = (bf16[1,96,1920]{2,1,0:T(8,128)(2,1)S(1)}, bf16[1,96,1920]{2,1,0:T(8,128)(2,1)}, u32[]{:S(2)}) copy-start(bf16[1,96,1920]{2,1,0:T(8,128)(2,1)} %copy-done.17) | copy-start | bytes 1105924
  123.8 10.9 %copy-start.20 = (bf16[1,48,1920]{2,1,0:T(8,128)(2,1)S(1)}, bf16[1,48,1920]{2,1,0:T(8,128)(2,1)}, u32[]{:S(2)}) copy-start(bf16[1,48,1920]{2,1,0:T(8,128)(2,1)} %copy-done.19) | copy-start | bytes 552964
  123.8 10.9 %copy-start.22 = (bf16[1,48,1920]{2,1,0:T(8,128)(2,1)S(1)}, bf16[1,48,1920]{2,1,0:T(8,128)(2,1)}, u32[]{:S(2)}) copy-start(bf16[1,48,1920]{2,1,0:T(8,128)(2,1)} %copy-done.21) | copy-start | bytes 552964
  147.8 8.7 %collective-permute-start.24 = (bf16[512,1536]{1,0:T(8,128)(2,1)}, bf16[512,1536]{1,0:T(8,128)(2,1)S(1)}, u32[]{:S(2)}, u32[]{:S(2)}) collective-permute-start(bf16[512,1536]{1,0:T(8,128)(2,1)} %shard_map.85.activated_ref), channel_id=1, source_target_pairs={{0,8},{8,0},{1,9},{9,1},{2,10},{10,2},{3,11},{11,3},{4,12},{12,4},... | collective-permute-start | bytes 4718600 | tf_op jit(solution)/shard_map/ppermute | solution.py:311
  148.8 7.7 %collective-permute-start.23 = (bf16[512,384]{1,0:T(8,128)(2,1)}, bf16[512,384]{1,0:T(8,128)(2,1)S(1)}, u32[]{:S(2)}, u32[]{:S(2)}) collective-permute-start(bf16[512,384]{1,0:T(8,128)(2,1)} %shard_map.83.attended_ref), channel_id=1, source_target_pairs={{0,8},{8,0},{1,9},{9,1},{2,10},{10,2},{3,11},{11,3},{4,12},{12,4},... | collective-permute-start | bytes 1179656 | tf_op jit(solution)/shard_map/ppermute | solution.py:311
  160.7 22.7 %collective-permute-start.25 = (bf16[4,192,512]{2,1,0:T(8,128)(2,1)S(1)}, bf16[4,192,512]{2,1,0:T(8,128)(2,1)}, u32[]{:S(2)}, u32[]{:S(2)}) collective-permute-start(bf16[4,192,512]{2,1,0:T(8,128)(2,1)S(1)} %get-tuple-element.66), channel_id=1, source_target_pairs={{0,8},{8,0},{1,9},{9,1},{2,10},{10,2},{3,11},{11,3},{4,12},{12,4},... | collective-permute-start | bytes 2359304 | tf_op jit(solution)/shard_map/ppermute | solution.py:99
  161.3 22.1 %collective-permute-start.26 = (bf16[4,192,512]{2,1,0:T(8,128)(2,1)S(1)}, bf16[4,192,512]{2,1,0:T(8,128)(2,1)}, u32[]{:S(2)}, u32[]{:S(2)}) collective-permute-start(bf16[4,192,512]{2,1,0:T(8,128)(2,1)S(1)} %get-tuple-element.65), channel_id=1, source_target_pairs={{0,12},{4,8},{8,4},{12,0},{1,13},{5,9},{9,5},{13,1},{2,14},{6,10},... | collective-permute-start | bytes 2359304 | tf_op jit(solution)/shard_map/ppermute | solution.py:98
  162.4 12.0 %collective-permute-start.20 = (bf16[2,192,512]{2,1,0:T(8,128)(2,1)S(1)}, bf16[2,192,512]{2,1,0:T(8,128)(2,1)S(1)}, u32[]{:S(2)}, u32[]{:S(2)}) collective-permute-start(bf16[2,192,512]{2,1,0:T(8,128)(2,1)S(1)} %get-tuple-element.69), channel_id=1, source_target_pairs={{0,2},{1,3},{2,0},{3,1},{4,6},{5,7},{6,4},{7,5},{8,10},{9,11},{10,... | collective-permute-start | bytes 1179656 | tf_op jit(solution)/shard_map/ppermute | solution.py:88
  165.5 18.0 %collective-permute-start.21 = (bf16[2,192,512]{2,1,0:T(8,128)(2,1)S(1)}, bf16[2,192,512]{2,1,0:T(8,128)(2,1)S(1)}, u32[]{:S(2)}, u32[]{:S(2)}) collective-permute-start(bf16[2,192,512]{2,1,0:T(8,128)(2,1)S(1)} %get-tuple-element.68), channel_id=1, source_target_pairs={{0,1},{1,2},{2,3},{3,0},{4,5},{5,6},{6,7},{7,4},{8,9},{9,10},{10,1... | collective-permute-start | bytes 1179656 | tf_op jit(solution)/shard_map/ppermute | solution.py:88
  165.8 17.7 %collective-permute-start.22 = (bf16[2,192,512]{2,1,0:T(8,128)(2,1)S(1)}, bf16[2,192,512]{2,1,0:T(8,128)(2,1)S(1)}, u32[]{:S(2)}, u32[]{:S(2)}) collective-permute-start(bf16[2,192,512]{2,1,0:T(8,128)(2,1)S(1)} %get-tuple-element.67), channel_id=1, source_target_pairs={{0,3},{1,0},{2,1},{3,2},{4,7},{5,4},{6,5},{7,6},{8,11},{9,8},{10,9... | collective-permute-start | bytes 1179656 | tf_op jit(solution)/shard_map/ppermute | solution.py:88
  185.9 5.0 %copy-start.31 = (bf16[512,384]{1,0:T(8,128)(2,1)S(1)}, bf16[512,384]{1,0:T(8,128)(2,1)}, u32[]{:S(2)}) copy-start(bf16[512,384]{1,0:T(8,128)(2,1)} %param.8) | copy-start | bytes 1179652
  186.8 5.9 %collective-permute-start.27 = (bf16[192,512]{1,0:T(8,128)(2,1)}, bf16[192,512]{1,0:T(8,128)(2,1)}, u32[]{:S(2)}, u32[]{:S(2)}) collective-permute-start(bf16[192,512]{1,0:T(8,128)(2,1)} %fusion.5), channel_id=1, source_target_pairs={{0,4},{4,0},{1,5},{5,1},{2,6},{6,2},{3,7},{7,3},{8,12},{12,8},{9,1... | collective-permute-start | bytes 589832 | tf_op jit(solution)/shard_map/ppermute | solution.py:114
  187.3 6.3 %collective-permute-start.30 = (bf16[192,512]{1,0:T(8,128)(2,1)}, bf16[192,512]{1,0:T(8,128)(2,1)}, u32[]{:S(2)}, u32[]{:S(2)}) collective-permute-start(bf16[192,512]{1,0:T(8,128)(2,1)} %get-tuple-element.74), channel_id=1, source_target_pairs={{0,3},{1,0},{2,1},{3,2},{4,7},{5,4},{6,5},{7,6},{8,11},{9,8},{10,9... | collective-permute-start | bytes 589832 | tf_op jit(solution)/shard_map/ppermute | solution.py:88
  189.7 7.9 %collective-permute-start.29 = (bf16[192,512]{1,0:T(8,128)(2,1)S(1)}, bf16[192,512]{1,0:T(8,128)(2,1)}, u32[]{:S(2)}, u32[]{:S(2)}) collective-permute-start(bf16[192,512]{1,0:T(8,128)(2,1)S(1)} %get-tuple-element.75), channel_id=1, source_target_pairs={{0,1},{1,2},{2,3},{3,0},{4,5},{5,6},{6,7},{7,4},{8,9},{9,10},{10,1... | collective-permute-start | bytes 589832 | tf_op jit(solution)/shard_map/ppermute | solution.py:88
  189.7 9.7 %collective-permute-start.28 = (bf16[192,512]{1,0:T(8,128)(2,1)S(1)}, bf16[192,512]{1,0:T(8,128)(2,1)}, u32[]{:S(2)}, u32[]{:S(2)}) collective-permute-start(bf16[192,512]{1,0:T(8,128)(2,1)S(1)} %get-tuple-element.73), channel_id=1, source_target_pairs={{0,2},{1,3},{2,0},{3,1},{4,6},{5,7},{6,4},{7,5},{8,10},{9,11},{10,... | collective-permute-start | bytes 589832 | tf_op jit(solution)/shard_map/ppermute | solution.py:88
  (17 other events, 34.8 us)
Sparse Core Ops, SparseCore 0:
  9.2 48.6 all-gather.2
  59.8 72.0 all-gather.4

commit v3 on v2

--- a/solution.py
+++ b/solution.py
@@ -196,7 +196,7 @@
             out_ref[at : at + ref.shape[1]] = ref[i]
 
 
-def side_by_side(rows, shards):
+def side_by_side(rows, shards, count):
     places = tuple(places for places, _ in shards)
     slots = list(dict.fromkeys(place[:2] for group in places for place in group))
     width = shards[0][1].shape[2]
@@ -205,44 +205,49 @@
         functools.partial(gather_kernel, places, slots, rows),
         in_specs=[vmem] * len(shards),
         out_specs=vmem,
-        out_shape=jax.ShapeDtypeStruct((16 * rows, width), jnp.bfloat16),
+        out_shape=jax.ShapeDtypeStruct((count * rows, width), jnp.bfloat16),
         compiler_params=pltpu.CompilerParams(vmem_limit_bytes=32 * 2**20),
     )(*(arrays for _, arrays in shards))
     return gathered, slots
 
 
-def out_kernel(slots, at_ref, weights_ref, attended_ref, activated_ref, out_ref):
+def out_kernel(slots, at_ref, weights_ref, low_ref, high_ref, distant_ref, attended_ref, activated_ref, out_ref):
     yh, z = at_ref[0], at_ref[1]
     rows = out_ref.shape[1]
     split = attended_ref.shape[1]
     contract = (((1,), (1,)), ((), ()))
-    step = 4
-    for first in range(0, len(slots), step):
-        at = slice(first * rows, (first + step) * rows)
+
+    def put(block, slots):
         total = lax.dot_general(
-            weights_ref[at, :split], attended_ref[...], contract, preferred_element_type=jnp.float32
+            block[:, :split], attended_ref[...], contract, preferred_element_type=jnp.float32
         )
         total += lax.dot_general(
-            weights_ref[at, split:], activated_ref[...], contract, preferred_element_type=jnp.float32
+            block[:, split:], activated_ref[...], contract, preferred_element_type=jnp.float32
         )
         total = total.astype(out_ref.dtype)
-        for i in range(step):
-            other, offset = slots[first + i]
+        for i, (other, offset) in enumerate(slots):
             owner = (1 - yh if other else yh) * 8 + lax.rem(z + offset + 8, 8)
             out_ref[owner] = total[i * rows : (i + 1) * rows]
 
-
-def out_terms(place, slots, weights, attended, activated):
-    rows = weights.shape[0] // 16
+    early = weights_ref.shape[0] // rows
+    step = 4
+    for first in range(0, early, step):
+        last = min(first + step, early)
+        put(weights_ref[first * rows : last * rows], slots[first:last])
+    put(jnp.concatenate([low_ref[0], high_ref[0], *distant_ref[...]]), slots[early:])
+
+
+def out_terms(place, slots, weights, low, high, distant, attended, activated):
+    rows = low.shape[1]
     tokens = attended.shape[0]
     vmem = pl.BlockSpec(memory_space=pltpu.VMEM)
     return pl.pallas_call(
         functools.partial(out_kernel, slots),
-        in_specs=[pl.BlockSpec(memory_space=pltpu.SMEM), vmem, vmem, vmem],
+        in_specs=[pl.BlockSpec(memory_space=pltpu.SMEM)] + [vmem] * 6,
         out_specs=vmem,
         out_shape=jax.ShapeDtypeStruct((16, rows, tokens), jnp.bfloat16),
         compiler_params=pltpu.CompilerParams(vmem_limit_bytes=32 * 2**20),
-    )(place, weights, attended, activated)
+    )(place, weights, low, high, distant, attended, activated)
 
 
 def local(tokens, ln_gain, w_qkv, w_up, q_gain, k_gain, w_proj, w_down):
@@ -286,31 +291,31 @@
     far_a, far_b = up(right[0], "x", 4), down(left[1], "x", 4)
     shards += [([(0, -3, 0)], low), ([(0, 3, 0)], high)]
     end_a, end_b = up(low[:, :half]), down(high[:, half:])
-    other_low, other_high = tie((near[:1], near[2:]), (low, high))
-    other_low, other_high = up(other_low), down(other_high)
     shards += [([(0, 4, 0)], end_a), ([(0, 4, half)], end_b)]
-    shards += [([(1, -2, 0)], other_low), ([(1, 2, 0)], other_high)]
-    other_c = tie(other_c, (far_a, far_b, end_a, end_b))
+
+    ends = tie((near[:1], near[2:]), (low, high))
+    other_low, other_high = up(ends[0]), down(ends[1])
+
+    normed = norm_tokens(lax.axis_index("x"), ln_gain, pair, right, left, far_a, far_b)
+    other_c = tie(other_c, (normed, end_a, end_b))
     other_d = lax.ppermute(other_c, "c", SWAP)
-
-    normed = norm_tokens(lax.axis_index("x"), ln_gain, pair, right, left, far_a, far_b)
 
     base = (1 - yh) * 2 * quarter
     starts = jnp.stack([yh * 2 * quarter, base + c * quarter, base + (1 - c) * quarter])
     distant = jnp.concatenate([low, jnp.concatenate([end_a, end_b], axis=1), high])
-    normed = tie(normed, distant)
-    distant, other_d = lax.optimization_barrier((distant, other_d))
-    distant = across(distant)
-    shards += [([(1, -3, 0), (1, 4, 0), (1, 3, 0)], distant)]
+    distant = across(tie(distant, other_d))
     attended = attention(starts, normed, own_qkv, other_c, other_d, q_gain, k_gain)
-    shards = [(places, tie(arrays, attended)) for places, arrays in shards[-3:]] + shards[:-3]
-    weights, slots = side_by_side(piece, shards)
+
+    shards = [(places, tie(arrays, attended)) for places, arrays in shards]
+    weights, slots = side_by_side(piece, shards, 11)
+    slots += [(1, -2), (1, 2), (1, -3), (1, 4), (1, 3)]
+    weights = (weights, other_low, other_high, distant)
     activated = up_gelu(tie(normed, (attended, weights)), up_all)
 
     place = jnp.stack([yh, z])
     swapped = (lax.ppermute(attended, "c", SWAP), lax.ppermute(activated, "c", SWAP))
-    mine = out_terms(place, slots, weights, attended, activated)
-    theirs = out_terms(place, slots, weights, *tie(swapped, mine))
+    mine = out_terms(place, slots, *weights, attended, activated)
+    theirs = out_terms(place, slots, *weights, *tie(swapped, mine))
     mine, theirs = scatter_end(*scatter_start(mine, theirs))
     mine = mine.reshape(2, 1, piece, tok_count)
     theirs = theirs.reshape(2, 1, piece, tok_count)

time: 211 us -> 209 us (level)
  waiting for transfers between devices: 81.3 us -> 74.9 us
  local copies, waits for them, and re-layouts: 21.6 us -> 24 us
  Pallas kernels: 31.1 us -> 33.4 us
    ppermute x7, waiting for transfers between devices: 12.2 us -> 1.1 us  [down(): return lax.ppermute(v, axis, shift(size, -1))]
    unnamed x65 -> x55, local copies, waits for them, and re-layouts: 15.2 us -> 13.2 us
  transfers between devices with their start and end apart: 33 -> 33, of which waited for: 15 -> 15; matrix products, arithmetic and copies ran while one was open for 5% -> 8% of each run, Pallas kernels for 9% -> 10%
where the time goes in v3:
time: 209 us; the launch traced here: 207 us
  waiting for transfers between devices  74.9 us (36%)
  starting transfers between devices  50 us (24%)
  Pallas kernels  33.4 us (16%)
  local copies, waits for them, and re-layouts  24 us (11%)
  between operations  13.7 us (7%)
  other arithmetic  11.2 us (5%)
    ppermute x4, waiting for transfers between devices, across(): return lax.ppermute(v, 'yh', SWAP)  24.9 us
    ppermute x6, waiting for transfers between devices, to_peers_x(): lax.ppermute(pick(blocks, (x + k) % 4, axis), 'x', shift(4, k))  22.4 us
    ppermute x7, waiting for transfers between devices, up(): return lax.ppermute(v, axis, shift(size, 1))  19.7 us
    ppermute x7, starting transfers between devices, down(): return lax.ppermute(v, axis, shift(size, -1))  19 us
    unnamed x55, local copies, waits for them, and re-layouts  13.2 us
    pallas_call x2, Pallas kernels, out_terms(): pl.pallas_call(functools.partial(out_kernel, slots), in_specs=[pl.BlockSp...  10.5 us
    ppermute x6, starting transfers between devices, to_peers_x(): lax.ppermute(pick(blocks, (x + k) % 4, axis), 'x', shift(4, k))  9.49 us
    ppermute x4, starting transfers between devices, across(): return lax.ppermute(v, 'yh', SWAP)  8.7 us
  transfers between devices with their start and end apart: 33, of which 15 were waited for; matrix products, arithmetic and copies ran while one was open for 8% of the time, Pallas kernels for 10%

profile of v3, /device:TPU:1, one launch (start us, length us, event | category | flops | bytes accessed | tf_op | source)
XLA Modules:
  0.0 207.2 jit_solution(15913652131386346477)
XLA Ops:
  7.3 2.2 %collective-permute-start = (bf16[512,384]{1,0:T(8,128)(2,1)}, bf16[512,384]{1,0:T(8,128)(2,1)S(1)}, u32[]{:S(2)}, u32[]{:S(2)}) collective-permute-start(bf16[512,384]{1,0:T(8,128)(2,1)} %param.8), channel_id=1, source_target_pairs={{0,4},{4,0},{1,5},{5,1},{2,6},{6,2},{3,7},{7,3},{8,12},{12,8},{9,1... | collective-permute-start | bytes 1179656 | tf_op jit(solution)/shard_map/ppermute | solution.py:270
  10.5 1.7 collective-permute-start.2
  12.2 4.0 %collective-permute-start.3 = (bf16[1,96,1920]{2,1,0:T(8,128)(2,1)S(1)}, bf16[1,96,1920]{2,1,0:T(8,128)(2,1)}, u32[]{:S(2)}, u32[]{:S(2)}) collective-permute-start(bf16[1,96,1920]{2,1,0:T(8,128)(2,1)S(1)} %maximum_bitcast_fusion.refs_0_), channel_id=1, source_target_pairs={{0,112},{16,0},{32,16},{48,32},{64,48},{80,64},{96,80},{112,96},{1... | collective-permute-start | bytes 1105928 | tf_op jit(solution)/shard_map/ppermute | solution.py:262
  16.3 2.6 %collective-permute-start.1 = (bf16[96,1536]{1,0:T(8,128)(2,1)}, bf16[96,1536]{1,0:T(8,128)(2,1)S(1)}, u32[]{:S(2)}, u32[]{:S(2)}) collective-permute-start(bf16[96,1536]{1,0:T(8,128)(2,1)} %param.11), channel_id=1, source_target_pairs={{0,128},{128,0},{1,129},{129,1},{2,130},{130,2},{3,131},{131,3},{4... | collective-permute-start | bytes 884744 | tf_op jit(solution)/shard_map/ppermute | solution.py:119
  18.9 8.3 %collective-permute-done.1 = bf16[96,1536]{1,0:T(8,128)(2,1)S(1)} collective-permute-done((bf16[96,1536]{1,0:T(8,128)(2,1)}, bf16[96,1536]{1,0:T(8,128)(2,1)S(1)}, u32[]{:S(2)}, u32[]{:S(2)}) %collective-permute-start.1) | collective-permute-done | bytes 294944 | tf_op jit(solution)/shard_map/ppermute | solution.py:119
  27.2 2.1 %maximum_select_fusion = bf16[2,96,1536]{2,1,0:T(8,128)(2,1)} fusion(bf16[1,96,1536]{2,1,0:T(8,128)(2,1)S(1)} %bitcast.77, bf16[1,96,1536]{2,1,0:T(8,128)(2,1)} %bitcast.76, pred[]{:T(512)S(6)} %eq.20), kind=kLoop, calls=%fused_computation.10 | loop fusion | flops 884736 | bytes 1179649 | tf_op jit(solution)/shard_map/jit(_where)/select_n | solution.py:78
  29.3 2.2 %pad_maximum_fusion = bf16[3,96,1920]{2,1,0:T(8,128)(2,1)} fusion(bf16[1,96,1920]{2,1,0:T(8,128)(2,1)} %collective-permute-done.3.refs_2_, bf16[1,96,1920]{2,1,0:T(8,128)(2,1)S(1)} %maximum_bitcast_fusion.refs_0_, bf16[1,96,1920]{2,1,0:T(8,128)(2,1)S(1)} %collective-permute-done.2.refs_1_), kind=kLoop, calls=%fused_computation.1 | loop fusion | flops 1105920 | bytes 2211840 | tf_op jit(solution)/shard_map/concatenate | solution.py:280
  32.4 1.3 collective-permute-start.4
  33.7 1.5 collective-permute-start.5
  35.1 1.3 collective-permute-start.7
  36.5 4.1 %collective-permute-start.8 = (bf16[1,96,1920]{2,1,0:T(8,128)(2,1)}, bf16[1,96,1920]{2,1,0:T(8,128)(2,1)}, u32[]{:S(2)}, u32[]{:S(2)}) collective-permute-start(bf16[1,96,1920]{2,1,0:T(8,128)(2,1)} %collective-permute-done.3.refs_2_), channel_id=1, source_target_pairs={{0,112},{16,0},{32,16},{48,32},{64,48},{80,64},{96,80},{112,96},{1... | collective-permute-start | bytes 1105928 | tf_op jit(solution)/shard_map/ppermute | solution.py:262
  40.5 14.1 %collective-permute-done.7.refs_3_ = bf16[1,96,1920]{2,1,0:T(8,128)(2,1)} collective-permute-done((bf16[1,96,1920]{2,1,0:T(8,128)(2,1)S(1)}, bf16[1,96,1920]{2,1,0:T(8,128)(2,1)}, u32[]{:S(2)}, u32[]{:S(2)}) %collective-permute-start.7) | collective-permute-done | bytes 368672 | tf_op jit(solution)/shard_map/ppermute | solution.py:259
  54.7 3.3 %all-gather.3.cloned.1.call-done.own_ref = bf16[3,1536,384]{2,1,0:T(8,128)(2,1)} async-done(((bf16[3,96,384]{2,1,0:T(8,128)(2,1)}), bf16[3,1536,384]{2,1,0:T(8,128)(2,1)}) %all-gather.3.cloned.1.call-update) | async-done | bytes 3538960 | tf_op jit(solution)/shard_map/all_gather | solution.py:264
  57.9 2.9 %constant_dynamic-slice_fusion = bf16[3,768,384]{2,1,0:T(8,128)(2,1)} fusion(bf16[3,1536,384]{2,1,0:T(8,128)(2,1)} %all-gather.3.cloned.1.call-done.own_ref, s32[]{:T(128)S(6)} %select_n.111), kind=kLoop, calls=%fused_computation.31 | loop fusion | bytes 3538948 | tf_op jit(solution)/shard_map/dynamic_slice | solution.py:282
  60.9 2.8 %collective-permute-start.11 = (bf16[3,768,384]{2,1,0:T(8,128)(2,1)}, bf16[3,768,384]{2,1,0:T(8,128)(2,1)}, u32[]{:S(2)}, u32[]{:S(2)}) collective-permute-start(bf16[3,768,384]{2,1,0:T(8,128)(2,1)} %constant_dynamic-slice_fusion), channel_id=1, source_target_pairs={{0,128},{128,0},{1,129},{129,1},{2,130},{130,2},{3,131},{131,3},{4... | collective-permute-start | bytes 5308424 | tf_op jit(solution)/shard_map/ppermute | solution.py:119
  64.0 2.4 %collective-permute-start.14 = (bf16[1,96,1920]{2,1,0:T(8,128)(2,1)}, bf16[1,96,1920]{2,1,0:T(8,128)(2,1)S(1)}, u32[]{:S(2)}, u32[]{:S(2)}) collective-permute-start(bf16[1,96,1920]{2,1,0:T(8,128)(2,1)} %collective-permute-done.8.refs_4_), channel_id=1, source_target_pairs={{0,112},{16,0},{32,16},{48,32},{64,48},{80,64},{96,80},{112,96},{1... | collective-permute-start | bytes 1105928 | tf_op jit(solution)/shard_map/ppermute | solution.py:262
  67.2 1.4 collective-permute-start.9
  68.6 1.9 slice_bitcast_fusion
  71.7 4.7 %collective-permute-done.12.refs_6_ = bf16[1,96,1920]{2,1,0:T(8,128)(2,1)S(1)} collective-permute-done((bf16[1,96,1920]{2,1,0:T(8,128)(2,1)}, bf16[1,96,1920]{2,1,0:T(8,128)(2,1)S(1)}, u32[]{:S(2)}, u32[]{:S(2)}) %collective-permute-start.12) | collective-permute-done | bytes 368672 | tf_op jit(solution)/shard_map/ppermute | solution.py:259
  78.9 3.4 %collective-permute-start.15 = (bf16[1,48,1920]{2,1,0:T(8,128)(2,1)}, bf16[1,48,1920]{2,1,0:T(8,128)(2,1)}, u32[]{:S(2)}, u32[]{:S(2)}) collective-permute-start(bf16[1,48,1920]{2,1,0:T(8,128)(2,1)} %slice.25), channel_id=1, source_target_pairs={{0,112},{16,0},{32,16},{48,32},{64,48},{80,64},{96,80},{112,96},{1... | collective-permute-start | bytes 552968 | tf_op jit(solution)/shard_map/ppermute | solution.py:262
  86.4 4.3 %shard_map.82.x_ref = bf16[512,3072]{1,0:T(8,128)(2,1)S(1)} custom-call(s32[1]{0:T(128)} %bitcast.8.x_ref, f32[1,3072]{1,0:T(1,128)S(1)} %bitcast.71, bf16[2,512,384]{2,1,0:T(8,128)(2,1)S(1)} %copy-done.4, bf16[2,512,384]{2,1,0:T(8,128)(2,1)S(1)} %copy-done.17, bf16[2,512,384]{2,1,0:T(8,128)(2,1)} %collective-permute-done.5.left_ref, ...), custom_call_target="tpu_custom_call" | custom-call | tf_op jit(solution)/shard_map/pallas_call | solution.py:58
  90.8 11.9 %collective-permute-done.11.near_ref = bf16[3,768,384]{2,1,0:T(8,128)(2,1)} collective-permute-done((bf16[3,768,384]{2,1,0:T(8,128)(2,1)}, bf16[3,768,384]{2,1,0:T(8,128)(2,1)}, u32[]{:S(2)}, u32[]{:S(2)}) %collective-permute-start.11) | collective-permute-done | bytes 1769504 | tf_op jit(solution)/shard_map/ppermute | solution.py:119
  103.8 2.2 %pad_maximum_fusion.1 = bf16[3,96,1920]{2,1,0:T(8,128)(2,1)} fusion(bf16[1,96,1920]{2,1,0:T(8,128)(2,1)S(1)} %copy-done.12, bf16[1,48,1920]{2,1,0:T(8,128)(2,1)} %collective-permute-done.15.refs_9_, bf16[1,48,1920]{2,1,0:T(8,128)(2,1)} %collective-permute-done.13.refs_8_, bf16[1,96,1920]{2,1,0:T(8,128)(2,1)S(1)} %copy-done.9), kind=kLoop, calls=%fused_computation.2 | loop fusion | flops 4423680 | bytes 2211840 | tf_op jit(solution)/shard_map/concatenate | solution.py:305
  106.0 1.5 collective-permute-done.16.far_ref
  107.5 1.3 copy-done.14
  108.8 2.6 %collective-permute-start.19 = (bf16[3,96,1920]{2,1,0:T(8,128)(2,1)}, bf16[3,96,1920]{2,1,0:T(8,128)(2,1)}, u32[]{:S(2)}, u32[]{:S(2)}) collective-permute-start(bf16[3,96,1920]{2,1,0:T(8,128)(2,1)} %pad_maximum_fusion.1), channel_id=1, source_target_pairs={{0,128},{128,0},{1,129},{129,1},{2,130},{130,2},{3,131},{131,3},{4... | collective-permute-start | bytes 3317768 | tf_op jit(solution)/shard_map/ppermute | solution.py:119
  112.6 2.4 %collective-permute-start.18 = (bf16[1,96,1920]{2,1,0:T(8,128)(2,1)}, bf16[1,96,1920]{2,1,0:T(8,128)(2,1)}, u32[]{:S(2)}, u32[]{:S(2)}) collective-permute-start(bf16[1,96,1920]{2,1,0:T(8,128)(2,1)} %get-tuple-element.58), channel_id=1, source_target_pairs={{0,112},{16,0},{32,16},{48,32},{64,48},{80,64},{96,80},{112,96},{1... | collective-permute-start | bytes 1105928 | tf_op jit(solution)/shard_map/ppermute | solution.py:262
  115.1 2.0 copy-done.2
  117.1 1.5 copy-done.15
  118.6 8.5 %shard_map.83.attended_ref = bf16[512,384]{1,0:T(8,128)(2,1)} custom-call(s32[3]{0:T(128)S(1)} %pad_add_fusion.1.starts_ref, bf16[512,3072]{1,0:T(8,128)(2,1)S(1)} %shard_map.82.x_ref, bf16[3,1536,384]{2,1,0:T(8,128)(2,1)S(1)} %copy-done.2, bf16[3,768,384]{2,1,0:T(8,128)(2,1)} %collective-permute-done.11.near_ref, bf16[3,768,384]{2,1,0:T(8,128)(2,1)S(1)} %copy-done.15, ...), custom_call_target="tpu_custom_call" | custom-call | tf_op jit(solution)/shard_map/pallas_call | solution.py:181
  127.1 1.6 shard_map.84.weights_ref
  128.7 2.0 copy-done
  131.6 4.7 %collective-permute-done.19.distant_ref = bf16[3,96,1920]{2,1,0:T(8,128)(2,1)} collective-permute-done((bf16[3,96,1920]{2,1,0:T(8,128)(2,1)}, bf16[3,96,1920]{2,1,0:T(8,128)(2,1)}, u32[]{:S(2)}, u32[]{:S(2)}) %collective-permute-start.19) | collective-permute-done | bytes 1105952 | tf_op jit(solution)/shard_map/ppermute | solution.py:119
  136.2 8.5 %shard_map.85.activated_ref = bf16[512,1536]{1,0:T(8,128)(2,1)} custom-call(bf16[512,3072]{1,0:T(8,128)(2,1)S(1)} %shard_map.82.x_ref, bf16[3072,1536]{1,0:T(8,128)(2,1)} %bitcast.72), custom_call_target="tpu_custom_call" | custom-call | tf_op jit(solution)/shard_map/pallas_call | solution.py:131
  144.8 1.2 collective-permute-start.24
  146.1 2.1 %copy-done.1 = bf16[1056,1920]{1,0:T(8,128)(2,1)S(1)} copy-done((bf16[1056,1920]{1,0:T(8,128)(2,1)S(1)}, bf16[1056,1920]{1,0:T(8,128)(2,1)}, u32[]{:S(2)}) %copy-start.1) | copy-done | bytes 4055064
  148.2 5.5 %shard_map.86 = bf16[16,96,512]{2,1,0:T(8,128)(2,1)S(1)} custom-call(s32[2]{0:T(128)S(1)} %pad_add_fusion.at_ref, bf16[1056,1920]{1,0:T(8,128)(2,1)S(1)} %copy-done.1, bf16[1,96,1920]{2,1,0:T(8,128)(2,1)} %collective-permute-done.17.low_ref, bf16[1,96,1920]{2,1,0:T(8,128)(2,1)} %collective-permute-done.18.high_ref, ...), custom_call_target="tpu_custom_call" | custom-call | tf_op jit(solution)/shard_map/pallas_call | solution.py:244
  153.8 4.9 %shard_map.87 = bf16[16,96,512]{2,1,0:T(8,128)(2,1)S(1)} custom-call(s32[2]{0:T(128)S(1)} %pad_add_fusion.at_ref, bf16[1056,1920]{1,0:T(8,128)(2,1)S(1)} %copy-done.1, bf16[1,96,1920]{2,1,0:T(8,128)(2,1)} %collective-permute-done.17.low_ref, bf16[1,96,1920]{2,1,0:T(8,128)(2,1)} %collective-permute-done.18.high_ref, ...), custom_call_target="tpu_custom_call" | custom-call | tf_op jit(solution)/shard_map/pallas_call | solution.py:244
  160.6 3.0 %collective-permute-start.20 = (bf16[2,192,512]{2,1,0:T(8,128)(2,1)S(1)}, bf16[2,192,512]{2,1,0:T(8,128)(2,1)S(1)}, u32[]{:S(2)}, u32[]{:S(2)}) collective-permute-start(bf16[2,192,512]{2,1,0:T(8,128)(2,1)S(1)} %get-tuple-element.79), channel_id=1, source_target_pairs={{0,2},{1,3},{2,0},{3,1},{4,6},{5,7},{6,4},{7,5},{8,10},{9,11},{10,... | collective-permute-start | bytes 1179656 | tf_op jit(solution)/shard_map/ppermute | solution.py:88
  163.9 2.3 %collective-permute-start.22 = (bf16[2,192,512]{2,1,0:T(8,128)(2,1)S(1)}, bf16[2,192,512]{2,1,0:T(8,128)(2,1)S(1)}, u32[]{:S(2)}, u32[]{:S(2)}) collective-permute-start(bf16[2,192,512]{2,1,0:T(8,128)(2,1)S(1)} %get-tuple-element.77), channel_id=1, source_target_pairs={{0,3},{1,0},{2,1},{3,2},{4,7},{5,4},{6,5},{7,6},{8,11},{9,8},{10,9... | collective-permute-start | bytes 1179656 | tf_op jit(solution)/shard_map/ppermute | solution.py:88
  166.2 6.2 %collective-permute-done.20 = bf16[2,192,512]{2,1,0:T(8,128)(2,1)S(1)} collective-permute-done((bf16[2,192,512]{2,1,0:T(8,128)(2,1)S(1)}, bf16[2,192,512]{2,1,0:T(8,128)(2,1)S(1)}, u32[]{:S(2)}, u32[]{:S(2)}) %collective-permute-start.20) | collective-permute-done | bytes 393248 | tf_op jit(solution)/shard_map/ppermute | solution.py:88
  172.5 9.2 %collective-permute-done.21 = bf16[2,192,512]{2,1,0:T(8,128)(2,1)S(1)} collective-permute-done((bf16[2,192,512]{2,1,0:T(8,128)(2,1)S(1)}, bf16[2,192,512]{2,1,0:T(8,128)(2,1)S(1)}, u32[]{:S(2)}, u32[]{:S(2)}) %collective-permute-start.21) | collective-permute-done | bytes 393248 | tf_op jit(solution)/shard_map/ppermute | solution.py:88
  181.6 1.7 convert_add_fusion
  185.4 2.6 %collective-permute-start.30 = (bf16[192,512]{1,0:T(8,128)(2,1)}, bf16[192,512]{1,0:T(8,128)(2,1)}, u32[]{:S(2)}, u32[]{:S(2)}) collective-permute-start(bf16[192,512]{1,0:T(8,128)(2,1)} %get-tuple-element.84), channel_id=1, source_target_pairs={{0,3},{1,0},{2,1},{3,2},{4,7},{5,4},{6,5},{7,6},{8,11},{9,8},{10,9... | collective-permute-start | bytes 589832 | tf_op jit(solution)/shard_map/ppermute | solution.py:88
  189.5 1.4 collective-permute-done.27
  191.9 4.1 %collective-permute-done.29 = bf16[192,512]{1,0:T(8,128)(2,1)} collective-permute-done((bf16[192,512]{1,0:T(8,128)(2,1)S(1)}, bf16[192,512]{1,0:T(8,128)(2,1)}, u32[]{:S(2)}, u32[]{:S(2)}) %collective-permute-start.29) | collective-permute-done | bytes 196640 | tf_op jit(solution)/shard_map/ppermute | solution.py:88
  196.0 1.9 collective-permute-done.28
  197.8 1.4 fusion.4
  (106 shorter events, 22.7 us)
Async XLA Ops:
  6.5 51.4 %all-gather.3.cloned.1.call-start = ((), (), s32[]{:S(2)}) async-start(), calls=%async_computation | async-start | bytes 3760128 | tf_op jit(solution)/shard_map/all_gather | solution.py:264
  7.3 129.0 %all-gather.5.cloned.1.call-start = ((), (), s32[]{:S(2)}) async-start(), calls=%async_computation.1 | async-start | bytes 10027008 | tf_op jit(solution)/shard_map/all_gather | solution.py:273
  7.3 19.9 %collective-permute-start = (bf16[512,384]{1,0:T(8,128)(2,1)}, bf16[512,384]{1,0:T(8,128)(2,1)S(1)}, u32[]{:S(2)}, u32[]{:S(2)}) collective-permute-start(bf16[512,384]{1,0:T(8,128)(2,1)} %param.8), channel_id=1, source_target_pairs={{0,4},{4,0},{1,5},{5,1},{2,6},{6,2},{3,7},{7,3},{8,12},{12,8},{9,1... | collective-permute-start | bytes 1179656 | tf_op jit(solution)/shard_map/ppermute | solution.py:270
  10.5 16.7 %collective-permute-start.2 = (bf16[1,96,1920]{2,1,0:T(8,128)(2,1)S(1)}, bf16[1,96,1920]{2,1,0:T(8,128)(2,1)S(1)}, u32[]{:S(2)}, u32[]{:S(2)}) collective-permute-start(bf16[1,96,1920]{2,1,0:T(8,128)(2,1)S(1)} %maximum_bitcast_fusion.refs_0_), channel_id=1, source_target_pairs={{0,16},{16,32},{32,48},{48,64},{64,80},{80,96},{96,112},{112,0},{1... | collective-permute-start | bytes 1105928 | tf_op jit(solution)/shard_map/ppermute | solution.py:259
  12.2 15.0 %collective-permute-start.3 = (bf16[1,96,1920]{2,1,0:T(8,128)(2,1)S(1)}, bf16[1,96,1920]{2,1,0:T(8,128)(2,1)}, u32[]{:S(2)}, u32[]{:S(2)}) collective-permute-start(bf16[1,96,1920]{2,1,0:T(8,128)(2,1)S(1)} %maximum_bitcast_fusion.refs_0_), channel_id=1, source_target_pairs={{0,112},{16,0},{32,16},{48,32},{64,48},{80,64},{96,80},{112,96},{1... | collective-permute-start | bytes 1105928 | tf_op jit(solution)/shard_map/ppermute | solution.py:262
  16.3 10.9 %collective-permute-start.1 = (bf16[96,1536]{1,0:T(8,128)(2,1)}, bf16[96,1536]{1,0:T(8,128)(2,1)S(1)}, u32[]{:S(2)}, u32[]{:S(2)}) collective-permute-start(bf16[96,1536]{1,0:T(8,128)(2,1)} %param.11), channel_id=1, source_target_pairs={{0,128},{128,0},{1,129},{129,1},{2,130},{130,2},{3,131},{131,3},{4... | collective-permute-start | bytes 884744 | tf_op jit(solution)/shard_map/ppermute | solution.py:119
  27.2 8.0 %copy-start.18 = (bf16[1,96,1920]{2,1,0:T(8,128)(2,1)}, bf16[1,96,1920]{2,1,0:T(8,128)(2,1)S(1)}, u32[]{:S(2)}) copy-start(bf16[1,96,1920]{2,1,0:T(8,128)(2,1)S(1)} %collective-permute-done.2.refs_1_) | copy-start | bytes 1105924
  31.5 29.3 %collective-permute-start.6 = (bf16[3,96,1920]{2,1,0:T(8,128)(2,1)}, bf16[3,96,1920]{2,1,0:T(8,128)(2,1)S(1)}, u32[]{:S(2)}, u32[]{:S(2)}) collective-permute-start(bf16[3,96,1920]{2,1,0:T(8,128)(2,1)} %pad_maximum_fusion), channel_id=1, source_target_pairs={{0,128},{128,0},{1,129},{129,1},{2,130},{130,2},{3,131},{131,3},{4... | collective-permute-start | bytes 3317768 | tf_op jit(solution)/shard_map/ppermute | solution.py:119
  32.4 28.4 %copy-start.3 = (bf16[2,512,384]{2,1,0:T(8,128)(2,1)}, bf16[2,512,384]{2,1,0:T(8,128)(2,1)S(1)}, u32[]{:S(2)}) copy-start(bf16[2,512,384]{2,1,0:T(8,128)(2,1)S(1)} %pad_maximum_fusion.2.pair_ref) | copy-start | bytes 2359300
  32.4 28.4 %collective-permute-start.4 = (bf16[2,512,384]{2,1,0:T(8,128)(2,1)S(1)}, bf16[2,512,384]{2,1,0:T(8,128)(2,1)S(1)}, u32[]{:S(2)}, u32[]{:S(2)}) collective-permute-start(bf16[2,512,384]{2,1,0:T(8,128)(2,1)S(1)} %pad_maximum_fusion.2.pair_ref), channel_id=1, source_target_pairs={{0,1},{1,2},{2,3},{3,0},{4,5},{5,6},{6,7},{7,4},{8,9},{9,10},{10,1... | collective-permute-start | bytes 2359304 | tf_op jit(solution)/shard_map/ppermute | solution.py:259
  33.7 27.2 %collective-permute-start.5 = (bf16[2,512,384]{2,1,0:T(8,128)(2,1)S(1)}, bf16[2,512,384]{2,1,0:T(8,128)(2,1)}, u32[]{:S(2)}, u32[]{:S(2)}) collective-permute-start(bf16[2,512,384]{2,1,0:T(8,128)(2,1)S(1)} %pad_maximum_fusion.2.pair_ref), channel_id=1, source_target_pairs={{0,3},{1,0},{2,1},{3,2},{4,7},{5,4},{6,5},{7,6},{8,11},{9,8},{10,9... | collective-permute-start | bytes 2359304 | tf_op jit(solution)/shard_map/ppermute | solution.py:262
  35.1 19.5 %collective-permute-start.7 = (bf16[1,96,1920]{2,1,0:T(8,128)(2,1)S(1)}, bf16[1,96,1920]{2,1,0:T(8,128)(2,1)}, u32[]{:S(2)}, u32[]{:S(2)}) collective-permute-start(bf16[1,96,1920]{2,1,0:T(8,128)(2,1)S(1)} %collective-permute-done.2.refs_1_), channel_id=1, source_target_pairs={{0,16},{16,32},{32,48},{48,64},{64,80},{80,96},{96,112},{112,0},{1... | collective-permute-start | bytes 1105928 | tf_op jit(solution)/shard_map/ppermute | solution.py:259
  36.5 18.2 %collective-permute-start.8 = (bf16[1,96,1920]{2,1,0:T(8,128)(2,1)}, bf16[1,96,1920]{2,1,0:T(8,128)(2,1)}, u32[]{:S(2)}, u32[]{:S(2)}) collective-permute-start(bf16[1,96,1920]{2,1,0:T(8,128)(2,1)} %collective-permute-done.3.refs_2_), channel_id=1, source_target_pairs={{0,112},{16,0},{32,16},{48,32},{64,48},{80,64},{96,80},{112,96},{1... | collective-permute-start | bytes 1105928 | tf_op jit(solution)/shard_map/ppermute | solution.py:262
  60.8 22.3 %copy-start.22 = (f32[3072]{0:T(1024)S(1)}, f32[3072]{0:T(1024)}, u32[]{:S(2)}) copy-start(f32[3072]{0:T(1024)} %param.9) | copy-start | bytes 36868
  60.8 22.3 %copy-start.16 = (bf16[2,512,384]{2,1,0:T(8,128)(2,1)}, bf16[2,512,384]{2,1,0:T(8,128)(2,1)S(1)}, u32[]{:S(2)}) copy-start(bf16[2,512,384]{2,1,0:T(8,128)(2,1)S(1)} %collective-permute-done.4.right_ref) | copy-start | bytes 2359300
  60.9 22.2 %copy-start.5 = (bf16[3,96,1920]{2,1,0:T(8,128)(2,1)}, bf16[3,96,1920]{2,1,0:T(8,128)(2,1)S(1)}, u32[]{:S(2)}) copy-start(bf16[3,96,1920]{2,1,0:T(8,128)(2,1)S(1)} %collective-permute-done.6.refs_5_) | copy-start | bytes 3317764
  60.9 41.8 %collective-permute-start.11 = (bf16[3,768,384]{2,1,0:T(8,128)(2,1)}, bf16[3,768,384]{2,1,0:T(8,128)(2,1)}, u32[]{:S(2)}, u32[]{:S(2)}) collective-permute-start(bf16[3,768,384]{2,1,0:T(8,128)(2,1)} %constant_dynamic-slice_fusion), channel_id=1, source_target_pairs={{0,128},{128,0},{1,129},{129,1},{2,130},{130,2},{3,131},{131,3},{4... | collective-permute-start | bytes 5308424 | tf_op jit(solution)/shard_map/ppermute | solution.py:119
  63.7 12.6 %collective-permute-start.12 = (bf16[1,96,1920]{2,1,0:T(8,128)(2,1)}, bf16[1,96,1920]{2,1,0:T(8,128)(2,1)S(1)}, u32[]{:S(2)}, u32[]{:S(2)}) collective-permute-start(bf16[1,96,1920]{2,1,0:T(8,128)(2,1)} %collective-permute-done.7.refs_3_), channel_id=1, source_target_pairs={{0,16},{16,32},{32,48},{48,64},{64,80},{80,96},{96,112},{112,0},{1... | collective-permute-start | bytes 1105928 | tf_op jit(solution)/shard_map/ppermute | solution.py:259
  64.0 14.2 %collective-permute-start.14 = (bf16[1,96,1920]{2,1,0:T(8,128)(2,1)}, bf16[1,96,1920]{2,1,0:T(8,128)(2,1)S(1)}, u32[]{:S(2)}, u32[]{:S(2)}) collective-permute-start(bf16[1,96,1920]{2,1,0:T(8,128)(2,1)} %collective-permute-done.8.refs_4_), channel_id=1, source_target_pairs={{0,112},{16,0},{32,16},{48,32},{64,48},{80,64},{96,80},{112,96},{1... | collective-permute-start | bytes 1105928 | tf_op jit(solution)/shard_map/ppermute | solution.py:262
  67.2 15.2 %collective-permute-start.9 = (bf16[512,384]{1,0:T(8,128)(2,1)}, bf16[512,384]{1,0:T(8,128)(2,1)S(1)}, u32[]{:S(2)}, u32[]{:S(2)}) collective-permute-start(bf16[512,384]{1,0:T(8,128)(2,1)} %slice_bitcast_fusion.1), channel_id=1, source_target_pairs={{0,1},{1,2},{2,3},{3,0},{4,5},{5,6},{6,7},{7,4},{8,9},{9,10},{10,1... | collective-permute-start | bytes 1179656 | tf_op jit(solution)/shard_map/ppermute | solution.py:259
  70.5 12.6 %collective-permute-start.10 = (bf16[512,384]{1,0:T(8,128)(2,1)}, bf16[512,384]{1,0:T(8,128)(2,1)}, u32[]{:S(2)}, u32[]{:S(2)}) collective-permute-start(bf16[512,384]{1,0:T(8,128)(2,1)} %slice_bitcast_fusion), channel_id=1, source_target_pairs={{0,3},{1,0},{2,1},{3,2},{4,7},{5,4},{6,5},{7,6},{8,11},{9,8},{10,9... | collective-permute-start | bytes 1179656 | tf_op jit(solution)/shard_map/ppermute | solution.py:262
  76.4 6.8 %copy-start.8 = (bf16[1,96,1920]{2,1,0:T(8,128)(2,1)}, bf16[1,96,1920]{2,1,0:T(8,128)(2,1)S(1)}, u32[]{:S(2)}) copy-start(bf16[1,96,1920]{2,1,0:T(8,128)(2,1)S(1)} %collective-permute-done.12.refs_6_) | copy-start | bytes 1105924
  77.1 13.7 %collective-permute-start.13 = (bf16[1,48,1920]{2,1,0:T(8,128)(2,1)}, bf16[1,48,1920]{2,1,0:T(8,128)(2,1)}, u32[]{:S(2)}, u32[]{:S(2)}) collective-permute-start(bf16[1,48,1920]{2,1,0:T(8,128)(2,1)} %slice.24), channel_id=1, source_target_pairs={{0,16},{16,32},{32,48},{48,64},{64,80},{80,96},{96,112},{112,0},{1... | collective-permute-start | bytes 552968 | tf_op jit(solution)/shard_map/ppermute | solution.py:259
  78.9 11.9 %collective-permute-start.15 = (bf16[1,48,1920]{2,1,0:T(8,128)(2,1)}, bf16[1,48,1920]{2,1,0:T(8,128)(2,1)}, u32[]{:S(2)}, u32[]{:S(2)}) collective-permute-start(bf16[1,48,1920]{2,1,0:T(8,128)(2,1)} %slice.25), channel_id=1, source_target_pairs={{0,112},{16,0},{32,16},{48,32},{64,48},{80,64},{96,80},{112,96},{1... | collective-permute-start | bytes 552968 | tf_op jit(solution)/shard_map/ppermute | solution.py:262
  86.4 17.4 %copy-start.9 = (bf16[1,96,1920]{2,1,0:T(8,128)(2,1)S(1)}, bf16[1,96,1920]{2,1,0:T(8,128)(2,1)}, u32[]{:S(2)}) copy-start(bf16[1,96,1920]{2,1,0:T(8,128)(2,1)} %copy-done.8) | copy-start | bytes 1105924
  86.4 17.4 %copy-start.12 = (bf16[1,96,1920]{2,1,0:T(8,128)(2,1)S(1)}, bf16[1,96,1920]{2,1,0:T(8,128)(2,1)}, u32[]{:S(2)}) copy-start(bf16[1,96,1920]{2,1,0:T(8,128)(2,1)} %copy-done.11) | copy-start | bytes 1105924
  90.8 20.6 %copy-start.6 = (bf16[3,96,1920]{2,1,0:T(8,128)(2,1)S(1)}, bf16[3,96,1920]{2,1,0:T(8,128)(2,1)}, u32[]{:S(2)}) copy-start(bf16[3,96,1920]{2,1,0:T(8,128)(2,1)} %copy-done.5) | copy-start | bytes 3317764
  90.8 24.3 %copy-start.23 = (f32[3,128]{1,0:T(4,128)S(1)}, f32[3,128]{1,0:T(4,128)}, u32[]{:S(2)}) copy-start(f32[3,128]{1,0:T(4,128)} %q_gain_ref.1) | copy-start | bytes 4612
  90.8 24.3 %copy-start.24 = (f32[3,128]{1,0:T(4,128)S(1)}, f32[3,128]{1,0:T(4,128)}, u32[]{:S(2)}) copy-start(f32[3,128]{1,0:T(4,128)} %k_gain_ref.1) | copy-start | bytes 4612
  102.7 4.8 %collective-permute-start.16 = (bf16[3,768,384]{2,1,0:T(8,128)(2,1)}, bf16[3,768,384]{2,1,0:T(8,128)(2,1)S(1)}, u32[]{:S(2)}, u32[]{:S(2)}) collective-permute-start(bf16[3,768,384]{2,1,0:T(8,128)(2,1)} %collective-permute-done.11.near_ref), channel_id=1, source_target_pairs={{0,8},{8,0},{1,9},{9,1},{2,10},{10,2},{3,11},{11,3},{4,12},{12,4},... | collective-permute-start | bytes 5308424 | tf_op jit(solution)/shard_map/ppermute | solution.py:301
  108.8 27.4 %collective-permute-start.19 = (bf16[3,96,1920]{2,1,0:T(8,128)(2,1)}, bf16[3,96,1920]{2,1,0:T(8,128)(2,1)}, u32[]{:S(2)}, u32[]{:S(2)}) collective-permute-start(bf16[3,96,1920]{2,1,0:T(8,128)(2,1)} %pad_maximum_fusion.1), channel_id=1, source_target_pairs={{0,128},{128,0},{1,129},{129,1},{2,130},{130,2},{3,131},{131,3},{4... | collective-permute-start | bytes 3317768 | tf_op jit(solution)/shard_map/ppermute | solution.py:119
  112.3 19.3 %collective-permute-start.17 = (bf16[1,96,1920]{2,1,0:T(8,128)(2,1)}, bf16[1,96,1920]{2,1,0:T(8,128)(2,1)}, u32[]{:S(2)}, u32[]{:S(2)}) collective-permute-start(bf16[1,96,1920]{2,1,0:T(8,128)(2,1)} %get-tuple-element.57), channel_id=1, source_target_pairs={{0,16},{16,32},{32,48},{48,64},{64,80},{80,96},{96,112},{112,0},{1... | collective-permute-start | bytes 1105928 | tf_op jit(solution)/shard_map/ppermute | solution.py:259
  112.6 19.0 %collective-permute-start.18 = (bf16[1,96,1920]{2,1,0:T(8,128)(2,1)}, bf16[1,96,1920]{2,1,0:T(8,128)(2,1)}, u32[]{:S(2)}, u32[]{:S(2)}) collective-permute-start(bf16[1,96,1920]{2,1,0:T(8,128)(2,1)} %get-tuple-element.58), channel_id=1, source_target_pairs={{0,112},{16,0},{32,16},{48,32},{64,48},{80,64},{96,80},{112,96},{1... | collective-permute-start | bytes 1105928 | tf_op jit(solution)/shard_map/ppermute | solution.py:262
  118.6 8.5 %copy-start.7 = (bf16[3,96,1920]{2,1,0:T(8,128)(2,1)S(1)}, bf16[3,96,1920]{2,1,0:T(8,128)(2,1)}, u32[]{:S(2)}) copy-start(bf16[3,96,1920]{2,1,0:T(8,128)(2,1)} %copy-done.5) | copy-start | bytes 3317764
  118.6 8.5 %copy-start.10 = (bf16[1,96,1920]{2,1,0:T(8,128)(2,1)S(1)}, bf16[1,96,1920]{2,1,0:T(8,128)(2,1)}, u32[]{:S(2)}) copy-start(bf16[1,96,1920]{2,1,0:T(8,128)(2,1)} %copy-done.8) | copy-start | bytes 1105924
  118.6 8.5 %copy-start.13 = (bf16[1,96,1920]{2,1,0:T(8,128)(2,1)S(1)}, bf16[1,96,1920]{2,1,0:T(8,128)(2,1)}, u32[]{:S(2)}) copy-start(bf16[1,96,1920]{2,1,0:T(8,128)(2,1)} %copy-done.11) | copy-start | bytes 1105924
  118.6 8.5 %copy-start.19 = (bf16[1,96,1920]{2,1,0:T(8,128)(2,1)S(1)}, bf16[1,96,1920]{2,1,0:T(8,128)(2,1)}, u32[]{:S(2)}) copy-start(bf16[1,96,1920]{2,1,0:T(8,128)(2,1)} %copy-done.18) | copy-start | bytes 1105924
  144.8 9.0 %collective-permute-start.24 = (bf16[512,1536]{1,0:T(8,128)(2,1)}, bf16[512,1536]{1,0:T(8,128)(2,1)S(1)}, u32[]{:S(2)}, u32[]{:S(2)}) collective-permute-start(bf16[512,1536]{1,0:T(8,128)(2,1)} %shard_map.85.activated_ref), channel_id=1, source_target_pairs={{0,8},{8,0},{1,9},{9,1},{2,10},{10,2},{3,11},{11,3},{4,12},{12,4},... | collective-permute-start | bytes 4718600 | tf_op jit(solution)/shard_map/ppermute | solution.py:316
  146.0 7.8 %collective-permute-start.23 = (bf16[512,384]{1,0:T(8,128)(2,1)}, bf16[512,384]{1,0:T(8,128)(2,1)S(1)}, u32[]{:S(2)}, u32[]{:S(2)}) collective-permute-start(bf16[512,384]{1,0:T(8,128)(2,1)} %shard_map.83.attended_ref), channel_id=1, source_target_pairs={{0,8},{8,0},{1,9},{9,1},{2,10},{10,2},{3,11},{11,3},{4,12},{12,4},... | collective-permute-start | bytes 1179656 | tf_op jit(solution)/shard_map/ppermute | solution.py:316
  158.9 22.7 %collective-permute-start.25 = (bf16[4,192,512]{2,1,0:T(8,128)(2,1)S(1)}, bf16[4,192,512]{2,1,0:T(8,128)(2,1)}, u32[]{:S(2)}, u32[]{:S(2)}) collective-permute-start(bf16[4,192,512]{2,1,0:T(8,128)(2,1)S(1)} %get-tuple-element.76), channel_id=1, source_target_pairs={{0,8},{8,0},{1,9},{9,1},{2,10},{10,2},{3,11},{11,3},{4,12},{12,4},... | collective-permute-start | bytes 2359304 | tf_op jit(solution)/shard_map/ppermute | solution.py:99
  159.5 22.1 %collective-permute-start.26 = (bf16[4,192,512]{2,1,0:T(8,128)(2,1)S(1)}, bf16[4,192,512]{2,1,0:T(8,128)(2,1)}, u32[]{:S(2)}, u32[]{:S(2)}) collective-permute-start(bf16[4,192,512]{2,1,0:T(8,128)(2,1)S(1)} %get-tuple-element.75), channel_id=1, source_target_pairs={{0,12},{4,8},{8,4},{12,0},{1,13},{5,9},{9,5},{13,1},{2,14},{6,10},... | collective-permute-start | bytes 2359304 | tf_op jit(solution)/shard_map/ppermute | solution.py:98
  160.6 11.9 %collective-permute-start.20 = (bf16[2,192,512]{2,1,0:T(8,128)(2,1)S(1)}, bf16[2,192,512]{2,1,0:T(8,128)(2,1)S(1)}, u32[]{:S(2)}, u32[]{:S(2)}) collective-permute-start(bf16[2,192,512]{2,1,0:T(8,128)(2,1)S(1)} %get-tuple-element.79), channel_id=1, source_target_pairs={{0,2},{1,3},{2,0},{3,1},{4,6},{5,7},{6,4},{7,5},{8,10},{9,11},{10,... | collective-permute-start | bytes 1179656 | tf_op jit(solution)/shard_map/ppermute | solution.py:88
  163.5 18.1 %collective-permute-start.21 = (bf16[2,192,512]{2,1,0:T(8,128)(2,1)S(1)}, bf16[2,192,512]{2,1,0:T(8,128)(2,1)S(1)}, u32[]{:S(2)}, u32[]{:S(2)}) collective-permute-start(bf16[2,192,512]{2,1,0:T(8,128)(2,1)S(1)} %get-tuple-element.78), channel_id=1, source_target_pairs={{0,1},{1,2},{2,3},{3,0},{4,5},{5,6},{6,7},{7,4},{8,9},{9,10},{10,1... | collective-permute-start | bytes 1179656 | tf_op jit(solution)/shard_map/ppermute | solution.py:88
  163.9 17.7 %collective-permute-start.22 = (bf16[2,192,512]{2,1,0:T(8,128)(2,1)S(1)}, bf16[2,192,512]{2,1,0:T(8,128)(2,1)S(1)}, u32[]{:S(2)}, u32[]{:S(2)}) collective-permute-start(bf16[2,192,512]{2,1,0:T(8,128)(2,1)S(1)} %get-tuple-element.77), channel_id=1, source_target_pairs={{0,3},{1,0},{2,1},{3,2},{4,7},{5,4},{6,5},{7,6},{8,11},{9,8},{10,9... | collective-permute-start | bytes 1179656 | tf_op jit(solution)/shard_map/ppermute | solution.py:88
  184.9 5.9 %collective-permute-start.27 = (bf16[192,512]{1,0:T(8,128)(2,1)}, bf16[192,512]{1,0:T(8,128)(2,1)}, u32[]{:S(2)}, u32[]{:S(2)}) collective-permute-start(bf16[192,512]{1,0:T(8,128)(2,1)} %fusion.5), channel_id=1, source_target_pairs={{0,4},{4,0},{1,5},{5,1},{2,6},{6,2},{3,7},{7,3},{8,12},{12,8},{9,1... | collective-permute-start | bytes 589832 | tf_op jit(solution)/shard_map/ppermute | solution.py:114
  185.4 6.4 %collective-permute-start.30 = (bf16[192,512]{1,0:T(8,128)(2,1)}, bf16[192,512]{1,0:T(8,128)(2,1)}, u32[]{:S(2)}, u32[]{:S(2)}) collective-permute-start(bf16[192,512]{1,0:T(8,128)(2,1)} %get-tuple-element.84), channel_id=1, source_target_pairs={{0,3},{1,0},{2,1},{3,2},{4,7},{5,4},{6,5},{7,6},{8,11},{9,8},{10,9... | collective-permute-start | bytes 589832 | tf_op jit(solution)/shard_map/ppermute | solution.py:88
  188.1 7.9 %collective-permute-start.29 = (bf16[192,512]{1,0:T(8,128)(2,1)S(1)}, bf16[192,512]{1,0:T(8,128)(2,1)}, u32[]{:S(2)}, u32[]{:S(2)}) collective-permute-start(bf16[192,512]{1,0:T(8,128)(2,1)S(1)} %get-tuple-element.85), channel_id=1, source_target_pairs={{0,1},{1,2},{2,3},{3,0},{4,5},{5,6},{6,7},{7,4},{8,9},{9,10},{10,1... | collective-permute-start | bytes 589832 | tf_op jit(solution)/shard_map/ppermute | solution.py:88
  188.1 9.7 %collective-permute-start.28 = (bf16[192,512]{1,0:T(8,128)(2,1)S(1)}, bf16[192,512]{1,0:T(8,128)(2,1)}, u32[]{:S(2)}, u32[]{:S(2)}) collective-permute-start(bf16[192,512]{1,0:T(8,128)(2,1)S(1)} %get-tuple-element.83), channel_id=1, source_target_pairs={{0,2},{1,3},{2,0},{3,1},{4,6},{5,7},{6,4},{7,5},{8,10},{9,11},{10,... | collective-permute-start | bytes 589832 | tf_op jit(solution)/shard_map/ppermute | solution.py:88
  (12 other events, 26.1 us)
Sparse Core Ops, SparseCore 0:
  9.2 48.6 all-gather.2
  59.8 73.1 all-gather.4

commit v4 on v3

--- a/solution.py
+++ b/solution.py
@@ -82,26 +82,29 @@
     return lax.dynamic_index_in_dim(blocks, at, axis, keepdims=False)
 
 
-def to_peers_x(blocks, axis):
+def to_peers_x(blocks, axis, hop=0):
     x = lax.axis_index("x")
-    return [
-        lax.ppermute(pick(blocks, (x + k) % 4, axis), "x", shift(4, k)) for k in (2, 1, 3)
-    ]
+    arrived = []
+    for k in (2, 1, 3):
+        perm = [
+            (core * 4 + at, (core ^ hop) * 4 + (at + k) % 4) for core in range(2) for at in range(4)
+        ]
+        arrived.append(lax.ppermute(pick(blocks, (x + k) % 4, axis), ("c", "x"), perm))
+    return arrived
 
 
 def scatter_start(mine, theirs):
     yl, x = lax.axis_index("yl"), lax.axis_index("x")
     shape = (2, 4, mine.shape[0] // 8 * mine.shape[1], mine.shape[2])
     mine, theirs = mine.reshape(shape), theirs.reshape(shape)
-    over_x = to_peers_x(mine, 1)
-    both = [(core * 2 + at, (1 - core) * 2 + 1 - at) for core in range(2) for at in range(2)]
-    over_y = lax.ppermute(pick(theirs, 1 - yl, 0), ("c", "yl"), both)
-    kept = lax.ppermute(pick(theirs, yl, 0), "c", SWAP)
-    over_x = tie(over_x, kept)
-    return [pick(mine, x, 1)] + over_x, [kept, over_y]
-
-
-def scatter_end(over_x, over_y):
+    over_y = lax.ppermute(pick(mine, 1 - yl, 0), "yl", SWAP)
+    kept = lax.ppermute(pick(theirs, x, 1), "c", SWAP)
+    over_x = to_peers_x(theirs, 1, 1)
+    over_y = tie(over_y, kept)
+    return [pick(mine, yl, 0), over_y], [kept] + over_x
+
+
+def scatter_end(over_y, over_x):
     yl, x = lax.axis_index("yl"), lax.axis_index("x")
 
     def total(values):
@@ -112,7 +115,7 @@
     others = to_peers_x(rounded, 0)
     by_y = total(tie(over_x, rounded))
     other = lax.ppermute(pick(by_y, 1 - yl, 0).astype(jnp.bfloat16), "yl", SWAP)
-    return total([pick(by_y, yl, 0), other]), total([pick(by_x, x, 0)] + others)
+    return total([pick(by_x, x, 0)] + others), total([pick(by_y, yl, 0), other])
 
 
 def across(v):

time: 209 us -> 206 us (0.986)
  waiting for transfers between devices: 74.9 us -> 66.8 us
  local copies, waits for them, and re-layouts: 24 us -> 28.9 us
  starting transfers between devices: 50 us -> 52.3 us
    ppermute x8, waiting for transfers between devices: 22.4 us -> 15.1 us  [the longest x6 11.9 us: to_peers_x(): lax.ppermute(pick(blocks, (x + k) % 4, axis), ('c', 'x'), perm)]
    unnamed x55 -> x63, local copies, waits for them, and re-layouts: 13.2 us -> 17.1 us
    ppermute x8, starting transfers between devices: 11.1 us -> 13.2 us  [the longest x6 11.5 us: to_peers_x(): lax.ppermute(pick(blocks, (x + k) % 4, axis), ('c', 'x'), perm)]
  transfers between devices with their start and end apart: 33 -> 33, of which waited for: 15 -> 14; matrix products, arithmetic and copies ran while one was open for 8% -> 10% of each run, Pallas kernels for 10% -> 12%
where the time goes in v4:
time: 206 us; the launch traced here: 205 us
  waiting for transfers between devices  66.8 us (32%)
  starting transfers between devices  52.3 us (25%)
  Pallas kernels  32.7 us (16%)
  local copies, waits for them, and re-layouts  28.9 us (14%)
  between operations  13.8 us (7%)
  other arithmetic  11 us (5%)
    ppermute x4, waiting for transfers between devices, across(): return lax.ppermute(v, 'yh', SWAP)  24.9 us
    ppermute x7, starting transfers between devices, down(): return lax.ppermute(v, axis, shift(size, -1))  20.4 us
    ppermute x7, waiting for transfers between devices, up(): return lax.ppermute(v, axis, shift(size, 1))  20.2 us
    unnamed x63, local copies, waits for them, and re-layouts  17.1 us
    ppermute x6, waiting for transfers between devices, to_peers_x(): lax.ppermute(pick(blocks, (x + k) % 4, axis), ('c', 'x'), perm)  11.9 us
    ppermute x6, starting transfers between devices, to_peers_x(): lax.ppermute(pick(blocks, (x + k) % 4, axis), ('c', 'x'), perm)  11.5 us
    pallas_call x2, Pallas kernels, out_terms(): pl.pallas_call(functools.partial(out_kernel, slots), in_specs=[pl.BlockSp...  10.3 us
    ppermute x4, starting transfers between devices, across(): return lax.ppermute(v, 'yh', SWAP)  8.7 us
  transfers between devices with their start and end apart: 33, of which 14 were waited for; matrix products, arithmetic and copies ran while one was open for 10% of the time, Pallas kernels for 12%

profile of v4, /device:TPU:1, one launch (start us, length us, event | category | flops | bytes accessed | tf_op | source)
XLA Modules:
  0.0 205.4 jit_solution(8744283171476430624)
XLA Ops:
  7.3 2.2 %collective-permute-start = (bf16[512,384]{1,0:T(8,128)(2,1)}, bf16[512,384]{1,0:T(8,128)(2,1)S(1)}, u32[]{:S(2)}, u32[]{:S(2)}) collective-permute-start(bf16[512,384]{1,0:T(8,128)(2,1)} %param.8), channel_id=1, source_target_pairs={{0,4},{4,0},{1,5},{5,1},{2,6},{6,2},{3,7},{7,3},{8,12},{12,8},{9,1... | collective-permute-start | bytes 1179656 | tf_op jit(solution)/shard_map/ppermute | solution.py:273
  10.5 1.7 collective-permute-start.2
  12.2 4.0 %collective-permute-start.3 = (bf16[1,96,1920]{2,1,0:T(8,128)(2,1)S(1)}, bf16[1,96,1920]{2,1,0:T(8,128)(2,1)}, u32[]{:S(2)}, u32[]{:S(2)}) collective-permute-start(bf16[1,96,1920]{2,1,0:T(8,128)(2,1)S(1)} %maximum_bitcast_fusion.refs_0_), channel_id=1, source_target_pairs={{0,112},{16,0},{32,16},{48,32},{64,48},{80,64},{96,80},{112,96},{1... | collective-permute-start | bytes 1105928 | tf_op jit(solution)/shard_map/ppermute | solution.py:265
  16.3 2.6 %collective-permute-start.1 = (bf16[96,1536]{1,0:T(8,128)(2,1)}, bf16[96,1536]{1,0:T(8,128)(2,1)S(1)}, u32[]{:S(2)}, u32[]{:S(2)}) collective-permute-start(bf16[96,1536]{1,0:T(8,128)(2,1)} %param.11), channel_id=1, source_target_pairs={{0,128},{128,0},{1,129},{129,1},{2,130},{130,2},{3,131},{131,3},{4... | collective-permute-start | bytes 884744 | tf_op jit(solution)/shard_map/ppermute | solution.py:122
  18.9 8.3 %collective-permute-done.1 = bf16[96,1536]{1,0:T(8,128)(2,1)S(1)} collective-permute-done((bf16[96,1536]{1,0:T(8,128)(2,1)}, bf16[96,1536]{1,0:T(8,128)(2,1)S(1)}, u32[]{:S(2)}, u32[]{:S(2)}) %collective-permute-start.1) | collective-permute-done | bytes 294944 | tf_op jit(solution)/shard_map/ppermute | solution.py:122
  27.2 2.1 %maximum_select_fusion = bf16[2,96,1536]{2,1,0:T(8,128)(2,1)} fusion(bf16[1,96,1536]{2,1,0:T(8,128)(2,1)S(1)} %bitcast.80, bf16[1,96,1536]{2,1,0:T(8,128)(2,1)} %bitcast.79, pred[]{:T(512)S(6)} %eq.20), kind=kLoop, calls=%fused_computation.9 | loop fusion | flops 884736 | bytes 1179649 | tf_op jit(solution)/shard_map/jit(_where)/select_n | solution.py:78
  29.3 2.2 %pad_maximum_fusion = bf16[3,96,1920]{2,1,0:T(8,128)(2,1)} fusion(bf16[1,96,1920]{2,1,0:T(8,128)(2,1)} %collective-permute-done.3.refs_2_, bf16[1,96,1920]{2,1,0:T(8,128)(2,1)S(1)} %maximum_bitcast_fusion.refs_0_, bf16[1,96,1920]{2,1,0:T(8,128)(2,1)S(1)} %collective-permute-done.2.refs_1_), kind=kLoop, calls=%fused_computation.1 | loop fusion | flops 1105920 | bytes 2211840 | tf_op jit(solution)/shard_map/concatenate | solution.py:283
  33.7 1.5 collective-permute-start.5
  35.2 1.3 collective-permute-start.7
  36.5 4.1 %collective-permute-start.8 = (bf16[1,96,1920]{2,1,0:T(8,128)(2,1)}, bf16[1,96,1920]{2,1,0:T(8,128)(2,1)}, u32[]{:S(2)}, u32[]{:S(2)}) collective-permute-start(bf16[1,96,1920]{2,1,0:T(8,128)(2,1)} %collective-permute-done.3.refs_2_), channel_id=1, source_target_pairs={{0,112},{16,0},{32,16},{48,32},{64,48},{80,64},{96,80},{112,96},{1... | collective-permute-start | bytes 1105928 | tf_op jit(solution)/shard_map/ppermute | solution.py:265
  40.5 14.1 %collective-permute-done.7.refs_3_ = bf16[1,96,1920]{2,1,0:T(8,128)(2,1)} collective-permute-done((bf16[1,96,1920]{2,1,0:T(8,128)(2,1)S(1)}, bf16[1,96,1920]{2,1,0:T(8,128)(2,1)}, u32[]{:S(2)}, u32[]{:S(2)}) %collective-permute-start.7) | collective-permute-done | bytes 368672 | tf_op jit(solution)/shard_map/ppermute | solution.py:262
  54.7 3.3 %all-gather.3.cloned.1.call-done.own_ref = bf16[3,1536,384]{2,1,0:T(8,128)(2,1)} async-done(((bf16[3,96,384]{2,1,0:T(8,128)(2,1)}), bf16[3,1536,384]{2,1,0:T(8,128)(2,1)}) %all-gather.3.cloned.1.call-update) | async-done | bytes 3538960 | tf_op jit(solution)/shard_map/all_gather | solution.py:267
  57.9 2.9 %constant_dynamic-slice_fusion = bf16[3,768,384]{2,1,0:T(8,128)(2,1)} fusion(bf16[3,1536,384]{2,1,0:T(8,128)(2,1)} %all-gather.3.cloned.1.call-done.own_ref, s32[]{:T(128)S(6)} %select_n.111), kind=kLoop, calls=%fused_computation.30 | loop fusion | bytes 3538948 | tf_op jit(solution)/shard_map/dynamic_slice | solution.py:285
  60.9 2.8 %collective-permute-start.11 = (bf16[3,768,384]{2,1,0:T(8,128)(2,1)}, bf16[3,768,384]{2,1,0:T(8,128)(2,1)}, u32[]{:S(2)}, u32[]{:S(2)}) collective-permute-start(bf16[3,768,384]{2,1,0:T(8,128)(2,1)} %constant_dynamic-slice_fusion), channel_id=1, source_target_pairs={{0,128},{128,0},{1,129},{129,1},{2,130},{130,2},{3,131},{131,3},{4... | collective-permute-start | bytes 5308424 | tf_op jit(solution)/shard_map/ppermute | solution.py:122
  64.0 2.4 %collective-permute-start.14 = (bf16[1,96,1920]{2,1,0:T(8,128)(2,1)}, bf16[1,96,1920]{2,1,0:T(8,128)(2,1)S(1)}, u32[]{:S(2)}, u32[]{:S(2)}) collective-permute-start(bf16[1,96,1920]{2,1,0:T(8,128)(2,1)} %collective-permute-done.8.refs_4_), channel_id=1, source_target_pairs={{0,112},{16,0},{32,16},{48,32},{64,48},{80,64},{96,80},{112,96},{1... | collective-permute-start | bytes 1105928 | tf_op jit(solution)/shard_map/ppermute | solution.py:265
  66.4 1.8 slice_bitcast_fusion
  68.2 2.6 %collective-permute-start.10 = (bf16[512,384]{1,0:T(8,128)(2,1)}, bf16[512,384]{1,0:T(8,128)(2,1)S(1)}, u32[]{:S(2)}, u32[]{:S(2)}) collective-permute-start(bf16[512,384]{1,0:T(8,128)(2,1)} %slice_bitcast_fusion), channel_id=1, source_target_pairs={{0,3},{1,0},{2,1},{3,2},{4,7},{5,4},{6,5},{7,6},{8,11},{9,8},{10,9... | collective-permute-start | bytes 1179656 | tf_op jit(solution)/shard_map/ppermute | solution.py:265
  71.6 4.7 %collective-permute-done.12.refs_6_ = bf16[1,96,1920]{2,1,0:T(8,128)(2,1)S(1)} collective-permute-done((bf16[1,96,1920]{2,1,0:T(8,128)(2,1)}, bf16[1,96,1920]{2,1,0:T(8,128)(2,1)S(1)}, u32[]{:S(2)}, u32[]{:S(2)}) %collective-permute-start.12) | collective-permute-done | bytes 368672 | tf_op jit(solution)/shard_map/ppermute | solution.py:262
  78.9 3.4 %collective-permute-start.15 = (bf16[1,48,1920]{2,1,0:T(8,128)(2,1)}, bf16[1,48,1920]{2,1,0:T(8,128)(2,1)}, u32[]{:S(2)}, u32[]{:S(2)}) collective-permute-start(bf16[1,48,1920]{2,1,0:T(8,128)(2,1)} %slice.25), channel_id=1, source_target_pairs={{0,112},{16,0},{32,16},{48,32},{64,48},{80,64},{96,80},{112,96},{1... | collective-permute-start | bytes 552968 | tf_op jit(solution)/shard_map/ppermute | solution.py:265
  86.4 4.3 %shard_map.82.x_ref = bf16[512,3072]{1,0:T(8,128)(2,1)S(1)} custom-call(s32[1]{0:T(128)} %bitcast.8.x_ref, f32[1,3072]{1,0:T(1,128)S(1)} %bitcast.74, bf16[2,512,384]{2,1,0:T(8,128)(2,1)S(1)} %copy-done.5, bf16[2,512,384]{2,1,0:T(8,128)(2,1)S(1)} %copy-done.18, bf16[2,512,384]{2,1,0:T(8,128)(2,1)} %collective-permute-done.5.left_ref, ...), custom_call_target="tpu_custom_call" | custom-call | tf_op jit(solution)/shard_map/pallas_call | solution.py:58
  90.8 11.9 %collective-permute-done.11.near_ref = bf16[3,768,384]{2,1,0:T(8,128)(2,1)} collective-permute-done((bf16[3,768,384]{2,1,0:T(8,128)(2,1)}, bf16[3,768,384]{2,1,0:T(8,128)(2,1)}, u32[]{:S(2)}, u32[]{:S(2)}) %collective-permute-start.11) | collective-permute-done | bytes 1769504 | tf_op jit(solution)/shard_map/ppermute | solution.py:122
  103.8 2.2 %pad_maximum_fusion.1 = bf16[3,96,1920]{2,1,0:T(8,128)(2,1)} fusion(bf16[1,96,1920]{2,1,0:T(8,128)(2,1)S(1)} %copy-done.13, bf16[1,48,1920]{2,1,0:T(8,128)(2,1)} %collective-permute-done.15.refs_9_, bf16[1,48,1920]{2,1,0:T(8,128)(2,1)} %collective-permute-done.13.refs_8_, bf16[1,96,1920]{2,1,0:T(8,128)(2,1)S(1)} %copy-done.10), kind=kLoop, calls=%fused_computation.2 | loop fusion | flops 4423680 | bytes 2211840 | tf_op jit(solution)/shard_map/concatenate | solution.py:308
  106.0 1.5 collective-permute-done.16.far_ref
  107.5 1.3 copy-done.15
  108.8 2.6 %collective-permute-start.19 = (bf16[3,96,1920]{2,1,0:T(8,128)(2,1)}, bf16[3,96,1920]{2,1,0:T(8,128)(2,1)}, u32[]{:S(2)}, u32[]{:S(2)}) collective-permute-start(bf16[3,96,1920]{2,1,0:T(8,128)(2,1)} %pad_maximum_fusion.1), channel_id=1, source_target_pairs={{0,128},{128,0},{1,129},{129,1},{2,130},{130,2},{3,131},{131,3},{4... | collective-permute-start | bytes 3317768 | tf_op jit(solution)/shard_map/ppermute | solution.py:122
  112.6 2.4 %collective-permute-start.18 = (bf16[1,96,1920]{2,1,0:T(8,128)(2,1)}, bf16[1,96,1920]{2,1,0:T(8,128)(2,1)}, u32[]{:S(2)}, u32[]{:S(2)}) collective-permute-start(bf16[1,96,1920]{2,1,0:T(8,128)(2,1)} %get-tuple-element.56), channel_id=1, source_target_pairs={{0,112},{16,0},{32,16},{48,32},{64,48},{80,64},{96,80},{112,96},{1... | collective-permute-start | bytes 1105928 | tf_op jit(solution)/shard_map/ppermute | solution.py:265
  115.1 2.0 copy-done.3
  117.1 1.5 copy-done.16
  118.6 7.7 %shard_map.83.attended_ref = bf16[512,384]{1,0:T(8,128)(2,1)S(1)} custom-call(s32[3]{0:T(128)S(1)} %pad_add_fusion.1.starts_ref, bf16[512,3072]{1,0:T(8,128)(2,1)S(1)} %shard_map.82.x_ref, bf16[3,1536,384]{2,1,0:T(8,128)(2,1)S(1)} %copy-done.3, bf16[3,768,384]{2,1,0:T(8,128)(2,1)} %collective-permute-done.11.near_ref, bf16[3,768,384]{2,1,0:T(8,128)(2,1)S(1)} %copy-done.16, ...), custom_call_target="tpu_custom_call" | custom-call | tf_op jit(solution)/shard_map/pallas_call | solution.py:184
  126.4 1.8 shard_map.84.weights_ref
  128.2 2.0 copy-done
  130.2 1.4 collective-permute-done.17.low_ref
  131.6 4.7 %collective-permute-done.19.distant_ref = bf16[3,96,1920]{2,1,0:T(8,128)(2,1)} collective-permute-done((bf16[3,96,1920]{2,1,0:T(8,128)(2,1)}, bf16[3,96,1920]{2,1,0:T(8,128)(2,1)}, u32[]{:S(2)}, u32[]{:S(2)}) %collective-permute-start.19) | collective-permute-done | bytes 1105952 | tf_op jit(solution)/shard_map/ppermute | solution.py:122
  136.3 8.5 %shard_map.85.activated_ref = bf16[512,1536]{1,0:T(8,128)(2,1)} custom-call(bf16[512,3072]{1,0:T(8,128)(2,1)S(1)} %shard_map.82.x_ref, bf16[3072,1536]{1,0:T(8,128)(2,1)} %bitcast.75), custom_call_target="tpu_custom_call" | custom-call | tf_op jit(solution)/shard_map/pallas_call | solution.py:134
  146.1 2.1 %copy-done.1 = bf16[1056,1920]{1,0:T(8,128)(2,1)S(1)} copy-done((bf16[1056,1920]{1,0:T(8,128)(2,1)S(1)}, bf16[1056,1920]{1,0:T(8,128)(2,1)}, u32[]{:S(2)}) %copy-start.1) | copy-done | bytes 4055064
  149.2 5.4 %shard_map.86 = bf16[16,96,512]{2,1,0:T(8,128)(2,1)S(1)} custom-call(s32[2]{0:T(128)S(1)} %pad_add_fusion.at_ref, bf16[1056,1920]{1,0:T(8,128)(2,1)S(1)} %copy-done.1, bf16[1,96,1920]{2,1,0:T(8,128)(2,1)} %collective-permute-done.17.low_ref, bf16[1,96,1920]{2,1,0:T(8,128)(2,1)} %collective-permute-done.18.high_ref, ...), custom_call_target="tpu_custom_call" | custom-call | tf_op jit(solution)/shard_map/pallas_call | solution.py:247
  156.6 2.1 %copy-done.2 = bf16[1056,1920]{1,0:T(8,128)(2,1)S(1)} copy-done((bf16[1056,1920]{1,0:T(8,128)(2,1)S(1)}, bf16[1056,1920]{1,0:T(8,128)(2,1)}, u32[]{:S(2)}) %copy-start.2) | copy-done | bytes 4055064
  158.7 4.9 %shard_map.87 = bf16[16,96,512]{2,1,0:T(8,128)(2,1)S(1)} custom-call(s32[2]{0:T(128)S(1)} %pad_add_fusion.at_ref, bf16[1056,1920]{1,0:T(8,128)(2,1)S(1)} %copy-done.2, bf16[1,96,1920]{2,1,0:T(8,128)(2,1)} %collective-permute-done.17.low_ref, bf16[1,96,1920]{2,1,0:T(8,128)(2,1)} %collective-permute-done.18.high_ref, ...), custom_call_target="tpu_custom_call" | custom-call | tf_op jit(solution)/shard_map/pallas_call | solution.py:247
  165.5 2.9 %collective-permute-start.27 = (bf16[2,192,512]{2,1,0:T(8,128)(2,1)}, bf16[2,192,512]{2,1,0:T(8,128)(2,1)S(1)}, u32[]{:S(2)}, u32[]{:S(2)}) collective-permute-start(bf16[2,192,512]{2,1,0:T(8,128)(2,1)} %get-tuple-element.73), channel_id=1, source_target_pairs={{0,10},{1,11},{2,8},{3,9},{8,2},{9,3},{10,0},{11,1},{4,14},{5,15},... | collective-permute-start | bytes 1179656 | tf_op jit(solution)/shard_map/ppermute | solution.py:92
  169.1 2.3 %collective-permute-start.29 = (bf16[2,192,512]{2,1,0:T(8,128)(2,1)}, bf16[2,192,512]{2,1,0:T(8,128)(2,1)S(1)}, u32[]{:S(2)}, u32[]{:S(2)}) collective-permute-start(bf16[2,192,512]{2,1,0:T(8,128)(2,1)} %get-tuple-element.71), channel_id=1, source_target_pairs={{0,11},{1,8},{2,9},{3,10},{8,3},{9,0},{10,1},{11,2},{4,15},{5,12},... | collective-permute-start | bytes 1179656 | tf_op jit(solution)/shard_map/ppermute | solution.py:92
  171.3 3.2 %collective-permute-done.20 = bf16[4,192,512]{2,1,0:T(8,128)(2,1)} collective-permute-done((bf16[4,192,512]{2,1,0:T(8,128)(2,1)}, bf16[4,192,512]{2,1,0:T(8,128)(2,1)}, u32[]{:S(2)}, u32[]{:S(2)}) %collective-permute-start.20) | collective-permute-done | bytes 786464 | tf_op jit(solution)/shard_map/ppermute | solution.py:100
  174.5 1.4 fusion.6
  176.8 3.0 %collective-permute-start.24 = (bf16[192,512]{1,0:T(8,128)(2,1)}, bf16[192,512]{1,0:T(8,128)(2,1)}, u32[]{:S(2)}, u32[]{:S(2)}) collective-permute-start(bf16[192,512]{1,0:T(8,128)(2,1)} %get-tuple-element.77), channel_id=1, source_target_pairs={{0,2},{1,3},{2,0},{3,1},{8,10},{9,11},{10,8},{11,9},{4,6},{5,7},{6... | collective-permute-start | bytes 589832 | tf_op jit(solution)/shard_map/ppermute | solution.py:92
  180.0 2.4 %collective-permute-start.26 = (bf16[192,512]{1,0:T(8,128)(2,1)}, bf16[192,512]{1,0:T(8,128)(2,1)}, u32[]{:S(2)}, u32[]{:S(2)}) collective-permute-start(bf16[192,512]{1,0:T(8,128)(2,1)} %get-tuple-element.78), channel_id=1, source_target_pairs={{0,3},{1,0},{2,1},{3,2},{8,11},{9,8},{10,9},{11,10},{4,7},{5,4},{6... | collective-permute-start | bytes 589832 | tf_op jit(solution)/shard_map/ppermute | solution.py:92
  182.4 4.8 %collective-permute-done.28 = bf16[2,192,512]{2,1,0:T(8,128)(2,1)S(1)} collective-permute-done((bf16[2,192,512]{2,1,0:T(8,128)(2,1)}, bf16[2,192,512]{2,1,0:T(8,128)(2,1)S(1)}, u32[]{:S(2)}, u32[]{:S(2)}) %collective-permute-start.28) | collective-permute-done | bytes 393248 | tf_op jit(solution)/shard_map/ppermute | solution.py:92
  188.7 2.0 collective-permute-done.24
  190.7 4.6 %collective-permute-done.25 = bf16[192,512]{1,0:T(8,128)(2,1)} collective-permute-done((bf16[192,512]{1,0:T(8,128)(2,1)}, bf16[192,512]{1,0:T(8,128)(2,1)}, u32[]{:S(2)}, u32[]{:S(2)}) %collective-permute-start.25) | collective-permute-done | bytes 196640 | tf_op jit(solution)/shard_map/ppermute | solution.py:92
  196.0 1.4 fusion.4
  (114 shorter events, 25.3 us)
Async XLA Ops:
  6.5 51.4 %all-gather.3.cloned.1.call-start = ((), (), s32[]{:S(2)}) async-start(), calls=%async_computation | async-start | bytes 3760128 | tf_op jit(solution)/shard_map/all_gather | solution.py:267
  7.3 129.0 %all-gather.5.cloned.1.call-start = ((), (), s32[]{:S(2)}) async-start(), calls=%async_computation.1 | async-start | bytes 10027008 | tf_op jit(solution)/shard_map/all_gather | solution.py:276
  7.3 19.9 %collective-permute-start = (bf16[512,384]{1,0:T(8,128)(2,1)}, bf16[512,384]{1,0:T(8,128)(2,1)S(1)}, u32[]{:S(2)}, u32[]{:S(2)}) collective-permute-start(bf16[512,384]{1,0:T(8,128)(2,1)} %param.8), channel_id=1, source_target_pairs={{0,4},{4,0},{1,5},{5,1},{2,6},{6,2},{3,7},{7,3},{8,12},{12,8},{9,1... | collective-permute-start | bytes 1179656 | tf_op jit(solution)/shard_map/ppermute | solution.py:273
  10.5 16.7 %collective-permute-start.2 = (bf16[1,96,1920]{2,1,0:T(8,128)(2,1)S(1)}, bf16[1,96,1920]{2,1,0:T(8,128)(2,1)S(1)}, u32[]{:S(2)}, u32[]{:S(2)}) collective-permute-start(bf16[1,96,1920]{2,1,0:T(8,128)(2,1)S(1)} %maximum_bitcast_fusion.refs_0_), channel_id=1, source_target_pairs={{0,16},{16,32},{32,48},{48,64},{64,80},{80,96},{96,112},{112,0},{1... | collective-permute-start | bytes 1105928 | tf_op jit(solution)/shard_map/ppermute | solution.py:262
  12.2 15.0 %collective-permute-start.3 = (bf16[1,96,1920]{2,1,0:T(8,128)(2,1)S(1)}, bf16[1,96,1920]{2,1,0:T(8,128)(2,1)}, u32[]{:S(2)}, u32[]{:S(2)}) collective-permute-start(bf16[1,96,1920]{2,1,0:T(8,128)(2,1)S(1)} %maximum_bitcast_fusion.refs_0_), channel_id=1, source_target_pairs={{0,112},{16,0},{32,16},{48,32},{64,48},{80,64},{96,80},{112,96},{1... | collective-permute-start | bytes 1105928 | tf_op jit(solution)/shard_map/ppermute | solution.py:265
  16.3 10.9 %collective-permute-start.1 = (bf16[96,1536]{1,0:T(8,128)(2,1)}, bf16[96,1536]{1,0:T(8,128)(2,1)S(1)}, u32[]{:S(2)}, u32[]{:S(2)}) collective-permute-start(bf16[96,1536]{1,0:T(8,128)(2,1)} %param.11), channel_id=1, source_target_pairs={{0,128},{128,0},{1,129},{129,1},{2,130},{130,2},{3,131},{131,3},{4... | collective-permute-start | bytes 884744 | tf_op jit(solution)/shard_map/ppermute | solution.py:122
  27.2 8.0 %copy-start.21 = (bf16[1,96,1920]{2,1,0:T(8,128)(2,1)}, bf16[1,96,1920]{2,1,0:T(8,128)(2,1)S(1)}, u32[]{:S(2)}) copy-start(bf16[1,96,1920]{2,1,0:T(8,128)(2,1)S(1)} %collective-permute-done.2.refs_1_) | copy-start | bytes 1105924
  31.5 29.3 %collective-permute-start.6 = (bf16[3,96,1920]{2,1,0:T(8,128)(2,1)}, bf16[3,96,1920]{2,1,0:T(8,128)(2,1)S(1)}, u32[]{:S(2)}, u32[]{:S(2)}) collective-permute-start(bf16[3,96,1920]{2,1,0:T(8,128)(2,1)} %pad_maximum_fusion), channel_id=1, source_target_pairs={{0,128},{128,0},{1,129},{129,1},{2,130},{130,2},{3,131},{131,3},{4... | collective-permute-start | bytes 3317768 | tf_op jit(solution)/shard_map/ppermute | solution.py:122
  32.4 28.4 %copy-start.4 = (bf16[2,512,384]{2,1,0:T(8,128)(2,1)}, bf16[2,512,384]{2,1,0:T(8,128)(2,1)S(1)}, u32[]{:S(2)}) copy-start(bf16[2,512,384]{2,1,0:T(8,128)(2,1)S(1)} %pad_maximum_fusion.2.pair_ref) | copy-start | bytes 2359300
  32.4 28.4 %collective-permute-start.4 = (bf16[2,512,384]{2,1,0:T(8,128)(2,1)S(1)}, bf16[2,512,384]{2,1,0:T(8,128)(2,1)S(1)}, u32[]{:S(2)}, u32[]{:S(2)}) collective-permute-start(bf16[2,512,384]{2,1,0:T(8,128)(2,1)S(1)} %pad_maximum_fusion.2.pair_ref), channel_id=1, source_target_pairs={{0,1},{1,2},{2,3},{3,0},{4,5},{5,6},{6,7},{7,4},{8,9},{9,10},{10,1... | collective-permute-start | bytes 2359304 | tf_op jit(solution)/shard_map/ppermute | solution.py:262
  33.7 27.1 %collective-permute-start.5 = (bf16[2,512,384]{2,1,0:T(8,128)(2,1)S(1)}, bf16[2,512,384]{2,1,0:T(8,128)(2,1)}, u32[]{:S(2)}, u32[]{:S(2)}) collective-permute-start(bf16[2,512,384]{2,1,0:T(8,128)(2,1)S(1)} %pad_maximum_fusion.2.pair_ref), channel_id=1, source_target_pairs={{0,3},{1,0},{2,1},{3,2},{4,7},{5,4},{6,5},{7,6},{8,11},{9,8},{10,9... | collective-permute-start | bytes 2359304 | tf_op jit(solution)/shard_map/ppermute | solution.py:265
  35.2 19.5 %collective-permute-start.7 = (bf16[1,96,1920]{2,1,0:T(8,128)(2,1)S(1)}, bf16[1,96,1920]{2,1,0:T(8,128)(2,1)}, u32[]{:S(2)}, u32[]{:S(2)}) collective-permute-start(bf16[1,96,1920]{2,1,0:T(8,128)(2,1)S(1)} %collective-permute-done.2.refs_1_), channel_id=1, source_target_pairs={{0,16},{16,32},{32,48},{48,64},{64,80},{80,96},{96,112},{112,0},{1... | collective-permute-start | bytes 1105928 | tf_op jit(solution)/shard_map/ppermute | solution.py:262
  36.5 18.2 %collective-permute-start.8 = (bf16[1,96,1920]{2,1,0:T(8,128)(2,1)}, bf16[1,96,1920]{2,1,0:T(8,128)(2,1)}, u32[]{:S(2)}, u32[]{:S(2)}) collective-permute-start(bf16[1,96,1920]{2,1,0:T(8,128)(2,1)} %collective-permute-done.3.refs_2_), channel_id=1, source_target_pairs={{0,112},{16,0},{32,16},{48,32},{64,48},{80,64},{96,80},{112,96},{1... | collective-permute-start | bytes 1105928 | tf_op jit(solution)/shard_map/ppermute | solution.py:265
  60.8 22.3 %copy-start.25 = (f32[3072]{0:T(1024)S(1)}, f32[3072]{0:T(1024)}, u32[]{:S(2)}) copy-start(f32[3072]{0:T(1024)} %param.9) | copy-start | bytes 36868
  60.8 22.3 %copy-start.17 = (bf16[2,512,384]{2,1,0:T(8,128)(2,1)}, bf16[2,512,384]{2,1,0:T(8,128)(2,1)S(1)}, u32[]{:S(2)}) copy-start(bf16[2,512,384]{2,1,0:T(8,128)(2,1)S(1)} %collective-permute-done.4.right_ref) | copy-start | bytes 2359300
  60.9 22.3 %copy-start.6 = (bf16[3,96,1920]{2,1,0:T(8,128)(2,1)}, bf16[3,96,1920]{2,1,0:T(8,128)(2,1)S(1)}, u32[]{:S(2)}) copy-start(bf16[3,96,1920]{2,1,0:T(8,128)(2,1)S(1)} %collective-permute-done.6.refs_5_) | copy-start | bytes 3317764
  60.9 41.8 %collective-permute-start.11 = (bf16[3,768,384]{2,1,0:T(8,128)(2,1)}, bf16[3,768,384]{2,1,0:T(8,128)(2,1)}, u32[]{:S(2)}, u32[]{:S(2)}) collective-permute-start(bf16[3,768,384]{2,1,0:T(8,128)(2,1)} %constant_dynamic-slice_fusion), channel_id=1, source_target_pairs={{0,128},{128,0},{1,129},{129,1},{2,130},{130,2},{3,131},{131,3},{4... | collective-permute-start | bytes 5308424 | tf_op jit(solution)/shard_map/ppermute | solution.py:122
  63.7 12.6 %collective-permute-start.12 = (bf16[1,96,1920]{2,1,0:T(8,128)(2,1)}, bf16[1,96,1920]{2,1,0:T(8,128)(2,1)S(1)}, u32[]{:S(2)}, u32[]{:S(2)}) collective-permute-start(bf16[1,96,1920]{2,1,0:T(8,128)(2,1)} %collective-permute-done.7.refs_3_), channel_id=1, source_target_pairs={{0,16},{16,32},{32,48},{48,64},{64,80},{80,96},{96,112},{112,0},{1... | collective-permute-start | bytes 1105928 | tf_op jit(solution)/shard_map/ppermute | solution.py:262
  64.0 14.2 %collective-permute-start.14 = (bf16[1,96,1920]{2,1,0:T(8,128)(2,1)}, bf16[1,96,1920]{2,1,0:T(8,128)(2,1)S(1)}, u32[]{:S(2)}, u32[]{:S(2)}) collective-permute-start(bf16[1,96,1920]{2,1,0:T(8,128)(2,1)} %collective-permute-done.8.refs_4_), channel_id=1, source_target_pairs={{0,112},{16,0},{32,16},{48,32},{64,48},{80,64},{96,80},{112,96},{1... | collective-permute-start | bytes 1105928 | tf_op jit(solution)/shard_map/ppermute | solution.py:265
  68.2 14.1 %collective-permute-start.10 = (bf16[512,384]{1,0:T(8,128)(2,1)}, bf16[512,384]{1,0:T(8,128)(2,1)S(1)}, u32[]{:S(2)}, u32[]{:S(2)}) collective-permute-start(bf16[512,384]{1,0:T(8,128)(2,1)} %slice_bitcast_fusion), channel_id=1, source_target_pairs={{0,3},{1,0},{2,1},{3,2},{4,7},{5,4},{6,5},{7,6},{8,11},{9,8},{10,9... | collective-permute-start | bytes 1179656 | tf_op jit(solution)/shard_map/ppermute | solution.py:265
  71.6 11.5 %collective-permute-start.9 = (bf16[512,384]{1,0:T(8,128)(2,1)}, bf16[512,384]{1,0:T(8,128)(2,1)}, u32[]{:S(2)}, u32[]{:S(2)}) collective-permute-start(bf16[512,384]{1,0:T(8,128)(2,1)} %slice_bitcast_fusion.1), channel_id=1, source_target_pairs={{0,1},{1,2},{2,3},{3,0},{4,5},{5,6},{6,7},{7,4},{8,9},{9,10},{10,1... | collective-permute-start | bytes 1179656 | tf_op jit(solution)/shard_map/ppermute | solution.py:262
  77.1 13.7 %collective-permute-start.13 = (bf16[1,48,1920]{2,1,0:T(8,128)(2,1)}, bf16[1,48,1920]{2,1,0:T(8,128)(2,1)}, u32[]{:S(2)}, u32[]{:S(2)}) collective-permute-start(bf16[1,48,1920]{2,1,0:T(8,128)(2,1)} %slice.24), channel_id=1, source_target_pairs={{0,16},{16,32},{32,48},{48,64},{64,80},{80,96},{96,112},{112,0},{1... | collective-permute-start | bytes 552968 | tf_op jit(solution)/shard_map/ppermute | solution.py:262
  78.9 11.9 %collective-permute-start.15 = (bf16[1,48,1920]{2,1,0:T(8,128)(2,1)}, bf16[1,48,1920]{2,1,0:T(8,128)(2,1)}, u32[]{:S(2)}, u32[]{:S(2)}) collective-permute-start(bf16[1,48,1920]{2,1,0:T(8,128)(2,1)} %slice.25), channel_id=1, source_target_pairs={{0,112},{16,0},{32,16},{48,32},{64,48},{80,64},{96,80},{112,96},{1... | collective-permute-start | bytes 552968 | tf_op jit(solution)/shard_map/ppermute | solution.py:265
  86.4 17.4 %copy-start.10 = (bf16[1,96,1920]{2,1,0:T(8,128)(2,1)S(1)}, bf16[1,96,1920]{2,1,0:T(8,128)(2,1)}, u32[]{:S(2)}) copy-start(bf16[1,96,1920]{2,1,0:T(8,128)(2,1)} %copy-done.9) | copy-start | bytes 1105924
  86.4 17.4 %copy-start.13 = (bf16[1,96,1920]{2,1,0:T(8,128)(2,1)S(1)}, bf16[1,96,1920]{2,1,0:T(8,128)(2,1)}, u32[]{:S(2)}) copy-start(bf16[1,96,1920]{2,1,0:T(8,128)(2,1)} %copy-done.12) | copy-start | bytes 1105924
  90.8 20.7 %copy-start.7 = (bf16[3,96,1920]{2,1,0:T(8,128)(2,1)S(1)}, bf16[3,96,1920]{2,1,0:T(8,128)(2,1)}, u32[]{:S(2)}) copy-start(bf16[3,96,1920]{2,1,0:T(8,128)(2,1)} %copy-done.6) | copy-start | bytes 3317764
  90.8 24.3 %copy-start.26 = (f32[3,128]{1,0:T(4,128)S(1)}, f32[3,128]{1,0:T(4,128)}, u32[]{:S(2)}) copy-start(f32[3,128]{1,0:T(4,128)} %q_gain_ref.1) | copy-start | bytes 4612
  90.8 24.3 %copy-start.27 = (f32[3,128]{1,0:T(4,128)S(1)}, f32[3,128]{1,0:T(4,128)}, u32[]{:S(2)}) copy-start(f32[3,128]{1,0:T(4,128)} %k_gain_ref.1) | copy-start | bytes 4612
  102.7 4.8 %collective-permute-start.16 = (bf16[3,768,384]{2,1,0:T(8,128)(2,1)}, bf16[3,768,384]{2,1,0:T(8,128)(2,1)S(1)}, u32[]{:S(2)}, u32[]{:S(2)}) collective-permute-start(bf16[3,768,384]{2,1,0:T(8,128)(2,1)} %collective-permute-done.11.near_ref), channel_id=1, source_target_pairs={{0,8},{8,0},{1,9},{9,1},{2,10},{10,2},{3,11},{11,3},{4,12},{12,4},... | collective-permute-start | bytes 5308424 | tf_op jit(solution)/shard_map/ppermute | solution.py:304
  108.8 27.4 %collective-permute-start.19 = (bf16[3,96,1920]{2,1,0:T(8,128)(2,1)}, bf16[3,96,1920]{2,1,0:T(8,128)(2,1)}, u32[]{:S(2)}, u32[]{:S(2)}) collective-permute-start(bf16[3,96,1920]{2,1,0:T(8,128)(2,1)} %pad_maximum_fusion.1), channel_id=1, source_target_pairs={{0,128},{128,0},{1,129},{129,1},{2,130},{130,2},{3,131},{131,3},{4... | collective-permute-start | bytes 3317768 | tf_op jit(solution)/shard_map/ppermute | solution.py:122
  112.4 19.2 %collective-permute-start.17 = (bf16[1,96,1920]{2,1,0:T(8,128)(2,1)}, bf16[1,96,1920]{2,1,0:T(8,128)(2,1)}, u32[]{:S(2)}, u32[]{:S(2)}) collective-permute-start(bf16[1,96,1920]{2,1,0:T(8,128)(2,1)} %get-tuple-element.55), channel_id=1, source_target_pairs={{0,16},{16,32},{32,48},{48,64},{64,80},{80,96},{96,112},{112,0},{1... | collective-permute-start | bytes 1105928 | tf_op jit(solution)/shard_map/ppermute | solution.py:262
  112.6 19.0 %collective-permute-start.18 = (bf16[1,96,1920]{2,1,0:T(8,128)(2,1)}, bf16[1,96,1920]{2,1,0:T(8,128)(2,1)}, u32[]{:S(2)}, u32[]{:S(2)}) collective-permute-start(bf16[1,96,1920]{2,1,0:T(8,128)(2,1)} %get-tuple-element.56), channel_id=1, source_target_pairs={{0,112},{16,0},{32,16},{48,32},{64,48},{80,64},{96,80},{112,96},{1... | collective-permute-start | bytes 1105928 | tf_op jit(solution)/shard_map/ppermute | solution.py:265
  118.6 7.7 %copy-start.8 = (bf16[3,96,1920]{2,1,0:T(8,128)(2,1)S(1)}, bf16[3,96,1920]{2,1,0:T(8,128)(2,1)}, u32[]{:S(2)}) copy-start(bf16[3,96,1920]{2,1,0:T(8,128)(2,1)} %copy-done.6) | copy-start | bytes 3317764
  118.6 7.7 %copy-start.11 = (bf16[1,96,1920]{2,1,0:T(8,128)(2,1)S(1)}, bf16[1,96,1920]{2,1,0:T(8,128)(2,1)}, u32[]{:S(2)}) copy-start(bf16[1,96,1920]{2,1,0:T(8,128)(2,1)} %copy-done.9) | copy-start | bytes 1105924
  118.6 7.8 %copy-start.14 = (bf16[1,96,1920]{2,1,0:T(8,128)(2,1)S(1)}, bf16[1,96,1920]{2,1,0:T(8,128)(2,1)}, u32[]{:S(2)}) copy-start(bf16[1,96,1920]{2,1,0:T(8,128)(2,1)} %copy-done.12) | copy-start | bytes 1105924
  118.6 7.8 %copy-start.22 = (bf16[1,96,1920]{2,1,0:T(8,128)(2,1)S(1)}, bf16[1,96,1920]{2,1,0:T(8,128)(2,1)}, u32[]{:S(2)}) copy-start(bf16[1,96,1920]{2,1,0:T(8,128)(2,1)} %copy-done.21) | copy-start | bytes 1105924
  144.8 11.8 %collective-permute-start.22 = (bf16[512,1536]{1,0:T(8,128)(2,1)}, bf16[512,1536]{1,0:T(8,128)(2,1)S(1)}, u32[]{:S(2)}, u32[]{:S(2)}) collective-permute-start(bf16[512,1536]{1,0:T(8,128)(2,1)} %shard_map.85.activated_ref), channel_id=1, source_target_pairs={{0,8},{8,0},{1,9},{9,1},{2,10},{10,2},{3,11},{11,3},{4,12},{12,4},... | collective-permute-start | bytes 4718600 | tf_op jit(solution)/shard_map/ppermute | solution.py:319
  146.0 10.6 %collective-permute-start.21 = (bf16[512,384]{1,0:T(8,128)(2,1)}, bf16[512,384]{1,0:T(8,128)(2,1)S(1)}, u32[]{:S(2)}, u32[]{:S(2)}) collective-permute-start(bf16[512,384]{1,0:T(8,128)(2,1)} %copy-done.19), channel_id=1, source_target_pairs={{0,8},{8,0},{1,9},{9,1},{2,10},{10,2},{3,11},{11,3},{4,12},{12,4},... | collective-permute-start | bytes 1179656 | tf_op jit(solution)/shard_map/ppermute | solution.py:319
  155.6 18.9 %collective-permute-start.20 = (bf16[4,192,512]{2,1,0:T(8,128)(2,1)}, bf16[4,192,512]{2,1,0:T(8,128)(2,1)}, u32[]{:S(2)}, u32[]{:S(2)}) collective-permute-start(bf16[4,192,512]{2,1,0:T(8,128)(2,1)} %dynamic-slice_bitcast_fusion), channel_id=1, source_target_pairs={{0,4},{4,0},{1,5},{5,1},{2,6},{6,2},{3,7},{7,3},{8,12},{12,8},{9,1... | collective-permute-start | bytes 2359304 | tf_op jit(solution)/shard_map/ppermute | solution.py:100
  164.7 9.8 %collective-permute-start.23 = (bf16[2,192,512]{2,1,0:T(8,128)(2,1)S(1)}, bf16[2,192,512]{2,1,0:T(8,128)(2,1)S(1)}, u32[]{:S(2)}, u32[]{:S(2)}) collective-permute-start(bf16[2,192,512]{2,1,0:T(8,128)(2,1)S(1)} %get-tuple-element.74), channel_id=1, source_target_pairs={{0,8},{8,0},{1,9},{9,1},{2,10},{10,2},{3,11},{11,3},{4,12},{12,4},... | collective-permute-start | bytes 1179656 | tf_op jit(solution)/shard_map/ppermute | solution.py:101
  165.5 14.5 %collective-permute-start.27 = (bf16[2,192,512]{2,1,0:T(8,128)(2,1)}, bf16[2,192,512]{2,1,0:T(8,128)(2,1)S(1)}, u32[]{:S(2)}, u32[]{:S(2)}) collective-permute-start(bf16[2,192,512]{2,1,0:T(8,128)(2,1)} %get-tuple-element.73), channel_id=1, source_target_pairs={{0,10},{1,11},{2,8},{3,9},{8,2},{9,3},{10,0},{11,1},{4,14},{5,15},... | collective-permute-start | bytes 1179656 | tf_op jit(solution)/shard_map/ppermute | solution.py:92
  168.4 18.8 %collective-permute-start.28 = (bf16[2,192,512]{2,1,0:T(8,128)(2,1)}, bf16[2,192,512]{2,1,0:T(8,128)(2,1)S(1)}, u32[]{:S(2)}, u32[]{:S(2)}) collective-permute-start(bf16[2,192,512]{2,1,0:T(8,128)(2,1)} %get-tuple-element.72), channel_id=1, source_target_pairs={{0,9},{1,10},{2,11},{3,8},{8,1},{9,2},{10,3},{11,0},{4,13},{5,14},... | collective-permute-start | bytes 1179656 | tf_op jit(solution)/shard_map/ppermute | solution.py:92
  169.1 18.7 %collective-permute-start.29 = (bf16[2,192,512]{2,1,0:T(8,128)(2,1)}, bf16[2,192,512]{2,1,0:T(8,128)(2,1)S(1)}, u32[]{:S(2)}, u32[]{:S(2)}) collective-permute-start(bf16[2,192,512]{2,1,0:T(8,128)(2,1)} %get-tuple-element.71), channel_id=1, source_target_pairs={{0,11},{1,8},{2,9},{3,10},{8,3},{9,0},{10,1},{11,2},{4,15},{5,12},... | collective-permute-start | bytes 1179656 | tf_op jit(solution)/shard_map/ppermute | solution.py:92
  176.8 11.8 %copy-start.29 = (bf16[512,384]{1,0:T(8,128)(2,1)S(1)}, bf16[512,384]{1,0:T(8,128)(2,1)}, u32[]{:S(2)}) copy-start(bf16[512,384]{1,0:T(8,128)(2,1)} %param.8) | copy-start | bytes 1179652
  176.8 13.9 %collective-permute-start.24 = (bf16[192,512]{1,0:T(8,128)(2,1)}, bf16[192,512]{1,0:T(8,128)(2,1)}, u32[]{:S(2)}, u32[]{:S(2)}) collective-permute-start(bf16[192,512]{1,0:T(8,128)(2,1)} %get-tuple-element.77), channel_id=1, source_target_pairs={{0,2},{1,3},{2,0},{3,1},{8,10},{9,11},{10,8},{11,9},{4,6},{5,7},{6... | collective-permute-start | bytes 589832 | tf_op jit(solution)/shard_map/ppermute | solution.py:92
  179.7 15.6 %collective-permute-start.25 = (bf16[192,512]{1,0:T(8,128)(2,1)}, bf16[192,512]{1,0:T(8,128)(2,1)}, u32[]{:S(2)}, u32[]{:S(2)}) collective-permute-start(bf16[192,512]{1,0:T(8,128)(2,1)} %get-tuple-element.79), channel_id=1, source_target_pairs={{0,1},{1,2},{2,3},{3,0},{8,9},{9,10},{10,11},{11,8},{4,5},{5,6},{6... | collective-permute-start | bytes 589832 | tf_op jit(solution)/shard_map/ppermute | solution.py:92
  180.0 15.3 %collective-permute-start.26 = (bf16[192,512]{1,0:T(8,128)(2,1)}, bf16[192,512]{1,0:T(8,128)(2,1)}, u32[]{:S(2)}, u32[]{:S(2)}) collective-permute-start(bf16[192,512]{1,0:T(8,128)(2,1)} %get-tuple-element.78), channel_id=1, source_target_pairs={{0,3},{1,0},{2,1},{3,2},{8,11},{9,8},{10,9},{11,10},{4,7},{5,4},{6... | collective-permute-start | bytes 589832 | tf_op jit(solution)/shard_map/ppermute | solution.py:92
  188.0 7.3 %collective-permute-start.30 = (bf16[192,512]{1,0:T(8,128)(2,1)S(1)}, bf16[192,512]{1,0:T(8,128)(2,1)S(1)}, u32[]{:S(2)}, u32[]{:S(2)}) collective-permute-start(bf16[192,512]{1,0:T(8,128)(2,1)S(1)} %fusion.5), channel_id=1, source_target_pairs={{0,4},{4,0},{1,5},{5,1},{2,6},{6,2},{3,7},{7,3},{8,12},{12,8},{9,1... | collective-permute-start | bytes 589832 | tf_op jit(solution)/shard_map/ppermute | solution.py:117
  (16 other events, 33.3 us)
Sparse Core Ops, SparseCore 0:
  9.2 48.6 all-gather.2
  59.8 73.1 all-gather.4

commit v5 on v4

--- a/solution.py
+++ b/solution.py
@@ -300,13 +300,13 @@
     other_low, other_high = up(ends[0]), down(ends[1])
 
     normed = norm_tokens(lax.axis_index("x"), ln_gain, pair, right, left, far_a, far_b)
-    other_c = tie(other_c, (normed, end_a, end_b))
+    distant = jnp.concatenate([low, jnp.concatenate([end_a, end_b], axis=1), high])
+    other_c, distant, normed = lax.optimization_barrier((other_c, distant, normed))
     other_d = lax.ppermute(other_c, "c", SWAP)
+    distant = across(distant)
 
     base = (1 - yh) * 2 * quarter
     starts = jnp.stack([yh * 2 * quarter, base + c * quarter, base + (1 - c) * quarter])
-    distant = jnp.concatenate([low, jnp.concatenate([end_a, end_b], axis=1), high])
-    distant = across(tie(distant, other_d))
     attended = attention(starts, normed, own_qkv, other_c, other_d, q_gain, k_gain)
 
     shards = [(places, tie(arrays, attended)) for places, arrays in shards]

time: 206 us -> 201 us (0.976)
  local copies, waits for them, and re-layouts: 28.9 us -> 23.2 us
  waiting for transfers between devices: 66.8 us -> 68.9 us
    ppermute x7, waiting for transfers between devices: 20.2 us -> 28.3 us  [up(): return lax.ppermute(v, axis, shift(size, 1))]
    ppermute x4, waiting for transfers between devices: 24.9 us -> 17.4 us  [across(): return lax.ppermute(v, 'yh', SWAP)]
    unnamed x63 -> x57, local copies, waits for them, and re-layouts: 17.1 us -> 10.9 us
    ppermute x7, waiting for transfers between devices: 1.11 us -> 4.77 us  [down(): return lax.ppermute(v, axis, shift(size, -1))]
    ppermute x6, waiting for transfers between devices: 11.9 us -> 9.34 us  [to_peers_x(): lax.ppermute(pick(blocks, (x + k) % 4, axis), ('c', 'x'), perm)]
    ppermute x1, starting transfers between devices: 1.09 us -> 3.59 us  [local(): other_d = lax.ppermute(other_c, 'c', SWAP)]
    ppermute x4, starting transfers between devices: 8.7 us -> 6.38 us  [across(): return lax.ppermute(v, 'yh', SWAP)]
  transfers between devices with their start and end apart: 33 -> 33, of which waited for: 14 -> 16; matrix products, arithmetic and copies ran while one was open for 10% -> 10% of each run, Pallas kernels for 12% -> 12%
where the time goes in v5:
time: 201 us; the launch traced here: 200 us
  waiting for transfers between devices  68.9 us (34%)
  starting transfers between devices  51.2 us (25%)
  Pallas kernels  33.1 us (16%)
  local copies, waits for them, and re-layouts  23.2 us (12%)
  between operations  13.7 us (7%)
  other arithmetic  9.83 us (5%)
    ppermute x7, waiting for transfers between devices, up(): return lax.ppermute(v, axis, shift(size, 1))  28.3 us
    ppermute x7, starting transfers between devices, down(): return lax.ppermute(v, axis, shift(size, -1))  19 us
    ppermute x4, waiting for transfers between devices, across(): return lax.ppermute(v, 'yh', SWAP)  17.4 us
    unnamed x57, local copies, waits for them, and re-layouts  10.9 us
    pallas_call x2, Pallas kernels, out_terms(): pl.pallas_call(functools.partial(out_kernel, slots), in_specs=[pl.BlockSp...  10.4 us
    ppermute x6, starting transfers between devices, to_peers_x(): lax.ppermute(pick(blocks, (x + k) % 4, axis), ('c', 'x'), perm)  10.3 us
    ppermute x6, waiting for transfers between devices, to_peers_x(): lax.ppermute(pick(blocks, (x + k) % 4, axis), ('c', 'x'), perm)  9.34 us
    pallas_call x1, Pallas kernels, up_gelu(): pl.pallas_call(up_kernel, grid=(hidden // tile,), in_specs=[pl.BlockSpec(...  8.53 us
  transfers between devices with their start and end apart: 33, of which 16 were waited for; matrix products, arithmetic and copies ran while one was open for 10% of the time, Pallas kernels for 12%

profile of v5, /device:TPU:1, one launch (start us, length us, event | category | flops | bytes accessed | tf_op | source)
XLA Modules:
  0.0 200.0 jit_solution(9384130981235108422)
XLA Ops:
  7.3 2.2 %collective-permute-start = (bf16[512,384]{1,0:T(8,128)(2,1)}, bf16[512,384]{1,0:T(8,128)(2,1)S(1)}, u32[]{:S(2)}, u32[]{:S(2)}) collective-permute-start(bf16[512,384]{1,0:T(8,128)(2,1)} %param.8), channel_id=1, source_target_pairs={{0,4},{4,0},{1,5},{5,1},{2,6},{6,2},{3,7},{7,3},{8,12},{12,8},{9,1... | collective-permute-start | bytes 1179656 | tf_op jit(solution)/shard_map/ppermute | solution.py:273
  10.5 1.7 collective-permute-start.2
  12.2 4.0 %collective-permute-start.3 = (bf16[1,96,1920]{2,1,0:T(8,128)(2,1)S(1)}, bf16[1,96,1920]{2,1,0:T(8,128)(2,1)}, u32[]{:S(2)}, u32[]{:S(2)}) collective-permute-start(bf16[1,96,1920]{2,1,0:T(8,128)(2,1)S(1)} %maximum_bitcast_fusion.refs_0_), channel_id=1, source_target_pairs={{0,112},{16,0},{32,16},{48,32},{64,48},{80,64},{96,80},{112,96},{1... | collective-permute-start | bytes 1105928 | tf_op jit(solution)/shard_map/ppermute | solution.py:265
  16.3 2.6 %collective-permute-start.1 = (bf16[96,1536]{1,0:T(8,128)(2,1)}, bf16[96,1536]{1,0:T(8,128)(2,1)S(1)}, u32[]{:S(2)}, u32[]{:S(2)}) collective-permute-start(bf16[96,1536]{1,0:T(8,128)(2,1)} %param.11), channel_id=1, source_target_pairs={{0,128},{128,0},{1,129},{129,1},{2,130},{130,2},{3,131},{131,3},{4... | collective-permute-start | bytes 884744 | tf_op jit(solution)/shard_map/ppermute | solution.py:122
  18.9 8.3 %collective-permute-done.1 = bf16[96,1536]{1,0:T(8,128)(2,1)S(1)} collective-permute-done((bf16[96,1536]{1,0:T(8,128)(2,1)}, bf16[96,1536]{1,0:T(8,128)(2,1)S(1)}, u32[]{:S(2)}, u32[]{:S(2)}) %collective-permute-start.1) | collective-permute-done | bytes 294944 | tf_op jit(solution)/shard_map/ppermute | solution.py:122
  27.2 2.1 %maximum_select_fusion = bf16[2,96,1536]{2,1,0:T(8,128)(2,1)} fusion(bf16[1,96,1536]{2,1,0:T(8,128)(2,1)S(1)} %bitcast.80, bf16[1,96,1536]{2,1,0:T(8,128)(2,1)} %bitcast.79, pred[]{:T(512)S(6)} %eq.20), kind=kLoop, calls=%fused_computation.9 | loop fusion | flops 884736 | bytes 1179649 | tf_op jit(solution)/shard_map/jit(_where)/select_n | solution.py:78
  29.3 2.2 %pad_maximum_fusion = bf16[3,96,1920]{2,1,0:T(8,128)(2,1)} fusion(bf16[1,96,1920]{2,1,0:T(8,128)(2,1)} %collective-permute-done.3.refs_2_, bf16[1,96,1920]{2,1,0:T(8,128)(2,1)S(1)} %maximum_bitcast_fusion.refs_0_, bf16[1,96,1920]{2,1,0:T(8,128)(2,1)S(1)} %collective-permute-done.2.refs_1_), kind=kLoop, calls=%fused_computation.1 | loop fusion | flops 1105920 | bytes 2211840 | tf_op jit(solution)/shard_map/concatenate | solution.py:283
  32.4 1.3 collective-permute-start.4
  33.7 1.5 collective-permute-start.5
  35.1 1.3 collective-permute-start.7
  36.5 4.1 %collective-permute-start.8 = (bf16[1,96,1920]{2,1,0:T(8,128)(2,1)}, bf16[1,96,1920]{2,1,0:T(8,128)(2,1)}, u32[]{:S(2)}, u32[]{:S(2)}) collective-permute-start(bf16[1,96,1920]{2,1,0:T(8,128)(2,1)} %collective-permute-done.3.refs_2_), channel_id=1, source_target_pairs={{0,112},{16,0},{32,16},{48,32},{64,48},{80,64},{96,80},{112,96},{1... | collective-permute-start | bytes 1105928 | tf_op jit(solution)/shard_map/ppermute | solution.py:265
  40.5 14.1 %collective-permute-done.7.refs_3_ = bf16[1,96,1920]{2,1,0:T(8,128)(2,1)} collective-permute-done((bf16[1,96,1920]{2,1,0:T(8,128)(2,1)S(1)}, bf16[1,96,1920]{2,1,0:T(8,128)(2,1)}, u32[]{:S(2)}, u32[]{:S(2)}) %collective-permute-start.7) | collective-permute-done | bytes 368672 | tf_op jit(solution)/shard_map/ppermute | solution.py:262
  54.7 3.3 %all-gather.3.cloned.1.call-done.own_ref = bf16[3,1536,384]{2,1,0:T(8,128)(2,1)} async-done(((bf16[3,96,384]{2,1,0:T(8,128)(2,1)}), bf16[3,1536,384]{2,1,0:T(8,128)(2,1)}) %all-gather.3.cloned.1.call-update) | async-done | bytes 3538960 | tf_op jit(solution)/shard_map/all_gather | solution.py:267
  57.9 2.9 %constant_dynamic-slice_fusion = bf16[3,768,384]{2,1,0:T(8,128)(2,1)} fusion(bf16[3,1536,384]{2,1,0:T(8,128)(2,1)} %all-gather.3.cloned.1.call-done.own_ref, s32[]{:T(128)S(6)} %select_n.111), kind=kLoop, calls=%fused_computation.30 | loop fusion | bytes 3538948 | tf_op jit(solution)/shard_map/dynamic_slice | solution.py:285
  60.8 2.8 %collective-permute-start.9 = (bf16[3,768,384]{2,1,0:T(8,128)(2,1)}, bf16[3,768,384]{2,1,0:T(8,128)(2,1)}, u32[]{:S(2)}, u32[]{:S(2)}) collective-permute-start(bf16[3,768,384]{2,1,0:T(8,128)(2,1)} %constant_dynamic-slice_fusion), channel_id=1, source_target_pairs={{0,128},{128,0},{1,129},{129,1},{2,130},{130,2},{3,131},{131,3},{4... | collective-permute-start | bytes 5308424 | tf_op jit(solution)/shard_map/ppermute | solution.py:122
  64.0 2.4 %collective-permute-start.12 = (bf16[1,96,1920]{2,1,0:T(8,128)(2,1)}, bf16[1,96,1920]{2,1,0:T(8,128)(2,1)S(1)}, u32[]{:S(2)}, u32[]{:S(2)}) collective-permute-start(bf16[1,96,1920]{2,1,0:T(8,128)(2,1)} %collective-permute-done.8.refs_4_), channel_id=1, source_target_pairs={{0,112},{16,0},{32,16},{48,32},{64,48},{80,64},{96,80},{112,96},{1... | collective-permute-start | bytes 1105928 | tf_op jit(solution)/shard_map/ppermute | solution.py:265
  66.4 9.9 %collective-permute-done.10.refs_6_ = bf16[1,96,1920]{2,1,0:T(8,128)(2,1)S(1)} collective-permute-done((bf16[1,96,1920]{2,1,0:T(8,128)(2,1)}, bf16[1,96,1920]{2,1,0:T(8,128)(2,1)S(1)}, u32[]{:S(2)}, u32[]{:S(2)}) %collective-permute-start.10) | collective-permute-done | bytes 368672 | tf_op jit(solution)/shard_map/ppermute | solution.py:262
  78.9 3.4 %collective-permute-start.13 = (bf16[1,48,1920]{2,1,0:T(8,128)(2,1)}, bf16[1,48,1920]{2,1,0:T(8,128)(2,1)S(1)}, u32[]{:S(2)}, u32[]{:S(2)}) collective-permute-start(bf16[1,48,1920]{2,1,0:T(8,128)(2,1)} %slice.25), channel_id=1, source_target_pairs={{0,112},{16,0},{32,16},{48,32},{64,48},{80,64},{96,80},{112,96},{1... | collective-permute-start | bytes 552968 | tf_op jit(solution)/shard_map/ppermute | solution.py:265
  83.1 1.6 collective-permute-start.14
  84.7 1.8 slice_bitcast_fusion
  86.5 1.2 collective-permute-start.15
  87.9 1.6 collective-permute-done.13.refs_9_
  91.7 2.0 %collective-permute-done.15.far_b_ref = bf16[512,384]{1,0:T(8,128)(2,1)} collective-permute-done((bf16[512,384]{1,0:T(8,128)(2,1)}, bf16[512,384]{1,0:T(8,128)(2,1)}, u32[]{:S(2)}, u32[]{:S(2)}) %collective-permute-start.15) | collective-permute-done | bytes 393248 | tf_op jit(solution)/shard_map/ppermute | solution.py:265
  96.0 4.4 %shard_map.82.x_ref = bf16[512,3072]{1,0:T(8,128)(2,1)S(1)} custom-call(s32[1]{0:T(128)} %bitcast.11.x_ref, f32[1,3072]{1,0:T(1,128)S(1)} %bitcast.74, bf16[2,512,384]{2,1,0:T(8,128)(2,1)S(1)} %copy-done.5, bf16[2,512,384]{2,1,0:T(8,128)(2,1)S(1)} %copy-done.14, bf16[2,512,384]{2,1,0:T(8,128)(2,1)} %collective-permute-done.5.left_ref, ...), custom_call_target="tpu_custom_call" | custom-call | tf_op jit(solution)/shard_map/pallas_call | solution.py:58
  100.4 2.3 %collective-permute-done.9.near_ref = bf16[3,768,384]{2,1,0:T(8,128)(2,1)} collective-permute-done((bf16[3,768,384]{2,1,0:T(8,128)(2,1)}, bf16[3,768,384]{2,1,0:T(8,128)(2,1)}, u32[]{:S(2)}, u32[]{:S(2)}) %collective-permute-start.9) | collective-permute-done | bytes 1769504 | tf_op jit(solution)/shard_map/ppermute | solution.py:122
  102.7 3.6 %collective-permute-start.16 = (bf16[3,768,384]{2,1,0:T(8,128)(2,1)}, bf16[3,768,384]{2,1,0:T(8,128)(2,1)}, u32[]{:S(2)}, u32[]{:S(2)}) collective-permute-start(bf16[3,768,384]{2,1,0:T(8,128)(2,1)} %collective-permute-done.9.near_ref), channel_id=1, source_target_pairs={{0,8},{8,0},{1,9},{9,1},{2,10},{10,2},{3,11},{11,3},{4,12},{12,4},... | collective-permute-start | bytes 5308424 | tf_op jit(solution)/shard_map/ppermute | solution.py:305
  107.7 2.4 %collective-permute-start.18 = (bf16[1,96,1920]{2,1,0:T(8,128)(2,1)}, bf16[1,96,1920]{2,1,0:T(8,128)(2,1)}, u32[]{:S(2)}, u32[]{:S(2)}) collective-permute-start(bf16[1,96,1920]{2,1,0:T(8,128)(2,1)} %get-tuple-element.58), channel_id=1, source_target_pairs={{0,112},{16,0},{32,16},{48,32},{64,48},{80,64},{96,80},{112,96},{1... | collective-permute-start | bytes 1105928 | tf_op jit(solution)/shard_map/ppermute | solution.py:265
  110.3 2.0 %copy-done.3 = bf16[3,1536,384]{2,1,0:T(8,128)(2,1)S(1)} copy-done((bf16[3,1536,384]{2,1,0:T(8,128)(2,1)S(1)}, bf16[3,1536,384]{2,1,0:T(8,128)(2,1)}, u32[]{:S(2)}) %copy-start.3) | copy-done | bytes 3538968
  112.3 8.1 %shard_map.83.attended_ref = bf16[512,384]{1,0:T(8,128)(2,1)S(1)} custom-call(s32[3]{0:T(128)S(1)} %pad_add_fusion.1.starts_ref, bf16[512,3072]{1,0:T(8,128)(2,1)S(1)} %shard_map.82.x_ref, bf16[3,1536,384]{2,1,0:T(8,128)(2,1)S(1)} %copy-done.3, bf16[3,768,384]{2,1,0:T(8,128)(2,1)} %collective-permute-done.9.near_ref, ...), custom_call_target="tpu_custom_call" | custom-call | tf_op jit(solution)/shard_map/pallas_call | solution.py:184
  120.5 1.7 shard_map.84.weights_ref
  122.2 2.0 %copy-done = bf16[1056,1920]{1,0:T(8,128)(2,1)} copy-done((bf16[1056,1920]{1,0:T(8,128)(2,1)}, bf16[1056,1920]{1,0:T(8,128)(2,1)S(1)}, u32[]{:S(2)}) %copy-start) | copy-done | bytes 4055064
  124.3 3.0 %collective-permute-done.17.low_ref = bf16[1,96,1920]{2,1,0:T(8,128)(2,1)} collective-permute-done((bf16[1,96,1920]{2,1,0:T(8,128)(2,1)}, bf16[1,96,1920]{2,1,0:T(8,128)(2,1)}, u32[]{:S(2)}, u32[]{:S(2)}) %collective-permute-start.17) | collective-permute-done | bytes 368672 | tf_op jit(solution)/shard_map/ppermute | solution.py:262
  127.2 6.8 %collective-permute-done.19.distant_ref = bf16[3,96,1920]{2,1,0:T(8,128)(2,1)} collective-permute-done((bf16[3,96,1920]{2,1,0:T(8,128)(2,1)}, bf16[3,96,1920]{2,1,0:T(8,128)(2,1)}, u32[]{:S(2)}, u32[]{:S(2)}) %collective-permute-start.19) | collective-permute-done | bytes 1105952 | tf_op jit(solution)/shard_map/ppermute | solution.py:122
  134.1 8.5 %shard_map.85.activated_ref = bf16[512,1536]{1,0:T(8,128)(2,1)} custom-call(bf16[512,3072]{1,0:T(8,128)(2,1)S(1)} %shard_map.82.x_ref, bf16[3072,1536]{1,0:T(8,128)(2,1)} %bitcast.75), custom_call_target="tpu_custom_call" | custom-call | tf_op jit(solution)/shard_map/pallas_call | solution.py:134
  143.7 2.1 %copy-done.1 = bf16[1056,1920]{1,0:T(8,128)(2,1)S(1)} copy-done((bf16[1056,1920]{1,0:T(8,128)(2,1)S(1)}, bf16[1056,1920]{1,0:T(8,128)(2,1)}, u32[]{:S(2)}) %copy-start.1) | copy-done | bytes 4055064
  145.8 5.4 %shard_map.86 = bf16[16,96,512]{2,1,0:T(8,128)(2,1)S(1)} custom-call(s32[2]{0:T(128)S(1)} %pad_add_fusion.at_ref, bf16[1056,1920]{1,0:T(8,128)(2,1)S(1)} %copy-done.1, bf16[1,96,1920]{2,1,0:T(8,128)(2,1)} %collective-permute-done.17.low_ref, bf16[1,96,1920]{2,1,0:T(8,128)(2,1)} %collective-permute-done.18.high_ref, ...), custom_call_target="tpu_custom_call" | custom-call | tf_op jit(solution)/shard_map/pallas_call | solution.py:247
  152.2 2.1 %copy-done.2 = bf16[1056,1920]{1,0:T(8,128)(2,1)S(1)} copy-done((bf16[1056,1920]{1,0:T(8,128)(2,1)S(1)}, bf16[1056,1920]{1,0:T(8,128)(2,1)}, u32[]{:S(2)}) %copy-start.2) | copy-done | bytes 4055064
  154.4 5.0 %shard_map.87 = bf16[16,96,512]{2,1,0:T(8,128)(2,1)S(1)} custom-call(s32[2]{0:T(128)S(1)} %pad_add_fusion.at_ref, bf16[1056,1920]{1,0:T(8,128)(2,1)S(1)} %copy-done.2, bf16[1,96,1920]{2,1,0:T(8,128)(2,1)} %collective-permute-done.17.low_ref, bf16[1,96,1920]{2,1,0:T(8,128)(2,1)} %collective-permute-done.18.high_ref, ...), custom_call_target="tpu_custom_call" | custom-call | tf_op jit(solution)/shard_map/pallas_call | solution.py:247
  160.8 2.4 %collective-permute-start.27 = (bf16[2,192,512]{2,1,0:T(8,128)(2,1)}, bf16[2,192,512]{2,1,0:T(8,128)(2,1)S(1)}, u32[]{:S(2)}, u32[]{:S(2)}) collective-permute-start(bf16[2,192,512]{2,1,0:T(8,128)(2,1)} %get-tuple-element.75), channel_id=1, source_target_pairs={{0,10},{1,11},{2,8},{3,9},{8,2},{9,3},{10,0},{11,1},{4,14},{5,15},... | collective-permute-start | bytes 1179656 | tf_op jit(solution)/shard_map/ppermute | solution.py:92
  163.9 2.2 %collective-permute-start.29 = (bf16[2,192,512]{2,1,0:T(8,128)(2,1)}, bf16[2,192,512]{2,1,0:T(8,128)(2,1)S(1)}, u32[]{:S(2)}, u32[]{:S(2)}) collective-permute-start(bf16[2,192,512]{2,1,0:T(8,128)(2,1)} %get-tuple-element.73), channel_id=1, source_target_pairs={{0,11},{1,8},{2,9},{3,10},{8,3},{9,0},{10,1},{11,2},{4,15},{5,12},... | collective-permute-start | bytes 1179656 | tf_op jit(solution)/shard_map/ppermute | solution.py:92
  166.1 5.1 %collective-permute-done.20 = bf16[4,192,512]{2,1,0:T(8,128)(2,1)} collective-permute-done((bf16[4,192,512]{2,1,0:T(8,128)(2,1)}, bf16[4,192,512]{2,1,0:T(8,128)(2,1)}, u32[]{:S(2)}, u32[]{:S(2)}) %collective-permute-start.20) | collective-permute-done | bytes 786464 | tf_op jit(solution)/shard_map/ppermute | solution.py:100
  171.2 1.4 fusion.6
  173.4 2.3 %collective-permute-start.24 = (bf16[192,512]{1,0:T(8,128)(2,1)}, bf16[192,512]{1,0:T(8,128)(2,1)}, u32[]{:S(2)}, u32[]{:S(2)}) collective-permute-start(bf16[192,512]{1,0:T(8,128)(2,1)} %get-tuple-element.79), channel_id=1, source_target_pairs={{0,2},{1,3},{2,0},{3,1},{8,10},{9,11},{10,8},{11,9},{4,6},{5,7},{6... | collective-permute-start | bytes 589832 | tf_op jit(solution)/shard_map/ppermute | solution.py:92
  176.1 2.3 %collective-permute-start.26 = (bf16[192,512]{1,0:T(8,128)(2,1)S(1)}, bf16[192,512]{1,0:T(8,128)(2,1)}, u32[]{:S(2)}, u32[]{:S(2)}) collective-permute-start(bf16[192,512]{1,0:T(8,128)(2,1)S(1)} %get-tuple-element.80), channel_id=1, source_target_pairs={{0,3},{1,0},{2,1},{3,2},{8,11},{9,8},{10,9},{11,10},{4,7},{5,4},{6... | collective-permute-start | bytes 589832 | tf_op jit(solution)/shard_map/ppermute | solution.py:92
  178.4 4.1 %collective-permute-done.28 = bf16[2,192,512]{2,1,0:T(8,128)(2,1)S(1)} collective-permute-done((bf16[2,192,512]{2,1,0:T(8,128)(2,1)}, bf16[2,192,512]{2,1,0:T(8,128)(2,1)S(1)}, u32[]{:S(2)}, u32[]{:S(2)}) %collective-permute-start.28) | collective-permute-done | bytes 393248 | tf_op jit(solution)/shard_map/ppermute | solution.py:92
  183.4 1.8 collective-permute-start.30
  186.0 4.6 %collective-permute-done.25 = bf16[192,512]{1,0:T(8,128)(2,1)} collective-permute-done((bf16[192,512]{1,0:T(8,128)(2,1)S(1)}, bf16[192,512]{1,0:T(8,128)(2,1)}, u32[]{:S(2)}, u32[]{:S(2)}) %collective-permute-start.25) | collective-permute-done | bytes 196640 | tf_op jit(solution)/shard_map/ppermute | solution.py:92
  190.6 1.4 fusion.4
  (108 shorter events, 20.8 us)
Async XLA Ops:
  6.5 51.4 %all-gather.3.cloned.1.call-start = ((), (), s32[]{:S(2)}) async-start(), calls=%async_computation | async-start | bytes 3760128 | tf_op jit(solution)/shard_map/all_gather | solution.py:267
  7.3 126.8 %all-gather.5.cloned.1.call-start = ((), (), s32[]{:S(2)}) async-start(), calls=%async_computation.1 | async-start | bytes 10027008 | tf_op jit(solution)/shard_map/all_gather | solution.py:276
  7.3 19.9 %collective-permute-start = (bf16[512,384]{1,0:T(8,128)(2,1)}, bf16[512,384]{1,0:T(8,128)(2,1)S(1)}, u32[]{:S(2)}, u32[]{:S(2)}) collective-permute-start(bf16[512,384]{1,0:T(8,128)(2,1)} %param.8), channel_id=1, source_target_pairs={{0,4},{4,0},{1,5},{5,1},{2,6},{6,2},{3,7},{7,3},{8,12},{12,8},{9,1... | collective-permute-start | bytes 1179656 | tf_op jit(solution)/shard_map/ppermute | solution.py:273
  10.5 16.7 %collective-permute-start.2 = (bf16[1,96,1920]{2,1,0:T(8,128)(2,1)S(1)}, bf16[1,96,1920]{2,1,0:T(8,128)(2,1)S(1)}, u32[]{:S(2)}, u32[]{:S(2)}) collective-permute-start(bf16[1,96,1920]{2,1,0:T(8,128)(2,1)S(1)} %maximum_bitcast_fusion.refs_0_), channel_id=1, source_target_pairs={{0,16},{16,32},{32,48},{48,64},{64,80},{80,96},{96,112},{112,0},{1... | collective-permute-start | bytes 1105928 | tf_op jit(solution)/shard_map/ppermute | solution.py:262
  12.2 15.0 %collective-permute-start.3 = (bf16[1,96,1920]{2,1,0:T(8,128)(2,1)S(1)}, bf16[1,96,1920]{2,1,0:T(8,128)(2,1)}, u32[]{:S(2)}, u32[]{:S(2)}) collective-permute-start(bf16[1,96,1920]{2,1,0:T(8,128)(2,1)S(1)} %maximum_bitcast_fusion.refs_0_), channel_id=1, source_target_pairs={{0,112},{16,0},{32,16},{48,32},{64,48},{80,64},{96,80},{112,96},{1... | collective-permute-start | bytes 1105928 | tf_op jit(solution)/shard_map/ppermute | solution.py:265
  16.3 10.9 %collective-permute-start.1 = (bf16[96,1536]{1,0:T(8,128)(2,1)}, bf16[96,1536]{1,0:T(8,128)(2,1)S(1)}, u32[]{:S(2)}, u32[]{:S(2)}) collective-permute-start(bf16[96,1536]{1,0:T(8,128)(2,1)} %param.11), channel_id=1, source_target_pairs={{0,128},{128,0},{1,129},{129,1},{2,130},{130,2},{3,131},{131,3},{4... | collective-permute-start | bytes 884744 | tf_op jit(solution)/shard_map/ppermute | solution.py:122
  31.5 29.3 %collective-permute-start.6 = (bf16[3,96,1920]{2,1,0:T(8,128)(2,1)}, bf16[3,96,1920]{2,1,0:T(8,128)(2,1)S(1)}, u32[]{:S(2)}, u32[]{:S(2)}) collective-permute-start(bf16[3,96,1920]{2,1,0:T(8,128)(2,1)} %pad_maximum_fusion), channel_id=1, source_target_pairs={{0,128},{128,0},{1,129},{129,1},{2,130},{130,2},{3,131},{131,3},{4... | collective-permute-start | bytes 3317768 | tf_op jit(solution)/shard_map/ppermute | solution.py:122
  32.4 28.4 %copy-start.4 = (bf16[2,512,384]{2,1,0:T(8,128)(2,1)}, bf16[2,512,384]{2,1,0:T(8,128)(2,1)S(1)}, u32[]{:S(2)}) copy-start(bf16[2,512,384]{2,1,0:T(8,128)(2,1)S(1)} %pad_maximum_fusion.2.pair_ref) | copy-start | bytes 2359300
  32.4 28.4 %collective-permute-start.4 = (bf16[2,512,384]{2,1,0:T(8,128)(2,1)S(1)}, bf16[2,512,384]{2,1,0:T(8,128)(2,1)S(1)}, u32[]{:S(2)}, u32[]{:S(2)}) collective-permute-start(bf16[2,512,384]{2,1,0:T(8,128)(2,1)S(1)} %pad_maximum_fusion.2.pair_ref), channel_id=1, source_target_pairs={{0,1},{1,2},{2,3},{3,0},{4,5},{5,6},{6,7},{7,4},{8,9},{9,10},{10,1... | collective-permute-start | bytes 2359304 | tf_op jit(solution)/shard_map/ppermute | solution.py:262
  33.7 27.1 %collective-permute-start.5 = (bf16[2,512,384]{2,1,0:T(8,128)(2,1)S(1)}, bf16[2,512,384]{2,1,0:T(8,128)(2,1)}, u32[]{:S(2)}, u32[]{:S(2)}) collective-permute-start(bf16[2,512,384]{2,1,0:T(8,128)(2,1)S(1)} %pad_maximum_fusion.2.pair_ref), channel_id=1, source_target_pairs={{0,3},{1,0},{2,1},{3,2},{4,7},{5,4},{6,5},{7,6},{8,11},{9,8},{10,9... | collective-permute-start | bytes 2359304 | tf_op jit(solution)/shard_map/ppermute | solution.py:265
  35.1 19.5 %collective-permute-start.7 = (bf16[1,96,1920]{2,1,0:T(8,128)(2,1)S(1)}, bf16[1,96,1920]{2,1,0:T(8,128)(2,1)}, u32[]{:S(2)}, u32[]{:S(2)}) collective-permute-start(bf16[1,96,1920]{2,1,0:T(8,128)(2,1)S(1)} %collective-permute-done.2.refs_1_), channel_id=1, source_target_pairs={{0,16},{16,32},{32,48},{48,64},{64,80},{80,96},{96,112},{112,0},{1... | collective-permute-start | bytes 1105928 | tf_op jit(solution)/shard_map/ppermute | solution.py:262
  36.5 18.2 %collective-permute-start.8 = (bf16[1,96,1920]{2,1,0:T(8,128)(2,1)}, bf16[1,96,1920]{2,1,0:T(8,128)(2,1)}, u32[]{:S(2)}, u32[]{:S(2)}) collective-permute-start(bf16[1,96,1920]{2,1,0:T(8,128)(2,1)} %collective-permute-done.3.refs_2_), channel_id=1, source_target_pairs={{0,112},{16,0},{32,16},{48,32},{64,48},{80,64},{96,80},{112,96},{1... | collective-permute-start | bytes 1105928 | tf_op jit(solution)/shard_map/ppermute | solution.py:265
  60.8 29.7 %copy-start.13 = (bf16[2,512,384]{2,1,0:T(8,128)(2,1)}, bf16[2,512,384]{2,1,0:T(8,128)(2,1)S(1)}, u32[]{:S(2)}) copy-start(bf16[2,512,384]{2,1,0:T(8,128)(2,1)S(1)} %collective-permute-done.4.right_ref) | copy-start | bytes 2359300
  60.8 29.7 %copy-start.6 = (bf16[3,96,1920]{2,1,0:T(8,128)(2,1)}, bf16[3,96,1920]{2,1,0:T(8,128)(2,1)S(1)}, u32[]{:S(2)}) copy-start(bf16[3,96,1920]{2,1,0:T(8,128)(2,1)S(1)} %collective-permute-done.6.refs_5_) | copy-start | bytes 3317764
  60.8 41.8 %collective-permute-start.9 = (bf16[3,768,384]{2,1,0:T(8,128)(2,1)}, bf16[3,768,384]{2,1,0:T(8,128)(2,1)}, u32[]{:S(2)}, u32[]{:S(2)}) collective-permute-start(bf16[3,768,384]{2,1,0:T(8,128)(2,1)} %constant_dynamic-slice_fusion), channel_id=1, source_target_pairs={{0,128},{128,0},{1,129},{129,1},{2,130},{130,2},{3,131},{131,3},{4... | collective-permute-start | bytes 5308424 | tf_op jit(solution)/shard_map/ppermute | solution.py:122
  63.7 12.6 %collective-permute-start.10 = (bf16[1,96,1920]{2,1,0:T(8,128)(2,1)}, bf16[1,96,1920]{2,1,0:T(8,128)(2,1)S(1)}, u32[]{:S(2)}, u32[]{:S(2)}) collective-permute-start(bf16[1,96,1920]{2,1,0:T(8,128)(2,1)} %collective-permute-done.7.refs_3_), channel_id=1, source_target_pairs={{0,16},{16,32},{32,48},{48,64},{64,80},{80,96},{96,112},{112,0},{1... | collective-permute-start | bytes 1105928 | tf_op jit(solution)/shard_map/ppermute | solution.py:262
  64.0 14.2 %collective-permute-start.12 = (bf16[1,96,1920]{2,1,0:T(8,128)(2,1)}, bf16[1,96,1920]{2,1,0:T(8,128)(2,1)S(1)}, u32[]{:S(2)}, u32[]{:S(2)}) collective-permute-start(bf16[1,96,1920]{2,1,0:T(8,128)(2,1)} %collective-permute-done.8.refs_4_), channel_id=1, source_target_pairs={{0,112},{16,0},{32,16},{48,32},{64,48},{80,64},{96,80},{112,96},{1... | collective-permute-start | bytes 1105928 | tf_op jit(solution)/shard_map/ppermute | solution.py:265
  76.3 14.3 %copy-start.9 = (bf16[1,96,1920]{2,1,0:T(8,128)(2,1)}, bf16[1,96,1920]{2,1,0:T(8,128)(2,1)S(1)}, u32[]{:S(2)}) copy-start(bf16[1,96,1920]{2,1,0:T(8,128)(2,1)S(1)} %collective-permute-done.10.refs_6_) | copy-start | bytes 1105924
  77.0 10.8 %collective-permute-start.11 = (bf16[1,48,1920]{2,1,0:T(8,128)(2,1)}, bf16[1,48,1920]{2,1,0:T(8,128)(2,1)S(1)}, u32[]{:S(2)}, u32[]{:S(2)}) collective-permute-start(bf16[1,48,1920]{2,1,0:T(8,128)(2,1)} %slice.24), channel_id=1, source_target_pairs={{0,16},{16,32},{32,48},{48,64},{64,80},{80,96},{96,112},{112,0},{1... | collective-permute-start | bytes 552968 | tf_op jit(solution)/shard_map/ppermute | solution.py:262
  78.2 12.4 %copy-start.11 = (bf16[1,96,1920]{2,1,0:T(8,128)(2,1)}, bf16[1,96,1920]{2,1,0:T(8,128)(2,1)S(1)}, u32[]{:S(2)}) copy-start(bf16[1,96,1920]{2,1,0:T(8,128)(2,1)S(1)} %collective-permute-done.12.refs_7_) | copy-start | bytes 1105924
  78.9 10.5 %collective-permute-start.13 = (bf16[1,48,1920]{2,1,0:T(8,128)(2,1)}, bf16[1,48,1920]{2,1,0:T(8,128)(2,1)S(1)}, u32[]{:S(2)}, u32[]{:S(2)}) collective-permute-start(bf16[1,48,1920]{2,1,0:T(8,128)(2,1)} %slice.25), channel_id=1, source_target_pairs={{0,112},{16,0},{32,16},{48,32},{64,48},{80,64},{96,80},{112,96},{1... | collective-permute-start | bytes 552968 | tf_op jit(solution)/shard_map/ppermute | solution.py:265
  83.1 10.6 %copy-start.23 = (f32[3072]{0:T(1024)S(1)}, f32[3072]{0:T(1024)}, u32[]{:S(2)}) copy-start(f32[3072]{0:T(1024)} %param.9) | copy-start | bytes 36868
  83.1 8.6 %collective-permute-start.14 = (bf16[512,384]{1,0:T(8,128)(2,1)}, bf16[512,384]{1,0:T(8,128)(2,1)}, u32[]{:S(2)}, u32[]{:S(2)}) collective-permute-start(bf16[512,384]{1,0:T(8,128)(2,1)} %slice_bitcast_fusion.1), channel_id=1, source_target_pairs={{0,1},{1,2},{2,3},{3,0},{4,5},{5,6},{6,7},{7,4},{8,9},{9,10},{10,1... | collective-permute-start | bytes 1179656 | tf_op jit(solution)/shard_map/ppermute | solution.py:262
  86.5 7.2 %collective-permute-start.15 = (bf16[512,384]{1,0:T(8,128)(2,1)}, bf16[512,384]{1,0:T(8,128)(2,1)}, u32[]{:S(2)}, u32[]{:S(2)}) collective-permute-start(bf16[512,384]{1,0:T(8,128)(2,1)} %slice_bitcast_fusion), channel_id=1, source_target_pairs={{0,3},{1,0},{2,1},{3,2},{4,7},{5,4},{6,5},{7,6},{8,11},{9,8},{10,9... | collective-permute-start | bytes 1179656 | tf_op jit(solution)/shard_map/ppermute | solution.py:265
  96.0 10.5 %copy-start.7 = (bf16[3,96,1920]{2,1,0:T(8,128)(2,1)S(1)}, bf16[3,96,1920]{2,1,0:T(8,128)(2,1)}, u32[]{:S(2)}) copy-start(bf16[3,96,1920]{2,1,0:T(8,128)(2,1)} %copy-done.6) | copy-start | bytes 3317764
  96.0 14.2 %copy-start.24 = (f32[3,128]{1,0:T(4,128)S(1)}, f32[3,128]{1,0:T(4,128)}, u32[]{:S(2)}) copy-start(f32[3,128]{1,0:T(4,128)} %q_gain_ref.1) | copy-start | bytes 4612
  96.0 14.2 %copy-start.25 = (f32[3,128]{1,0:T(4,128)S(1)}, f32[3,128]{1,0:T(4,128)}, u32[]{:S(2)}) copy-start(f32[3,128]{1,0:T(4,128)} %k_gain_ref.1) | copy-start | bytes 4612
  102.7 7.6 %collective-permute-start.16 = (bf16[3,768,384]{2,1,0:T(8,128)(2,1)}, bf16[3,768,384]{2,1,0:T(8,128)(2,1)}, u32[]{:S(2)}, u32[]{:S(2)}) collective-permute-start(bf16[3,768,384]{2,1,0:T(8,128)(2,1)} %collective-permute-done.9.near_ref), channel_id=1, source_target_pairs={{0,8},{8,0},{1,9},{9,1},{2,10},{10,2},{3,11},{11,3},{4,12},{12,4},... | collective-permute-start | bytes 5308424 | tf_op jit(solution)/shard_map/ppermute | solution.py:305
  106.3 27.8 %collective-permute-start.19 = (bf16[3,96,1920]{2,1,0:T(8,128)(2,1)}, bf16[3,96,1920]{2,1,0:T(8,128)(2,1)}, u32[]{:S(2)}, u32[]{:S(2)}) collective-permute-start(bf16[3,96,1920]{2,1,0:T(8,128)(2,1)} %pad_maximum_fusion.1), channel_id=1, source_target_pairs={{0,128},{128,0},{1,129},{129,1},{2,130},{130,2},{3,131},{131,3},{4... | collective-permute-start | bytes 3317768 | tf_op jit(solution)/shard_map/ppermute | solution.py:122
  107.5 19.8 %collective-permute-start.17 = (bf16[1,96,1920]{2,1,0:T(8,128)(2,1)}, bf16[1,96,1920]{2,1,0:T(8,128)(2,1)}, u32[]{:S(2)}, u32[]{:S(2)}) collective-permute-start(bf16[1,96,1920]{2,1,0:T(8,128)(2,1)} %get-tuple-element.57), channel_id=1, source_target_pairs={{0,16},{16,32},{32,48},{48,64},{64,80},{80,96},{96,112},{112,0},{1... | collective-permute-start | bytes 1105928 | tf_op jit(solution)/shard_map/ppermute | solution.py:262
  107.7 19.5 %collective-permute-start.18 = (bf16[1,96,1920]{2,1,0:T(8,128)(2,1)}, bf16[1,96,1920]{2,1,0:T(8,128)(2,1)}, u32[]{:S(2)}, u32[]{:S(2)}) collective-permute-start(bf16[1,96,1920]{2,1,0:T(8,128)(2,1)} %get-tuple-element.58), channel_id=1, source_target_pairs={{0,112},{16,0},{32,16},{48,32},{64,48},{80,64},{96,80},{112,96},{1... | collective-permute-start | bytes 1105928 | tf_op jit(solution)/shard_map/ppermute | solution.py:265
  112.3 8.2 %copy-start.12 = (bf16[1,96,1920]{2,1,0:T(8,128)(2,1)S(1)}, bf16[1,96,1920]{2,1,0:T(8,128)(2,1)}, u32[]{:S(2)}) copy-start(bf16[1,96,1920]{2,1,0:T(8,128)(2,1)} %copy-done.11) | copy-start | bytes 1105924
  112.3 8.2 %copy-start.18 = (bf16[1,96,1920]{2,1,0:T(8,128)(2,1)S(1)}, bf16[1,96,1920]{2,1,0:T(8,128)(2,1)}, u32[]{:S(2)}) copy-start(bf16[1,96,1920]{2,1,0:T(8,128)(2,1)} %copy-done.17) | copy-start | bytes 1105924
  112.3 8.2 %copy-start.20 = (bf16[1,48,1920]{2,1,0:T(8,128)(2,1)S(1)}, bf16[1,48,1920]{2,1,0:T(8,128)(2,1)}, u32[]{:S(2)}) copy-start(bf16[1,48,1920]{2,1,0:T(8,128)(2,1)} %copy-done.19) | copy-start | bytes 552964
  112.3 8.2 %copy-start.22 = (bf16[1,48,1920]{2,1,0:T(8,128)(2,1)S(1)}, bf16[1,48,1920]{2,1,0:T(8,128)(2,1)}, u32[]{:S(2)}) copy-start(bf16[1,48,1920]{2,1,0:T(8,128)(2,1)} %copy-done.21) | copy-start | bytes 552964
  134.1 9.4 %copy-start.16 = (bf16[512,384]{1,0:T(8,128)(2,1)S(1)}, bf16[512,384]{1,0:T(8,128)(2,1)}, u32[]{:S(2)}) copy-start(bf16[512,384]{1,0:T(8,128)(2,1)} %copy-done.15) | copy-start | bytes 1179652
  142.6 9.6 %collective-permute-start.22 = (bf16[512,1536]{1,0:T(8,128)(2,1)}, bf16[512,1536]{1,0:T(8,128)(2,1)S(1)}, u32[]{:S(2)}, u32[]{:S(2)}) collective-permute-start(bf16[512,1536]{1,0:T(8,128)(2,1)} %shard_map.85.activated_ref), channel_id=1, source_target_pairs={{0,8},{8,0},{1,9},{9,1},{2,10},{10,2},{3,11},{11,3},{4,12},{12,4},... | collective-permute-start | bytes 4718600 | tf_op jit(solution)/shard_map/ppermute | solution.py:319
  143.5 8.7 %collective-permute-start.21 = (bf16[512,384]{1,0:T(8,128)(2,1)S(1)}, bf16[512,384]{1,0:T(8,128)(2,1)}, u32[]{:S(2)}, u32[]{:S(2)}) collective-permute-start(bf16[512,384]{1,0:T(8,128)(2,1)S(1)} %copy-done.16), channel_id=1, source_target_pairs={{0,8},{8,0},{1,9},{9,1},{2,10},{10,2},{3,11},{11,3},{4,12},{12,4},... | collective-permute-start | bytes 1179656 | tf_op jit(solution)/shard_map/ppermute | solution.py:319
  152.2 19.0 %collective-permute-start.20 = (bf16[4,192,512]{2,1,0:T(8,128)(2,1)}, bf16[4,192,512]{2,1,0:T(8,128)(2,1)}, u32[]{:S(2)}, u32[]{:S(2)}) collective-permute-start(bf16[4,192,512]{2,1,0:T(8,128)(2,1)} %dynamic-slice_bitcast_fusion), channel_id=1, source_target_pairs={{0,4},{4,0},{1,5},{5,1},{2,6},{6,2},{3,7},{7,3},{8,12},{12,8},{9,1... | collective-permute-start | bytes 2359304 | tf_op jit(solution)/shard_map/ppermute | solution.py:100
  160.4 10.8 %collective-permute-start.23 = (bf16[2,192,512]{2,1,0:T(8,128)(2,1)S(1)}, bf16[2,192,512]{2,1,0:T(8,128)(2,1)S(1)}, u32[]{:S(2)}, u32[]{:S(2)}) collective-permute-start(bf16[2,192,512]{2,1,0:T(8,128)(2,1)S(1)} %get-tuple-element.76), channel_id=1, source_target_pairs={{0,8},{8,0},{1,9},{9,1},{2,10},{10,2},{3,11},{11,3},{4,12},{12,4},... | collective-permute-start | bytes 1179656 | tf_op jit(solution)/shard_map/ppermute | solution.py:101
  160.8 15.4 %collective-permute-start.27 = (bf16[2,192,512]{2,1,0:T(8,128)(2,1)}, bf16[2,192,512]{2,1,0:T(8,128)(2,1)S(1)}, u32[]{:S(2)}, u32[]{:S(2)}) collective-permute-start(bf16[2,192,512]{2,1,0:T(8,128)(2,1)} %get-tuple-element.75), channel_id=1, source_target_pairs={{0,10},{1,11},{2,8},{3,9},{8,2},{9,3},{10,0},{11,1},{4,14},{5,15},... | collective-permute-start | bytes 1179656 | tf_op jit(solution)/shard_map/ppermute | solution.py:92
  163.1 19.3 %collective-permute-start.28 = (bf16[2,192,512]{2,1,0:T(8,128)(2,1)}, bf16[2,192,512]{2,1,0:T(8,128)(2,1)S(1)}, u32[]{:S(2)}, u32[]{:S(2)}) collective-permute-start(bf16[2,192,512]{2,1,0:T(8,128)(2,1)} %get-tuple-element.74), channel_id=1, source_target_pairs={{0,9},{1,10},{2,11},{3,8},{8,1},{9,2},{10,3},{11,0},{4,13},{5,14},... | collective-permute-start | bytes 1179656 | tf_op jit(solution)/shard_map/ppermute | solution.py:92
  163.9 18.6 %collective-permute-start.29 = (bf16[2,192,512]{2,1,0:T(8,128)(2,1)}, bf16[2,192,512]{2,1,0:T(8,128)(2,1)S(1)}, u32[]{:S(2)}, u32[]{:S(2)}) collective-permute-start(bf16[2,192,512]{2,1,0:T(8,128)(2,1)} %get-tuple-element.73), channel_id=1, source_target_pairs={{0,11},{1,8},{2,9},{3,10},{8,3},{9,0},{10,1},{11,2},{4,15},{5,12},... | collective-permute-start | bytes 1179656 | tf_op jit(solution)/shard_map/ppermute | solution.py:92
  173.4 11.8 %copy-start.27 = (bf16[512,384]{1,0:T(8,128)(2,1)S(1)}, bf16[512,384]{1,0:T(8,128)(2,1)}, u32[]{:S(2)}) copy-start(bf16[512,384]{1,0:T(8,128)(2,1)} %param.8) | copy-start | bytes 1179652
  173.4 12.7 %collective-permute-start.24 = (bf16[192,512]{1,0:T(8,128)(2,1)}, bf16[192,512]{1,0:T(8,128)(2,1)}, u32[]{:S(2)}, u32[]{:S(2)}) collective-permute-start(bf16[192,512]{1,0:T(8,128)(2,1)} %get-tuple-element.79), channel_id=1, source_target_pairs={{0,2},{1,3},{2,0},{3,1},{8,10},{9,11},{10,8},{11,9},{4,6},{5,7},{6... | collective-permute-start | bytes 589832 | tf_op jit(solution)/shard_map/ppermute | solution.py:92
  175.7 14.9 %collective-permute-start.25 = (bf16[192,512]{1,0:T(8,128)(2,1)S(1)}, bf16[192,512]{1,0:T(8,128)(2,1)}, u32[]{:S(2)}, u32[]{:S(2)}) collective-permute-start(bf16[192,512]{1,0:T(8,128)(2,1)S(1)} %get-tuple-element.81), channel_id=1, source_target_pairs={{0,1},{1,2},{2,3},{3,0},{8,9},{9,10},{10,11},{11,8},{4,5},{5,6},{6... | collective-permute-start | bytes 589832 | tf_op jit(solution)/shard_map/ppermute | solution.py:92
  176.1 14.5 %collective-permute-start.26 = (bf16[192,512]{1,0:T(8,128)(2,1)S(1)}, bf16[192,512]{1,0:T(8,128)(2,1)}, u32[]{:S(2)}, u32[]{:S(2)}) collective-permute-start(bf16[192,512]{1,0:T(8,128)(2,1)S(1)} %get-tuple-element.80), channel_id=1, source_target_pairs={{0,3},{1,0},{2,1},{3,2},{8,11},{9,8},{10,9},{11,10},{4,7},{5,4},{6... | collective-permute-start | bytes 589832 | tf_op jit(solution)/shard_map/ppermute | solution.py:92
  183.4 7.2 %collective-permute-start.30 = (bf16[192,512]{1,0:T(8,128)(2,1)}, bf16[192,512]{1,0:T(8,128)(2,1)}, u32[]{:S(2)}, u32[]{:S(2)}) collective-permute-start(bf16[192,512]{1,0:T(8,128)(2,1)} %fusion.5), channel_id=1, source_target_pairs={{0,4},{4,0},{1,5},{5,1},{2,6},{6,2},{3,7},{7,3},{8,12},{12,8},{9,1... | collective-permute-start | bytes 589832 | tf_op jit(solution)/shard_map/ppermute | solution.py:117
  (13 other events, 49.7 us)
Sparse Core Ops, SparseCore 0:
  9.2 48.6 all-gather.2
  59.8 73.8 all-gather.4
